TPU v7x, 32 devices: a whole 2x2x4 slice. The times are simulated.
32 devices in a mesh: groups: 2 (over x), dp: 2 (over core), tensor: 8 (over z, y).
Axes of the slice: x: 2, y: 2, z: 4, core: 2. Of those that a mesh axis runs over, the one named last changes fastest.
Arguments:
- gate_preactivation: bfloat16 [3072, 14336], P(('groups', 'dp'), 'tensor'), parts along dimension 0, may hold values from -6 to 6
- up_preactivation: bfloat16 [3072, 14336], P(('groups', 'dp'), 'tensor'), parts along dimension 0, may hold values from -6 to 6
- base_down_matrix: bfloat16 [14336, 8192], P('tensor'), may hold values from -0.0625 to 0.0625
- adapter_first_factor: bfloat16 [64, 14336, 64], P('dp', 'tensor'), may hold values from -0.046875 to 0.046875
- adapter_second_factor: bfloat16 [64, 64, 8192], P('dp', None, 'tensor'), may hold values from -0.75 to 0.75
- residual: bfloat16 [3072, 8192], P(('groups', 'dp'), 'tensor'), parts along dimension 0
- scoring_head_matrix: float32 [8192], replicated, may hold values from -0.0625 to 0.0625
- block_adapter_index: int32 [24], P('groups'), parts along dimension 0, may hold values from 0 to 63
- block_span_start: int32 [24], P(('groups', 'dp')), parts along dimension 0, may hold values from 0 to 127, as said below
- block_span_end: int32 [24], P(('groups', 'dp')), parts along dimension 0, may hold values from 1 to 128, as said below
Outputs:
- layer_out: bfloat16 [3072, 8192], P(('groups', 'dp'), 'tensor'), parts along dimension 0
- span_scores: float32 [24], P(('groups', 'dp')), parts along dimension 0
There are 2 independent parts, one for each index of `groups`. A program takes and returns all parts, laid end to end along the dimension named above; an argument that names none is the same for every part. Nothing has to cross between parts.
Inputs may be any that keep to these rules, and one draw needn't show every extreme that they name: Each block's scored positions satisfy 0 <= block_span_start < block_span_end <= 128. block_span_end is greater than block_span_start of the same block.
All inputs are finite; a program needn't handle non-finite values.
Results may differ from a plain program's by a relative error of at most 0.0049.
Values may be sent and summed in bfloat16 or wider, within the bound.
No kernel may reach another device: no remote copies, remote signals or barrier semaphores. Data moves between devices by JAX's collectives and lax.ppermute only.
A program may use at most 192 MiB of HBM per device.

v0:
```python
import jax
import jax.numpy as jnp
from jax import lax
from jax.sharding import PartitionSpec as P

MODEL_WIDTH = 8192
BLOCK = 128
BLK_DEV = 6


epsilon = 1e-05


def rank_partials(rank_terms):
    return lax.psum(rank_terms, "tensor").astype(jnp.bfloat16)


def shards(
    gate_preactivation,
    up_preactivation,
    base_down_matrix,
    adapter_first_factor,
    adapter_second_factor,
    residual,
    scoring_head_matrix,
    block_adapter_index,
    block_span_start,
    block_span_end,
):
    rows_local = gate_preactivation.shape[0]
    hidden_width = gate_preactivation.shape[1]
    slice_width = residual.shape[1]
    local_adapter_set = adapter_first_factor.shape[0]
    data_index = lax.axis_index("dp")
    data_size = lax.axis_size("dp")
    tensor_index = lax.axis_index("tensor")
    hidden = (
        jax.nn.silu(gate_preactivation.astype(jnp.float32)) * up_preactivation.astype(jnp.float32)
    ).astype(jnp.bfloat16)
    hidden_blocks = hidden.reshape(BLK_DEV, BLOCK, hidden_width)
    own_ids = lax.dynamic_slice_in_dim(block_adapter_index, data_index * BLK_DEV, BLK_DEV)
    owner_index = own_ids // local_adapter_set
    live_mask = owner_index[None, :] == jnp.arange(data_size, dtype=jnp.int32)[:, None]
    outgoing = jnp.where(
        live_mask[:, :, None, None], hidden_blocks[None], jnp.zeros((), jnp.bfloat16)
    )
    received_rows = lax.all_to_all(outgoing, "dp", split_axis=0, concat_axis=0, tiled=True)
    local_adapter_index = (
        block_adapter_index.reshape(data_size, BLK_DEV) - data_index * local_adapter_set
    )
    local_adapter_index = jnp.clip(local_adapter_index, 0, local_adapter_set - 1)
    rank_terms = jnp.einsum(
        "qlcj,qlje->qlce",
        received_rows,
        adapter_first_factor[local_adapter_index],
        preferred_element_type=jnp.float32,
    )
    low_rank_update = rank_partials(rank_terms)
    slot_delta = jnp.einsum(
        "zxcn,zxnt->zxct",
        low_rank_update,
        adapter_second_factor[local_adapter_index],
        preferred_element_type=jnp.float32,
    ).astype(jnp.bfloat16)
    returned = lax.all_to_all(slot_delta, "dp", split_axis=0, concat_axis=0, tiled=True)
    adapter_delta = jnp.sum(returned.astype(jnp.float32), 0).reshape(rows_local, slice_width)
    base_part = lax.psum_scatter(
        jnp.dot(hidden, base_down_matrix, preferred_element_type=jnp.float32),
        "tensor",
        scatter_dimension=1,
        tiled=True,
    )
    combined = residual.astype(jnp.float32) + base_part + adapter_delta
    layer_out = combined.astype(jnp.bfloat16)
    head_slice = lax.dynamic_slice_in_dim(
        scoring_head_matrix, tensor_index * slice_width, slice_width
    )
    square_sum, head_sum = lax.psum(
        (jnp.sum(combined * combined, 1), jnp.sum(combined * head_slice[None, :], 1)), "tensor"
    )
    all_scores = head_sum * lax.rsqrt(square_sum / MODEL_WIDTH + epsilon)
    position = jnp.arange(BLOCK, dtype=jnp.int32)
    inside = (position[None, :] >= block_span_start[:, None]) & (
        position[None, :] < block_span_end[:, None]
    )
    span_scores = jnp.sum(
        jnp.where(inside, all_scores.reshape(BLK_DEV, BLOCK), jnp.float32(0.0)), 1
    )
    return (layer_out, span_scores)


def solution(mesh):
    return jax.shard_map(
        shards,
        mesh=mesh,
        in_specs=(
            P(("groups", "dp"), "tensor"),
            P(("groups", "dp"), "tensor"),
            P("tensor", None),
            P("dp", "tensor", None),
            P("dp", None, "tensor"),
            P(("groups", "dp"), "tensor"),
            P(),
            P("groups"),
            P(("groups", "dp")),
            P(("groups", "dp")),
        ),
        out_specs=(P(("groups", "dp"), "tensor"), P(("groups", "dp"))),
        check_vma=False,
    )
```

profile of v0, /device:TPU:0, one launch (start us, length us, event | category | flops | bytes accessed | tf_op | source)
XLA Modules:
  0.0 486.6 jit_solution(7436766908062922414)
XLA Ops:
  7.2 0.0 reduce-scatter.2.cloned.1.call-start
  7.2 4.3 fusion.4
  11.5 29.1 %fusion.8 = f32[768,8192]{1,0:T(8,128)} fusion(bf16[768,1792]{1,0:T(8,128)(2,1)S(1)} %fusion.4, bf16[1792,8192]{1,0:T(8,128)(2,1)} %param.12), kind=kOutput, calls=%fused_computation.29 | convolution fusion | flops 22548578304 | bytes 57278464 | tf_op jit(solution)/shard_map/dot_general | solution.py:68
  40.6 0.0 copy-start.2
  40.6 0.0 reduce-scatter.2.cloned.1.call-update
  40.6 0.6 copy-done.2
  41.2 0.1 and_select_fusion
  41.3 2.8 broadcast_select_fusion
  44.1 6.1 %all-to-all-start = ((bf16[2,6,128,1792]{3,2,1,0:T(8,128)(2,1)}), bf16[2,6,128,1792]{3,2,1,0:T(8,128)(2,1)}, u32[]{:S(2)}, u32[]{:S(2)}) async-start(bf16[2,6,128,1792]{3,2,1,0:T(8,128)(2,1)} %broadcast_select_fusion), calls=%async_computation.1 | async-start | bytes 11010048 | tf_op jit(solution)/shard_map/all_to_all | solution.py:47
  50.2 0.1 min.12
  50.3 0.1 reshape.64
  50.4 4.5 gather_fusion.1
  54.9 3.8 gather_fusion
  58.7 0.0 all-to-all-done
  58.8 4.6 fusion.9
  63.4 53.0 %all-reduce.2 = bf16[2,6,128,64]{2,3,1,0:T(8,128)(2,1)S(1)} all-reduce(f32[2,6,128,64]{2,3,1,0:T(8,128)S(1)} %fusion.9), channel_id=1, replica_groups=mesh['groups'=2,'dp'=2,'tensor'=8] {'tensor'}, use_global_device_ids=true, to_apply=%region_1.2 | all-reduce | flops 98304 | bytes 589824 | tf_op jit(solution)/shard_map/psum | solution.py:15
  116.4 4.2 convolution_convert_fusion
  120.6 5.3 %all-to-all-start.1 = ((bf16[2,6,128,1024]{3,2,1,0:T(8,128)(2,1)}), bf16[2,6,128,1024]{3,2,1,0:T(8,128)(2,1)}, u32[]{:S(2)}, u32[]{:S(2)}) async-start(bf16[2,6,128,1024]{3,2,1,0:T(8,128)(2,1)} %convolution_convert_fusion), calls=%async_computation.2 | async-start | bytes 6291456 | tf_op jit(solution)/shard_map/all_to_all | solution.py:65
  125.9 0.0 dynamic-slice-start
  125.9 3.7 all-to-all-done.1
  129.6 3.0 convert_reduce_fusion
  132.6 0.0 copy-start
  132.6 0.0 copy-start.1
  132.6 322.1 %reduce-scatter.2.cloned.1.call-done = f32[768,1024]{1,0:T(8,128)} async-done(((f32[768,8192]{1,0:T(8,128)}), f32[768,1024]{1,0:T(8,128)}) %reduce-scatter.2.cloned.1.call-update) | async-done | bytes 3145744 | tf_op jit(solution)/shard_map/reduce_scatter | solution.py:67
  454.7 0.0 dynamic-slice-done
  454.7 4.7 multiply_reduce_fusion
  459.4 19.7 %all-reduce = (f32[768]{0:T(1024)S(1)}, f32[768]{0:T(1024)S(1)}) all-reduce(f32[768]{0:T(1024)S(1)} %get-tuple-element.3, f32[768]{0:T(1024)S(1)} %get-tuple-element.2), channel_id=1, replica_groups=mesh['groups'=2,'dp'=2,'tensor'=8] {'tensor'}, use_global_device_ids=true, to_apply=%region_4.5 | all-reduce | flops 1536 | bytes 12288 | tf_op jit(solution)/shard_map/psum | solution.py:78
  479.1 0.0 copy-done
  479.1 0.0 copy-done.1
  479.1 0.7 fusion.6
  (4 shorter events, 0.0 us)
Async XLA Ops:
  7.2 447.5 %reduce-scatter.2.cloned.1.call-start = ((), (), s32[]{:S(2)}) async-start(), calls=%async_computation.3 | async-start | bytes 28311552 | tf_op jit(solution)/shard_map/reduce_scatter | solution.py:67
  40.6 0.7 copy-start.2
  44.1 14.7 %all-to-all-start = ((bf16[2,6,128,1792]{3,2,1,0:T(8,128)(2,1)}), bf16[2,6,128,1792]{3,2,1,0:T(8,128)(2,1)}, u32[]{:S(2)}, u32[]{:S(2)}) async-start(bf16[2,6,128,1792]{3,2,1,0:T(8,128)(2,1)} %broadcast_select_fusion), calls=%async_computation.1 | async-start | bytes 11010048 | tf_op jit(solution)/shard_map/all_to_all | solution.py:47
  120.6 9.0 %all-to-all-start.1 = ((bf16[2,6,128,1024]{3,2,1,0:T(8,128)(2,1)}), bf16[2,6,128,1024]{3,2,1,0:T(8,128)(2,1)}, u32[]{:S(2)}, u32[]{:S(2)}) async-start(bf16[2,6,128,1024]{3,2,1,0:T(8,128)(2,1)} %convolution_convert_fusion), calls=%async_computation.2 | async-start | bytes 6291456 | tf_op jit(solution)/shard_map/all_to_all | solution.py:65
  125.9 328.8 %dynamic-slice-start = ((f32[8192]{0:T(1024)}, s32[]{:T(128)}), f32[1024]{0:T(1024)S(1)}, s32[]{:S(2)}) async-start(f32[8192]{0:T(1024)} %param.16, s32[]{:T(128)} %select_n.34), calls=%async_computation.4 | async-start | bytes 8704 | tf_op jit(solution)/shard_map/dynamic_slice | solution.py:75
  132.6 346.5 %copy-start = (s32[6]{0:T(128)S(1)}, s32[6]{0:T(128)}, u32[]{:S(2)}) copy-start(s32[6]{0:T(128)} %param.19) | copy-start | bytes 76
  132.6 346.5 %copy-start.1 = (s32[6]{0:T(128)S(1)}, s32[6]{0:T(128)}, u32[]{:S(2)}) copy-start(s32[6]{0:T(128)} %param.18) | copy-start | bytes 76
Sparse Core Ops, SparseCore 0:
  40.7 413.9 reduce-scatter.1
where the time goes:
time: 487 us
  waiting for transfers between devices  326 us (67%)
  blocking collectives  72.7 us (15%)
  matrix products  37.9 us (8%)
  other arithmetic  15.5 us (3%)
  between operations  14.2 us (3%)
  starting transfers between devices  11.4 us (2%)
  local copies, waits for them, and re-layouts  9.15 us (2%)
    reduce_scatter x1, waiting for transfers between devices, shards(): lax.psum_scatter(jnp.dot(hidden, base_down_matrix, preferred_element_type...  322 us
    psum x1, blocking collectives, rank_partials(): return lax.psum(rank_terms, 'tensor').astype(jnp.bfloat16)  53 us
    dot_general x1, matrix products, shards(): jnp.dot(hidden, base_down_matrix, preferred_element_type=jnp.float32)  29.1 us
    psum x1, blocking collectives, shards(): lax.psum((jnp.sum(combined * combined, 1), jnp.sum(combined * head_slice[...  19.7 us
  transfers between devices with their start and end apart: 3, of which 2 were waited for; matrix products, arithmetic and copies ran while one was open for 5% of the time, Pallas kernels for 0%

commit v1 on v0

v1 whole, which is shorter than its diff:
```python
import jax
import jax.numpy as jnp
from jax import lax
from jax.sharding import PartitionSpec as P

BLOCK = 128
EPSILON = 1e-05

f32 = jnp.float32
bf16 = jnp.bfloat16

LINE = 4
PAIR = 2
ORDER = ((3, 2, 1, 0), (3, 0, 2, 1), (0, 3, 1, 2), (0, 1, 2, 3))


def along_line(value, hops):
    pairs = [(a * PAIR + y, b * PAIR + y) for a, b in hops for y in range(PAIR)]
    return lax.ppermute(value, "tensor", pairs)


def across(value, bit):
    size = LINE * PAIR
    return lax.ppermute(value, "tensor", [(t, t ^ bit) for t in range(size)])


def line_sum(parts, z):
    first = along_line(parts[0].astype(bf16), [(0, 1), (3, 2)])
    at_end = (z == 0) | (z == LINE - 1)
    second = (jnp.where(at_end, parts[1], parts[0]) + first.astype(f32)).astype(bf16)
    up = along_line(second, [(0, 1), (1, 2)])
    down = along_line(second, [(3, 2), (2, 1)])
    low = z < LINE // 2
    third_up = (jnp.where(low, parts[2], parts[1]) + up.astype(f32)).astype(bf16)
    third_down = (jnp.where(low, parts[1], parts[2]) + down.astype(f32)).astype(bf16)
    up = along_line(third_up, [(0, 1), (1, 2), (2, 3)])
    down = along_line(third_down, [(3, 2), (2, 1), (1, 0)])
    return parts[3] + up.astype(f32) + down.astype(f32)


def grid_scatter(hidden, weights, width, tensor_index):
    z, y = tensor_index // PAIR, tensor_index % PAIR
    order = jnp.asarray(ORDER, jnp.int32)[z]
    depth = weights.shape[0]

    def product(rows, column):
        block = lax.dynamic_slice(weights, (0, column * width), (depth, width))
        return jnp.dot(rows, block, preferred_element_type=f32)

    sums = []
    for k in range(LINE):
        theirs = product(hidden, order[k] * PAIR + 1 - y).astype(bf16)
        arrived = across(theirs, 1)
        mine = product(hidden, order[k] * PAIR + y)
        sums.append(mine + arrived.astype(f32))
    return line_sum(sums, z)


def exchange_sum(value, wire):
    for bit in (1, 2, 4):
        value = value + across(value.astype(wire), bit).astype(f32)
    return value


def shards(
    gate_preactivation,
    up_preactivation,
    base_down_matrix,
    adapter_first_factor,
    adapter_second_factor,
    residual,
    scoring_head_matrix,
    block_adapter_index,
    block_span_start,
    block_span_end,
):
    rows_local, hidden_width = gate_preactivation.shape
    slice_width = residual.shape[1]
    model_width = scoring_head_matrix.shape[0]
    blocks = rows_local // BLOCK
    adapters_here = adapter_first_factor.shape[0]
    data_index = lax.axis_index("dp")
    data_size = lax.axis_size("dp")
    tensor_index = lax.axis_index("tensor")
    on_grid = lax.axis_size("tensor") == LINE * PAIR

    ids = block_adapter_index.reshape(data_size, blocks)
    own_ids = lax.dynamic_index_in_dim(ids, data_index, 0, keepdims=False)
    owner = own_ids // adapters_here

    def fetched(factors):
        def held(which):
            at = jnp.clip(which - data_index * adapters_here, 0, adapters_here - 1)
            return factors[at]

        result = held(own_ids)
        for step in range(1, data_size):
            there = (data_index + step) % data_size
            wanted = held(lax.dynamic_index_in_dim(ids, there, 0, keepdims=False))
            came = lax.ppermute(
                wanted, "dp", [(d, (d + step) % data_size) for d in range(data_size)]
            )
            source = (data_index - step) % data_size
            result = jnp.where((owner == source)[:, None, None], came, result)
        return result

    first_factors = fetched(adapter_first_factor)
    second_factors = fetched(adapter_second_factor)

    hidden = (
        jax.nn.silu(gate_preactivation.astype(f32)) * up_preactivation.astype(f32)
    ).astype(bf16)
    low_rank = jnp.einsum(
        "bcj,bje->bce",
        hidden.reshape(blocks, BLOCK, hidden_width),
        first_factors,
        preferred_element_type=f32,
    ).reshape(rows_local, -1)
    if on_grid:
        low_rank = exchange_sum(low_rank, f32)
    else:
        low_rank = lax.psum(low_rank, "tensor")
    delta = jnp.einsum(
        "bcn,bnt->bct",
        low_rank.astype(bf16).reshape(blocks, BLOCK, -1),
        second_factors,
        preferred_element_type=f32,
    ).reshape(rows_local, slice_width)
    delta = delta.astype(bf16).astype(f32)

    if on_grid:
        base_part = grid_scatter(hidden, base_down_matrix, slice_width, tensor_index)
    else:
        base_part = lax.psum_scatter(
            jnp.dot(hidden, base_down_matrix, preferred_element_type=f32),
            "tensor",
            scatter_dimension=1,
            tiled=True,
        )
    combined = residual.astype(f32) + base_part + delta
    layer_out = combined.astype(bf16)
    head = lax.dynamic_slice_in_dim(
        scoring_head_matrix, tensor_index * slice_width, slice_width
    )
    stats = jnp.stack([jnp.sum(combined * combined, 1), jnp.sum(combined * head[None, :], 1)])
    stats = stats.reshape(2 * blocks, BLOCK)
    stats = exchange_sum(stats, f32) if on_grid else lax.psum(stats, "tensor")
    square_sum, head_sum = stats[:blocks], stats[blocks:]
    scores = head_sum * lax.rsqrt(square_sum / model_width + EPSILON)
    position = jnp.arange(BLOCK, dtype=jnp.int32)
    inside = (position[None, :] >= block_span_start[:, None]) & (
        position[None, :] < block_span_end[:, None]
    )
    span_scores = jnp.sum(jnp.where(inside, scores, f32(0.0)), 1)
    return (layer_out, span_scores)


def solution(mesh):
    return jax.shard_map(
        shards,
        mesh=mesh,
        in_specs=(
            P(("groups", "dp"), "tensor"),
            P(("groups", "dp"), "tensor"),
            P("tensor", None),
            P("dp", "tensor", None),
            P("dp", None, "tensor"),
            P(("groups", "dp"), "tensor"),
            P(),
            P("groups"),
            P(("groups", "dp")),
            P(("groups", "dp")),
        ),
        out_specs=(P(("groups", "dp"), "tensor"), P(("groups", "dp"))),
        check_vma=False,
    )
```

time: 487 us -> 221 us (0.45)
  waiting for transfers between devices: 326 us -> 86.5 us
  blocking collectives: 72.7 us -> 0 us
  starting transfers between devices: 11.4 us -> 35.7 us
  matrix products: 37.9 us -> 55 us
  between operations: 14.2 us -> 3.45 us
  local copies, waits for them, and re-layouts: 9.15 us -> 18.6 us
  other arithmetic: 15.5 us -> 21.6 us
    reduce_scatter x1 -> x0, waiting for transfers between devices: 322 us -> none  [shards(): lax.psum_scatter(jnp.dot(hidden, base_down_matrix, preferred_element_type...]
    ppermute x0 -> x17, waiting for transfers between devices: none -> 86.5 us  [the longest x10 71.1 us: across(): return lax.ppermute(value, 'tensor', [(t, t ^ bit) for t in range(size)])]
    psum x2 -> x0, blocking collectives: 72.7 us -> none  [the longest x1 53 us: rank_partials(): return lax.psum(rank_terms, 'tensor').astype(jnp.bfloat16)]
    ppermute x0 -> x17, starting transfers between devices: none -> 35.7 us  [the longest x5 22.7 us: along_line(): return lax.ppermute(value, 'tensor', pairs)]
    dot_general x3 -> x10, matrix products: 37.9 us -> 55 us  [the longest x8 50.4 us: product(): return jnp.dot(rows, block, preferred_element_type=f32)]
    convert_element_type x1 -> x3, other arithmetic: 4.27 us -> 15.9 us  [the longest x1 6.47 us: line_sum(): (jnp.where(low, parts[2], parts[1]) + up.astype(f32)).astype(bf16)]
    all_to_all x2 -> x0, starting transfers between devices: 11.4 us -> none  [the longest x1 6.12 us: shards(): lax.all_to_all(outgoing, 'dp', split_axis=0, concat_axis=0, tiled=True)]
    gather x2 -> x4, local copies, waits for them, and re-layouts: 8.34 us -> 17.1 us  [held(): return factors[at]]
  transfers between devices with their start and end apart: 3 -> 17, of which waited for: 2 -> 9; matrix products, arithmetic and copies ran while one was open for 5% -> 35% of each run, Pallas kernels for 0% -> 0%
where the time goes in v1:
time: 221 us
  waiting for transfers between devices  86.5 us (39%)
  matrix products  55 us (25%)
  starting transfers between devices  35.7 us (16%)
  other arithmetic  21.6 us (10%)
  local copies, waits for them, and re-layouts  18.6 us (8%)
  between operations  3.45 us (2%)
    ppermute x10, waiting for transfers between devices, across(): return lax.ppermute(value, 'tensor', [(t, t ^ bit) for t in range(size)])  71.1 us
    dot_general x8, matrix products, product(): return jnp.dot(rows, block, preferred_element_type=f32)  50.4 us
    ppermute x5, starting transfers between devices, along_line(): return lax.ppermute(value, 'tensor', pairs)  22.7 us
    gather x4, local copies, waits for them, and re-layouts, held(): return factors[at]  17.1 us
    ppermute x5, waiting for transfers between devices, along_line(): return lax.ppermute(value, 'tensor', pairs)  15.4 us
    ppermute x10, starting transfers between devices, across(): return lax.ppermute(value, 'tensor', [(t, t ^ bit) for t in range(size)])  13 us
    convert_element_type x1, other arithmetic, line_sum(): (jnp.where(low, parts[2], parts[1]) + up.astype(f32)).astype(bf16)  6.47 us
    convert_element_type x1, other arithmetic, line_sum(): (jnp.where(at_end, parts[1], parts[0]) + first.astype(f32)).astype(bf16)  5.1 us
  transfers between devices with their start and end apart: 17, of which 9 were waited for; matrix products, arithmetic and copies ran while one was open for 35% of the time, Pallas kernels for 0%

profile of v1, /device:TPU:0, one launch (start us, length us, event | category | flops | bytes accessed | tf_op | source)
XLA Modules:
  0.0 220.9 jit_solution(4029860403438420147)
XLA Ops:
  0.7 0.7 constant_dynamic-slice_fusion.2
  1.3 0.7 fusion.65
  2.7 4.3 %fusion.4 = bf16[768,1792]{1,0:T(8,128)(2,1)S(1)} fusion(bf16[768,1792]{1,0:T(8,128)(2,1)} %param.12, bf16[768,1792]{1,0:T(8,128)(2,1)} %param.11), kind=kLoop, calls=%fused_computation.10 | loop fusion | flops 11010048 | bytes 8257536 | tf_op jit(solution)/shard_map/convert_element_type | solution.py:112
  6.9 0.0 copy-start.2
  7.0 7.1 %fusion.31 = bf16[768,1024]{1,0:T(8,128)(2,1)} fusion(bf16[768,1792]{1,0:T(8,128)(2,1)S(1)} %fusion.4, bf16[1792,8192]{1,0:T(8,128)(2,1)} %param.13, s32[]{:T(128)S(6)} %select_n.135), kind=kOutput, calls=%fused_computation.40 | convolution fusion | flops 2819358720 | bytes 7995396 | tf_op jit(solution)/shard_map/dot_general | solution.py:48
  14.1 3.0 %collective-permute-start.3 = (bf16[768,1024]{1,0:T(8,128)(2,1)}, bf16[768,1024]{1,0:T(8,128)(2,1)}, u32[]{:S(2)}, u32[]{:S(2)}) collective-permute-start(bf16[768,1024]{1,0:T(8,128)(2,1)} %fusion.31), channel_id=1, source_target_pairs={{0,1},{1,0},{2,3},{3,2},{4,5},{5,4},{6,7},{7,6},{8,9},{9,8},{10,11... | collective-permute-start | bytes 4718600 | tf_op jit(solution)/shard_map/ppermute | solution.py:24
  17.6 6.1 %fusion.28 = bf16[768,1024]{1,0:T(8,128)(2,1)} fusion(bf16[768,1792]{1,0:T(8,128)(2,1)S(1)} %fusion.4, bf16[1792,8192]{1,0:T(8,128)(2,1)} %param.13, s32[]{:T(128)S(6)} %select_n.131), kind=kOutput, calls=%fused_computation.39 | convolution fusion | flops 2819358720 | bytes 7995396 | tf_op jit(solution)/shard_map/dot_general | solution.py:48
  23.7 0.0 collective-permute-start.2
  23.7 28.8 %collective-permute-done.3 = bf16[768,1024]{1,0:T(8,128)(2,1)} collective-permute-done((bf16[768,1024]{1,0:T(8,128)(2,1)}, bf16[768,1024]{1,0:T(8,128)(2,1)}, u32[]{:S(2)}, u32[]{:S(2)}) %collective-permute-start.3) | collective-permute-done | bytes 1572896 | tf_op jit(solution)/shard_map/ppermute | solution.py:24
  52.6 6.9 %fusion.21 = (bf16[768,1024]{1,0:T(8,128)(2,1)}, f32[768,1024]{1,0:T(8,128)}) fusion(bf16[768,1024]{1,0:T(8,128)(2,1)} %collective-permute-done.3, bf16[768,1792]{1,0:T(8,128)(2,1)S(1)} %fusion.4, bf16[1792,8192]{1,0:T(8,128)(2,1)} %param.13, s32[]{:T(128)S(6)} %select_n.134), kind=kOutput, calls=%fused_computation.36 | convolution fusion | flops 2820931584 | bytes 12713988 | tf_op jit(solution)/shard_map/dot_general | solution.py:48
  59.4 5.2 %collective-permute-start.4 = (bf16[768,1024]{1,0:T(8,128)(2,1)}, bf16[768,1024]{1,0:T(8,128)(2,1)}, u32[]{:S(2)}, u32[]{:S(2)}) collective-permute-start(bf16[768,1024]{1,0:T(8,128)(2,1)} %get-tuple-element.13), channel_id=1, source_target_pairs={{0,2},{1,3},{6,4},{7,5},{8,10},{9,11},{14,12},{15,13},{16,18},{17,... | collective-permute-start | bytes 4718600 | tf_op jit(solution)/shard_map/ppermute | solution.py:19
  65.3 0.0 copy-done.2
  65.3 0.0 copy-start.8
  65.3 6.2 %fusion.25 = bf16[768,1024]{1,0:T(8,128)(2,1)} fusion(bf16[768,1792]{1,0:T(8,128)(2,1)S(1)} %fusion.4, bf16[1792,8192]{1,0:T(8,128)(2,1)} %param.13, s32[]{:T(128)S(6)} %select_n.129), kind=kOutput, calls=%fused_computation.38 | convolution fusion | flops 2819358720 | bytes 7995396 | tf_op jit(solution)/shard_map/dot_general | solution.py:48
  71.5 1.5 collective-permute-start.1
  73.0 0.0 copy-done.8
  73.0 0.1 reshape.126
  73.1 4.9 %gather_fusion = bf16[6,1792,64]{1,2,0:T(8,128)(2,1)} fusion(bf16[32,1792,64]{1,2,0:T(8,128)(2,1)} %param.14, s32[1024]{0:T(1024)S(1)} %pad_clamp_fusion.1), kind=kCustom, calls=%fused_computation | custom fusion | bytes 2752536 | tf_op jit(solution)/shard_map/gather | solution.py:94
  77.9 0.0 collective-permute-start.9
  78.6 0.0 copy-start.1
  78.6 6.0 %fusion.11 = f32[768,1024]{1,0:T(8,128)S(1)} fusion(bf16[768,1792]{1,0:T(8,128)(2,1)} %copy-done.2, bf16[1792,8192]{1,0:T(8,128)(2,1)} %param.13, s32[]{:T(128)S(6)} %select_n.130), kind=kOutput, calls=%fused_computation.17 | convolution fusion | flops 2818572288 | bytes 9568260 | tf_op jit(solution)/shard_map/dot_general | solution.py:48
  84.6 1.6 collective-permute-done.2
  86.3 9.1 %collective-permute-done.4 = bf16[768,1024]{1,0:T(8,128)(2,1)} collective-permute-done((bf16[768,1024]{1,0:T(8,128)(2,1)}, bf16[768,1024]{1,0:T(8,128)(2,1)}, u32[]{:S(2)}, u32[]{:S(2)}) %collective-permute-start.4) | collective-permute-done | bytes 1572896 | tf_op jit(solution)/shard_map/ppermute | solution.py:19
  95.4 5.1 %add_convert_fusion.2 = bf16[768,1024]{1,0:T(8,128)(2,1)} fusion(bf16[768,1024]{1,0:T(8,128)(2,1)} %collective-permute-done.4, f32[768,1024]{1,0:T(8,128)S(1)} %copy-done.1, bf16[768,1024]{1,0:T(8,128)(2,1)} %collective-permute-done.3, pred[]{:T(512)S(6)} %or.3, f32[768,1024]{1,0:T(8,128)S(1)} %fusion.11, bf16[768,1024]{1,0:T(8,128)(2,1)} %collective-permute-done.2), kind=kLoop, calls=%fused_computation.32 | loop fusion | flops 6291456 | bytes 12582913 | tf_op jit(solution)/shard_map/convert_element_type | solution.py:30
  100.5 5.5 %collective-permute-start.5 = (bf16[768,1024]{1,0:T(8,128)(2,1)}, bf16[768,1024]{1,0:T(8,128)(2,1)}, u32[]{:S(2)}, u32[]{:S(2)}) collective-permute-start(bf16[768,1024]{1,0:T(8,128)(2,1)} %add_convert_fusion.2), channel_id=1, source_target_pairs={{0,2},{1,3},{2,4},{3,5},{8,10},{9,11},{10,12},{11,13},{16,18},{17,... | collective-permute-start | bytes 4718600 | tf_op jit(solution)/shard_map/ppermute | solution.py:19
  106.0 1.9 collective-permute-start.7
  107.9 6.2 %fusion.22 = bf16[768,1024]{1,0:T(8,128)(2,1)} fusion(bf16[768,1792]{1,0:T(8,128)(2,1)S(1)} %copy-done.3, bf16[1792,8192]{1,0:T(8,128)(2,1)} %param.13, s32[]{:T(128)S(6)} %select_n.126), kind=kOutput, calls=%fused_computation.37 | convolution fusion | flops 2819358720 | bytes 7995396 | tf_op jit(solution)/shard_map/dot_general | solution.py:48
  114.1 1.5 collective-permute-start
  115.6 4.9 %gather_fusion.1 = bf16[6,1792,64]{1,2,0:T(8,128)(2,1)} fusion(bf16[32,1792,64]{1,2,0:T(8,128)(2,1)} %param.14, s32[1024]{0:T(1024)S(1)} %pad_clamp_fusion), kind=kCustom, calls=%fused_computation.1 | custom fusion | bytes 2752536 | tf_op jit(solution)/shard_map/gather | solution.py:94
  120.5 6.0 %fusion.15 = f32[768,1024]{1,0:T(8,128)S(1)} fusion(bf16[768,1792]{1,0:T(8,128)(2,1)} %copy-done.2, bf16[1792,8192]{1,0:T(8,128)(2,1)} %param.13, s32[]{:T(128)S(6)} %select_n.128), kind=kOutput, calls=%fused_computation.21 | convolution fusion | flops 2818572288 | bytes 9568260 | tf_op jit(solution)/shard_map/dot_general | solution.py:48
  126.5 0.0 collective-permute-done.9
  126.6 2.4 %fusion.37 = f32[6,8,8,128]{3,2,1,0:T(8,128)S(1)} fusion(bf16[6,128,1792]{2,1,0:T(8,128)(2,1)S(1)} %bitcast.50, bf16[6,1792,64]{1,2,0:T(8,128)(2,1)} %collective-permute-done.9, bf16[6,1792,64]{1,2,0:T(8,128)(2,1)S(1)} %copy-done, pred[6]{0:T(512)(128)(4,1)S(1)} %fusion.63), kind=kOutput, calls=%fused_computation.45 | convolution fusion | flops 176848896 | bytes 5701638 | tf_op jit(solution)/shard_map/bcj,bje->bce/dot_general | solution.py:113
  129.1 0.6 collective-permute-start.10
  129.6 0.0 collective-permute-done.1
  129.6 6.3 %collective-permute-done.5 = bf16[768,1024]{1,0:T(8,128)(2,1)} collective-permute-done((bf16[768,1024]{1,0:T(8,128)(2,1)}, bf16[768,1024]{1,0:T(8,128)(2,1)}, u32[]{:S(2)}, u32[]{:S(2)}) %collective-permute-start.5) | collective-permute-done | bytes 1572896 | tf_op jit(solution)/shard_map/ppermute | solution.py:19
  135.9 0.0 collective-permute-done.7
  135.9 6.5 %add_convert_fusion.1 = (bf16[768,1024]{1,0:T(8,128)(2,1)}, bf16[768,1024]{1,0:T(8,128)(2,1)}) fusion(bf16[768,1024]{1,0:T(8,128)(2,1)} %collective-permute-done.5, f32[768,1024]{1,0:T(8,128)S(1)} %fusion.15, bf16[768,1024]{1,0:T(8,128)(2,1)} %collective-permute-done.1, pred[]{:T(512)S(6)} %lt.96, f32[768,1024]{1,0:T(8,128)S(1)} %fusion.11, ...), kind=kLoop, calls=%fused_computation.31 | loop fusion | flops 9437184 | bytes 15728641 | tf_op jit(solution)/shard_map/convert_element_type | solution.py:34
  142.4 8.8 %collective-permute-start.6 = (bf16[768,1024]{1,0:T(8,128)(2,1)}, bf16[768,1024]{1,0:T(8,128)(2,1)}, u32[]{:S(2)}, u32[]{:S(2)}) collective-permute-start(bf16[768,1024]{1,0:T(8,128)(2,1)} %get-tuple-element.5), channel_id=1, source_target_pairs={{0,2},{1,3},{2,4},{3,5},{4,6},{5,7},{8,10},{9,11},{10,12},{11,13},... | collective-permute-start | bytes 4718600 | tf_op jit(solution)/shard_map/ppermute | solution.py:19
  151.2 1.3 collective-permute-start.8
  152.5 4.5 %collective-permute-done.10 = f32[768,64]{0,1:T(8,128)S(1)} collective-permute-done((f32[768,64]{0,1:T(8,128)S(1)}, f32[768,64]{0,1:T(8,128)S(1)}, u32[]{:S(2)}, u32[]{:S(2)}) %collective-permute-start.10) | collective-permute-done | bytes 196640 | tf_op jit(solution)/shard_map/ppermute | solution.py:24
  157.0 1.9 collective-permute-start.11
  158.9 3.7 %gather_fusion.2 = bf16[6,64,1024]{2,1,0:T(8,128)(2,1)} fusion(bf16[32,64,1024]{2,1,0:T(8,128)(2,1)} %param.15, s32[1024]{0:T(1024)S(1)} %pad_clamp_fusion.1), kind=kCustom, calls=%fused_computation.2 | custom fusion | bytes 1572888 | tf_op jit(solution)/shard_map/gather | solution.py:94
  162.6 0.0 collective-permute-start.13
  162.6 28.8 %collective-permute-done.11 = f32[768,64]{0,1:T(8,128)S(1)} collective-permute-done((f32[768,64]{0,1:T(8,128)S(1)}, f32[768,64]{0,1:T(8,128)S(1)}, u32[]{:S(2)}, u32[]{:S(2)}) %collective-permute-start.11) | collective-permute-done | bytes 196640 | tf_op jit(solution)/shard_map/ppermute | solution.py:24
  191.3 0.1 collective-permute-start.12
  191.4 5.9 %fusion.19 = f32[768,1024]{1,0:T(8,128)S(1)} fusion(bf16[768,1792]{1,0:T(8,128)(2,1)} %copy-done.2, bf16[1792,8192]{1,0:T(8,128)(2,1)} %param.13, s32[]{:T(128)S(6)} %select_n.125), kind=kOutput, calls=%fused_computation.25 | convolution fusion | flops 2818572288 | bytes 9568260 | tf_op jit(solution)/shard_map/dot_general | solution.py:48
  197.3 3.7 %gather_fusion.3 = bf16[6,64,1024]{2,1,0:T(8,128)(2,1)} fusion(bf16[32,64,1024]{2,1,0:T(8,128)(2,1)} %param.15, s32[1024]{0:T(1024)S(1)} %pad_clamp_fusion), kind=kCustom, calls=%fused_computation.3 | custom fusion | bytes 1572888 | tf_op jit(solution)/shard_map/gather | solution.py:94
  201.0 0.0 collective-permute-done.13
  201.0 0.0 collective-permute-done.12
  201.0 2.1 convolution_convert_fusion
  203.1 0.0 copy-start.6
  203.1 0.0 copy-start.7
  203.2 0.0 collective-permute-done
  203.2 0.0 collective-permute-done.6
  203.2 0.0 collective-permute-done.8
  203.2 5.0 %multiply_reduce_fusion.1 = (f32[768]{0:T(1024)S(1)}, f32[768]{0:T(1024)S(1)}, bf16[768,1024]{1,0:T(8,128)(2,1)}) fusion(f32[1024]{0:T(1024)S(1)} %dynamic-slice-done, bf16[6,128,1024]{2,1,0:T(8,128)(2,1)S(1)} %convolution_convert_fusion, bf16[768,1024]{1,0:T(8,128)(2,1)} %collective-permute-done.8, bf16[768,1024]{1,0:T(8,128)(2,1)} %collective-permute-done.6, ...), kind=kLoop, calls=%fused_computation.29 | loop fusion | flops 11794944 | bytes 12593152 | tf_op jit(solution)/shard_map/reduce_sum | solution.py:145
  208.3 1.6 collective-permute-start.14
  209.8 2.1 collective-permute-done.14
  212.0 0.0 collective-permute-start.15
  212.0 3.6 %collective-permute-done.15 = f32[12,128]{1,0:T(8,128)S(1)} collective-permute-done((f32[12,128]{1,0:T(8,128)S(1)}, f32[12,128]{1,0:T(8,128)S(1)}, u32[]{:S(2)}, u32[]{:S(2)}) %collective-permute-start.15) | collective-permute-done | bytes 6176 | tf_op jit(solution)/shard_map/ppermute | solution.py:24
  215.6 2.9 %collective-permute-start.16 = (f32[12,128]{1,0:T(8,128)S(1)}, f32[12,128]{1,0:T(8,128)S(1)}, u32[]{:S(2)}, u32[]{:S(2)}) collective-permute-start(f32[12,128]{1,0:T(8,128)S(1)} %add.210), channel_id=1, source_target_pairs={{0,4},{1,5},{2,6},{3,7},{4,0},{5,1},{6,2},{7,3},{8,12},{9,13},{10,... | collective-permute-start | bytes 18440 | tf_op jit(solution)/shard_map/ppermute | solution.py:24
  218.5 1.6 collective-permute-done.16
  220.2 0.0 copy-done.6
  220.2 0.7 fusion.49
  (26 shorter events, 0.2 us)
Async XLA Ops:
  6.9 58.3 %copy-start.2 = (bf16[768,1792]{1,0:T(8,128)(2,1)}, bf16[768,1792]{1,0:T(8,128)(2,1)S(1)}, u32[]{:S(2)}) copy-start(bf16[768,1792]{1,0:T(8,128)(2,1)S(1)} %fusion.4) | copy-start | bytes 8257540
  14.1 38.5 %collective-permute-start.3 = (bf16[768,1024]{1,0:T(8,128)(2,1)}, bf16[768,1024]{1,0:T(8,128)(2,1)}, u32[]{:S(2)}, u32[]{:S(2)}) collective-permute-start(bf16[768,1024]{1,0:T(8,128)(2,1)} %fusion.31), channel_id=1, source_target_pairs={{0,1},{1,0},{2,3},{3,2},{4,5},{5,4},{6,7},{7,6},{8,9},{9,8},{10,11... | collective-permute-start | bytes 4718600 | tf_op jit(solution)/shard_map/ppermute | solution.py:24
  23.7 62.5 %collective-permute-start.2 = (bf16[768,1024]{1,0:T(8,128)(2,1)}, bf16[768,1024]{1,0:T(8,128)(2,1)}, u32[]{:S(2)}, u32[]{:S(2)}) collective-permute-start(bf16[768,1024]{1,0:T(8,128)(2,1)} %fusion.28), channel_id=1, source_target_pairs={{0,1},{1,0},{2,3},{3,2},{4,5},{5,4},{6,7},{7,6},{8,9},{9,8},{10,11... | collective-permute-start | bytes 4718600 | tf_op jit(solution)/shard_map/ppermute | solution.py:24
  59.4 36.0 %collective-permute-start.4 = (bf16[768,1024]{1,0:T(8,128)(2,1)}, bf16[768,1024]{1,0:T(8,128)(2,1)}, u32[]{:S(2)}, u32[]{:S(2)}) collective-permute-start(bf16[768,1024]{1,0:T(8,128)(2,1)} %get-tuple-element.13), channel_id=1, source_target_pairs={{0,2},{1,3},{6,4},{7,5},{8,10},{9,11},{14,12},{15,13},{16,18},{17,... | collective-permute-start | bytes 4718600 | tf_op jit(solution)/shard_map/ppermute | solution.py:19
  65.3 7.7 %copy-start.8 = (s32[12]{0:T(128)S(1)}, s32[12]{0:T(128)}, u32[]{:S(2)}) copy-start(s32[12]{0:T(128)} %param.18) | copy-start | bytes 148
  71.5 58.2 %collective-permute-start.1 = (bf16[768,1024]{1,0:T(8,128)(2,1)}, bf16[768,1024]{1,0:T(8,128)(2,1)}, u32[]{:S(2)}, u32[]{:S(2)}) collective-permute-start(bf16[768,1024]{1,0:T(8,128)(2,1)} %fusion.25), channel_id=1, source_target_pairs={{0,1},{1,0},{2,3},{3,2},{4,5},{5,4},{6,7},{7,6},{8,9},{9,8},{10,11... | collective-permute-start | bytes 4718600 | tf_op jit(solution)/shard_map/ppermute | solution.py:24
  77.9 48.6 %collective-permute-start.9 = (bf16[6,1792,64]{1,2,0:T(8,128)(2,1)}, bf16[6,1792,64]{1,2,0:T(8,128)(2,1)}, u32[]{:S(2)}, u32[]{:S(2)}) collective-permute-start(bf16[6,1792,64]{1,2,0:T(8,128)(2,1)} %gather_fusion), channel_id=1, source_target_pairs={{0,8},{8,0},{1,9},{9,1},{2,10},{10,2},{3,11},{11,3},{4,12},{12,4},... | collective-permute-start | bytes 4128776 | tf_op jit(solution)/shard_map/ppermute | solution.py:100
  78.6 16.8 %copy-start.1 = (f32[768,1024]{1,0:T(8,128)S(1)}, f32[768,1024]{1,0:T(8,128)}, u32[]{:S(2)}) copy-start(f32[768,1024]{1,0:T(8,128)} %get-tuple-element.14) | copy-start | bytes 9437188
  95.4 12.5 %copy-start.3 = (bf16[768,1792]{1,0:T(8,128)(2,1)S(1)}, bf16[768,1792]{1,0:T(8,128)(2,1)}, u32[]{:S(2)}) copy-start(bf16[768,1792]{1,0:T(8,128)(2,1)} %copy-done.2) | copy-start | bytes 8257540
  100.5 35.4 %collective-permute-start.5 = (bf16[768,1024]{1,0:T(8,128)(2,1)}, bf16[768,1024]{1,0:T(8,128)(2,1)}, u32[]{:S(2)}, u32[]{:S(2)}) collective-permute-start(bf16[768,1024]{1,0:T(8,128)(2,1)} %add_convert_fusion.2), channel_id=1, source_target_pairs={{0,2},{1,3},{2,4},{3,5},{8,10},{9,11},{10,12},{11,13},{16,18},{17,... | collective-permute-start | bytes 4718600 | tf_op jit(solution)/shard_map/ppermute | solution.py:19
  106.0 29.9 %collective-permute-start.7 = (bf16[768,1024]{1,0:T(8,128)(2,1)}, bf16[768,1024]{1,0:T(8,128)(2,1)}, u32[]{:S(2)}, u32[]{:S(2)}) collective-permute-start(bf16[768,1024]{1,0:T(8,128)(2,1)} %add_convert_fusion.2), channel_id=1, source_target_pairs={{6,4},{7,5},{4,2},{5,3},{14,12},{15,13},{12,10},{13,11},{22,20},{2... | collective-permute-start | bytes 4718600 | tf_op jit(solution)/shard_map/ppermute | solution.py:19
  114.1 89.1 %collective-permute-start = (bf16[768,1024]{1,0:T(8,128)(2,1)}, bf16[768,1024]{1,0:T(8,128)(2,1)}, u32[]{:S(2)}, u32[]{:S(2)}) collective-permute-start(bf16[768,1024]{1,0:T(8,128)(2,1)} %fusion.22), channel_id=1, source_target_pairs={{0,1},{1,0},{2,3},{3,2},{4,5},{5,4},{6,7},{7,6},{8,9},{9,8},{10,11... | collective-permute-start | bytes 4718600 | tf_op jit(solution)/shard_map/ppermute | solution.py:24
  120.5 6.1 %copy-start = (bf16[6,1792,64]{1,2,0:T(8,128)(2,1)S(1)}, bf16[6,1792,64]{1,2,0:T(8,128)(2,1)}, u32[]{:S(2)}) copy-start(bf16[6,1792,64]{1,2,0:T(8,128)(2,1)} %gather_fusion.1) | copy-start | bytes 4128772
  120.5 6.1 %copy-start.4 = (bf16[768,1792]{1,0:T(8,128)(2,1)S(1)}, bf16[768,1792]{1,0:T(8,128)(2,1)}, u32[]{:S(2)}) copy-start(bf16[768,1792]{1,0:T(8,128)(2,1)} %copy-done.2) | copy-start | bytes 8257540
  129.1 27.9 %collective-permute-start.10 = (f32[768,64]{0,1:T(8,128)S(1)}, f32[768,64]{0,1:T(8,128)S(1)}, u32[]{:S(2)}, u32[]{:S(2)}) collective-permute-start(f32[768,64]{0,1:T(8,128)S(1)} %bitcast.51), channel_id=1, source_target_pairs={{0,1},{1,0},{2,3},{3,2},{4,5},{5,4},{6,7},{7,6},{8,9},{9,8},{10,11... | collective-permute-start | bytes 589832 | tf_op jit(solution)/shard_map/ppermute | solution.py:24
  142.4 60.8 %collective-permute-start.6 = (bf16[768,1024]{1,0:T(8,128)(2,1)}, bf16[768,1024]{1,0:T(8,128)(2,1)}, u32[]{:S(2)}, u32[]{:S(2)}) collective-permute-start(bf16[768,1024]{1,0:T(8,128)(2,1)} %get-tuple-element.5), channel_id=1, source_target_pairs={{0,2},{1,3},{2,4},{3,5},{4,6},{5,7},{8,10},{9,11},{10,12},{11,13},... | collective-permute-start | bytes 4718600 | tf_op jit(solution)/shard_map/ppermute | solution.py:19
  151.2 52.0 %collective-permute-start.8 = (bf16[768,1024]{1,0:T(8,128)(2,1)}, bf16[768,1024]{1,0:T(8,128)(2,1)}, u32[]{:S(2)}, u32[]{:S(2)}) collective-permute-start(bf16[768,1024]{1,0:T(8,128)(2,1)} %get-tuple-element.6), channel_id=1, source_target_pairs={{6,4},{7,5},{4,2},{5,3},{2,0},{3,1},{14,12},{15,13},{12,10},{13,11... | collective-permute-start | bytes 4718600 | tf_op jit(solution)/shard_map/ppermute | solution.py:19
  157.0 34.3 %collective-permute-start.11 = (f32[768,64]{0,1:T(8,128)S(1)}, f32[768,64]{0,1:T(8,128)S(1)}, u32[]{:S(2)}, u32[]{:S(2)}) collective-permute-start(f32[768,64]{0,1:T(8,128)S(1)} %fusion.64), channel_id=1, source_target_pairs={{0,2},{1,3},{2,0},{3,1},{4,6},{5,7},{6,4},{7,5},{8,10},{9,11},{10,... | collective-permute-start | bytes 589832 | tf_op jit(solution)/shard_map/ppermute | solution.py:24
  162.6 38.4 %collective-permute-start.13 = (bf16[6,64,1024]{2,1,0:T(8,128)(2,1)}, bf16[6,64,1024]{2,1,0:T(8,128)(2,1)}, u32[]{:S(2)}, u32[]{:S(2)}) collective-permute-start(bf16[6,64,1024]{2,1,0:T(8,128)(2,1)} %gather_fusion.2), channel_id=1, source_target_pairs={{0,8},{8,0},{1,9},{9,1},{2,10},{10,2},{3,11},{11,3},{4,12},{12,4},... | collective-permute-start | bytes 2359304 | tf_op jit(solution)/shard_map/ppermute | solution.py:100
  191.3 9.7 %collective-permute-start.12 = (f32[768,64]{0,1:T(8,128)S(1)}, f32[768,64]{0,1:T(8,128)S(1)}, u32[]{:S(2)}, u32[]{:S(2)}) collective-permute-start(f32[768,64]{0,1:T(8,128)S(1)} %add.205), channel_id=1, source_target_pairs={{0,4},{1,5},{2,6},{3,7},{4,0},{5,1},{6,2},{7,3},{8,12},{9,13},{10,... | collective-permute-start | bytes 589832 | tf_op jit(solution)/shard_map/ppermute | solution.py:24
  201.0 2.2 copy-start.5
  201.0 2.2 dynamic-slice-start
  203.1 17.0 %copy-start.6 = (s32[6]{0:T(128)S(1)}, s32[6]{0:T(128)}, u32[]{:S(2)}) copy-start(s32[6]{0:T(128)} %param.20) | copy-start | bytes 76
  203.1 17.0 %copy-start.7 = (s32[6]{0:T(128)S(1)}, s32[6]{0:T(128)}, u32[]{:S(2)}) copy-start(s32[6]{0:T(128)} %param.19) | copy-start | bytes 76
  208.3 3.7 %collective-permute-start.14 = (f32[12,128]{1,0:T(8,128)S(1)}, f32[12,128]{1,0:T(8,128)S(1)}, u32[]{:S(2)}, u32[]{:S(2)}) collective-permute-start(f32[12,128]{1,0:T(8,128)S(1)} %reshape.129), channel_id=1, source_target_pairs={{0,1},{1,0},{2,3},{3,2},{4,5},{5,4},{6,7},{7,6},{8,9},{9,8},{10,11... | collective-permute-start | bytes 18440 | tf_op jit(solution)/shard_map/ppermute | solution.py:24
  212.0 3.7 %collective-permute-start.15 = (f32[12,128]{1,0:T(8,128)S(1)}, f32[12,128]{1,0:T(8,128)S(1)}, u32[]{:S(2)}, u32[]{:S(2)}) collective-permute-start(f32[12,128]{1,0:T(8,128)S(1)} %add.209), channel_id=1, source_target_pairs={{0,2},{1,3},{2,0},{3,1},{4,6},{5,7},{6,4},{7,5},{8,10},{9,11},{10,... | collective-permute-start | bytes 18440 | tf_op jit(solution)/shard_map/ppermute | solution.py:24
  215.6 4.5 %collective-permute-start.16 = (f32[12,128]{1,0:T(8,128)S(1)}, f32[12,128]{1,0:T(8,128)S(1)}, u32[]{:S(2)}, u32[]{:S(2)}) collective-permute-start(f32[12,128]{1,0:T(8,128)S(1)} %add.210), channel_id=1, source_target_pairs={{0,4},{1,5},{2,6},{3,7},{4,0},{5,1},{6,2},{7,3},{8,12},{9,13},{10,... | collective-permute-start | bytes 18440 | tf_op jit(solution)/shard_map/ppermute | solution.py:24

commit v2 on v1

v2 whole, which is shorter than its diff:
```python
import jax
import jax.numpy as jnp
from jax import lax
from jax.experimental import pallas as pl
from jax.experimental.pallas import tpu as pltpu
from jax.sharding import PartitionSpec as P

BLOCK = 128
EPSILON = 1e-05

f32 = jnp.float32
bf16 = jnp.bfloat16

LINE = 4
PAIR = 2
ORDER = ((3, 2, 1, 0), (0, 3, 2, 1), (1, 0, 3, 2), (0, 1, 2, 3))
PIECES = (3, 3)
TILE = 512


def along_line(value, hops):
    pairs = [(a * PAIR + y, b * PAIR + y) for a, b in hops for y in range(PAIR)]
    return lax.ppermute(value, "tensor", pairs)


def across(value, bit):
    size = LINE * PAIR
    return lax.ppermute(value, "tensor", [(t, t ^ bit) for t in range(size)])


class Sequence:
    def __init__(self):
        self.last = None

    def __call__(self, stage, *values):
        if self.last is not None:
            values = lax.optimization_barrier((self.last,) + values)[1:]
        result = stage(*values)
        self.last = jax.tree.leaves(result)[0]
        return result


def product_kernel(cuts, index_ref, rows_ref, weights_ref, *out_refs):
    result = jnp.dot(rows_ref[...], weights_ref[...], preferred_element_type=f32)
    for ref, start, stop in zip(out_refs, cuts[:-1], cuts[1:]):
        ref[...] = result[start:stop].astype(ref.dtype)


def product(hidden, weights, tensor_index, turn, own, kinds, width):
    rows, depth = hidden.shape
    steps = width // TILE
    cuts = [0]
    for piece in PIECES:
        cuts.append(cuts[-1] + piece * BLOCK)

    def block(j, index):
        z, y = index[0] >> 1, index[0] & 1
        goal = ORDER[LINE - 1][turn]
        for other in range(LINE - 1):
            goal = jnp.where(z == other, ORDER[other][turn], goal)
        return (goal * PAIR + (y if own else 1 - y)) * steps + j

    sizes = [stop - start for start, stop in zip(cuts[:-1], cuts[1:])]
    return pl.pallas_call(
        lambda *refs: product_kernel(cuts, *refs),
        grid_spec=pltpu.PrefetchScalarGridSpec(
            num_scalar_prefetch=1,
            grid=(steps,),
            in_specs=[
                pl.BlockSpec((rows, depth), lambda j, index: (0, 0)),
                pl.BlockSpec((depth, TILE), lambda j, index: (0, block(j, index))),
            ],
            out_specs=[pl.BlockSpec((size, TILE), lambda j, index: (0, j)) for size in sizes],
        ),
        out_shape=[jax.ShapeDtypeStruct((size, width), kind) for size, kind in zip(sizes, kinds)],
        compiler_params=pltpu.CompilerParams(vmem_limit_bytes=40 * 1024 * 1024),
        cost_estimate=pl.CostEstimate(
            flops=0,
            bytes_accessed=0,
            transcendentals=0,
        ),
    )(tensor_index.reshape(1), hidden, weights)


def pick_kernel(count, ids_ref, *refs):
    sources, targets = refs[:2], refs[2:]
    step = pl.program_id(0)

    @pl.when(step < count)
    def _():
        for source, target in zip(sources, targets[:2]):
            target[...] = source[...]

    @pl.when(step >= count)
    def _():
        for source, target in zip(sources, targets[2:]):
            target[...] = source[...]


def pick(ids, count, first, second):
    both = (first, second)
    rest = ids.shape[0] - count
    shapes = [(n,) + f.shape[1:] for n in (count, rest) for f in both]
    spot = lambda n, ids: (jnp.minimum(n, count - 1), 0, 0)
    later = lambda n, ids: (jnp.maximum(n - count, 0), 0, 0)
    return pl.pallas_call(
        lambda *refs: pick_kernel(count, *refs),
        grid_spec=pltpu.PrefetchScalarGridSpec(
            num_scalar_prefetch=1,
            grid=(count + rest,),
            in_specs=[pl.BlockSpec((1,) + f.shape[1:], lambda n, ids: (ids[n], 0, 0)) for f in both],
            out_specs=[pl.BlockSpec((1,) + s[1:], m) for s, m in zip(shapes, (spot, spot, later, later))],
        ),
        out_shape=[jax.ShapeDtypeStruct(s, first.dtype) for s in shapes],
        cost_estimate=pl.CostEstimate(flops=0, bytes_accessed=0, transcendentals=0),
    )(ids, first, second)


def exchange_sum(value, wire):
    for bit in (1, 2, 4):
        value = value + across(value.astype(wire), bit).astype(f32)
    return value


UP = ((0, 1), (1, 2), (2, 3))
DOWN = ((3, 2), (2, 1), (1, 0))


def grid_sums(hidden, weights, tensor_index, width, low_rank_terms, adapter_delta):
    last_z = (tensor_index >> 1) == LINE - 1
    then = Sequence()
    pieces = range(len(PIECES))
    arrived, mine = {}, {}
    add = lambda *terms: sum(t.astype(f32) for t in terms)
    narrow = lambda *terms: add(*terms).astype(bf16)

    def theirs(k):
        kinds = [bf16] * len(PIECES)
        out = then(lambda h: product(h, weights, tensor_index, k, False, kinds, width), hidden)
        for p in pieces:
            arrived[p, k] = across(out[p], 1)

    def ours(k):
        kinds = [f32] * len(PIECES)
        out = then(lambda h: product(h, weights, tensor_index, k, True, kinds, width), hidden)
        for p in pieces:
            mine[p, k] = out[p]

    def part(p, k):
        return (mine[p, k], arrived[p, k])

    first, second, third = {}, {}, {}

    def hop_1(p):
        first[p] = along_line(then(narrow, *part(p, 0)), [UP[0], DOWN[0]])

    def hop_2(p):
        value = then(narrow, *part(p, 1), first[p])
        second[p] = (along_line(value, UP[:2]), along_line(value, DOWN[:2]))

    def hop_3(p):
        up, down = second[p]

        def stage(up, down, *parts):
            here, there = add(*parts[:2]), add(*parts[2:])
            return narrow(here, up), narrow(jnp.where(last_z, here, there), down)

        up, down = then(stage, up, down, *part(p, 2), *part(p, 0))
        third[p] = (along_line(up, UP), along_line(down, DOWN))

    theirs(0)
    low_rank = then(low_rank_terms, hidden)
    arriving = across(low_rank, 2)
    ours(0)
    low_rank = then(add, low_rank, arriving)
    arriving = across(low_rank, 4)
    ours(1)
    low_rank = then(add, low_rank, arriving)
    arriving = across(low_rank, 1)
    theirs(1)
    hop_1(0)
    theirs(2)
    hop_1(1)
    low_rank = then(add, low_rank, arriving)
    delta = then(adapter_delta, low_rank)
    ours(2)
    hop_2(0)
    theirs(3)
    hop_2(1)
    ours(3)
    hop_3(0)
    hop_3(1)
    return jnp.concatenate([add(*part(p, 3), *third[p]) for p in pieces], 0), delta


def shards(
    gate_preactivation,
    up_preactivation,
    base_down_matrix,
    adapter_first_factor,
    adapter_second_factor,
    residual,
    scoring_head_matrix,
    block_adapter_index,
    block_span_start,
    block_span_end,
):
    rows_local, hidden_width = gate_preactivation.shape
    slice_width = residual.shape[1]
    model_width = scoring_head_matrix.shape[0]
    blocks = rows_local // BLOCK
    adapters_here = adapter_first_factor.shape[0]
    data_index = lax.axis_index("dp")
    data_size = lax.axis_size("dp")
    tensor_index = lax.axis_index("tensor")
    on_grid = lax.axis_size("tensor") == LINE * PAIR

    ids = block_adapter_index.reshape(data_size, blocks)
    owner = lax.dynamic_index_in_dim(ids, data_index, 0, keepdims=False) // adapters_here
    first_turned = jnp.swapaxes(adapter_first_factor, 1, 2)
    steps = [step for step in range(1, data_size)] + [0]
    turned = jnp.concatenate(
        [lax.dynamic_slice_in_dim(ids, (data_index + step) % data_size, 1)[0] for step in steps]
    )
    turned = jnp.clip(turned - data_index * adapters_here, 0, adapters_here - 1)
    away = blocks * (data_size - 1)
    wanted_first, wanted_second, first_factors, second_factors = pick(
        turned, away, first_turned, adapter_second_factor
    )
    for n, step in enumerate(steps[:-1]):
        hop = [(d, (d + step) % data_size) for d in range(data_size)]
        take = (owner == (data_index - step) % data_size)[:, None, None]

        def fetched(wanted, kept):
            came = lax.ppermute(wanted[n * blocks : (n + 1) * blocks], "dp", hop)
            return jnp.where(take, came, kept)

        first_factors = fetched(wanted_first, first_factors)
        second_factors = fetched(wanted_second, second_factors)

    def low_rank_terms(rows, first_factors):
        return jnp.einsum(
            "bcj,bej->bce",
            rows.reshape(blocks, BLOCK, hidden_width),
            first_factors,
            preferred_element_type=f32,
        ).reshape(rows_local, -1)

    def adapter_delta(low_rank, second_factors):
        return jnp.einsum(
            "bcn,bnt->bct",
            low_rank.astype(bf16).reshape(blocks, BLOCK, -1),
            second_factors,
            preferred_element_type=f32,
        ).reshape(rows_local, slice_width).astype(bf16)

    hidden = (
        jax.nn.silu(gate_preactivation.astype(f32)) * up_preactivation.astype(f32)
    ).astype(bf16)
    if on_grid:
        base_part, delta = grid_sums(
            hidden, base_down_matrix, tensor_index, slice_width,
            lambda rows: low_rank_terms(rows, first_factors),
            lambda low_rank: adapter_delta(low_rank, second_factors),
        )
    else:
        delta = adapter_delta(lax.psum(low_rank_terms(hidden, first_factors), "tensor"), second_factors)
        base_part = lax.psum_scatter(
            jnp.dot(hidden, base_down_matrix, preferred_element_type=f32),
            "tensor",
            scatter_dimension=1,
            tiled=True,
        )
    combined = residual.astype(f32) + delta.astype(f32) + base_part
    layer_out = combined.astype(bf16)
    head = lax.dynamic_slice_in_dim(
        scoring_head_matrix, tensor_index * slice_width, slice_width
    )
    stats = jnp.stack([jnp.sum(combined * combined, 1), jnp.sum(combined * head[None, :], 1)])
    stats = stats.reshape(2 * blocks, BLOCK)
    stats = exchange_sum(stats, f32) if on_grid else lax.psum(stats, "tensor")
    square_sum, head_sum = stats[:blocks], stats[blocks:]
    scores = head_sum * lax.rsqrt(square_sum / model_width + EPSILON)
    position = jnp.arange(BLOCK, dtype=jnp.int32)
    inside = (position[None, :] >= block_span_start[:, None]) & (
        position[None, :] < block_span_end[:, None]
    )
    span_scores = jnp.sum(jnp.where(inside, scores, f32(0.0)), 1)
    return (layer_out, span_scores)


def solution(mesh):
    return jax.shard_map(
        shards,
        mesh=mesh,
        in_specs=(
            P(("groups", "dp"), "tensor"),
            P(("groups", "dp"), "tensor"),
            P("tensor", None),
            P("dp", "tensor", None),
            P("dp", None, "tensor"),
            P(("groups", "dp"), "tensor"),
            P(),
            P("groups"),
            P(("groups", "dp")),
            P(("groups", "dp")),
        ),
        out_specs=(P(("groups", "dp"), "tensor"), P(("groups", "dp"))),
        check_vma=False,
    )
```

time: 221 us -> 191 us (0.86)
  matrix products: 55 us -> 3.49 us
  Pallas kernels: 0 us -> 49.6 us
  waiting for transfers between devices: 86.5 us -> 59.6 us
  local copies, waits for them, and re-layouts: 18.6 us -> 3.1 us
  starting transfers between devices: 35.7 us -> 48.7 us
  other arithmetic: 21.6 us -> 25.1 us
  between operations: 3.45 us -> 1.12 us
    dot_general x10 -> x2, matrix products: 55 us -> 3.49 us  [the longest x1 2.85 us: low_rank_terms(): jnp.einsum('bcj,bej->bce', rows.reshape(blocks, BLOCK, hidden_width), fir...]
    pallas_call x0 -> x9, Pallas kernels: none -> 49.6 us  [the longest x8 40.1 us: product(): pl.pallas_call(lambda *refs: product_kernel(cuts, *refs), grid_spec=pltpu...]
    ppermute x10 -> x14, waiting for transfers between devices: 71.1 us -> 47.8 us  [across(): return lax.ppermute(value, 'tensor', [(t, t ^ bit) for t in range(size)])]
    gather x4 -> x0, local copies, waits for them, and re-layouts: 17.1 us -> none  [held(): return factors[at]]
    ppermute x5 -> x10, starting transfers between devices: 22.7 us -> 29.2 us  [along_line(): return lax.ppermute(value, 'tensor', pairs)]
    ppermute x10 -> x14, starting transfers between devices: 13 us -> 19 us  [across(): return lax.ppermute(value, 'tensor', [(t, t ^ bit) for t in range(size)])]
    add x0 -> x5, other arithmetic: none -> 5.8 us  [grid_sums(): add = lambda *terms: sum((t.astype(f32) for t in terms))]
    ppermute x5 -> x10, waiting for transfers between devices: 15.4 us -> 11.8 us  [along_line(): return lax.ppermute(value, 'tensor', pairs)]
  transfers between devices with their start and end apart: 17 -> 26, of which waited for: 9 -> 14; matrix products, arithmetic and copies ran while one was open for 35% -> 12% of each run, Pallas kernels for 0% -> 21%
where the time goes in v2:
time: 191 us
  waiting for transfers between devices  59.6 us (31%)
  Pallas kernels  49.6 us (26%)
  starting transfers between devices  48.7 us (25%)
  other arithmetic  25.1 us (13%)
  matrix products  3.49 us (2%)
  local copies, waits for them, and re-layouts  3.1 us (2%)
    ppermute x14, waiting for transfers between devices, across(): return lax.ppermute(value, 'tensor', [(t, t ^ bit) for t in range(size)])  47.8 us
    pallas_call x8, Pallas kernels, product(): pl.pallas_call(lambda *refs: product_kernel(cuts, *refs), grid_spec=pltpu...  40.1 us
    ppermute x10, starting transfers between devices, along_line(): return lax.ppermute(value, 'tensor', pairs)  29.2 us
    ppermute x14, starting transfers between devices, across(): return lax.ppermute(value, 'tensor', [(t, t ^ bit) for t in range(size)])  19 us
    ppermute x10, waiting for transfers between devices, along_line(): return lax.ppermute(value, 'tensor', pairs)  11.8 us
    convert_element_type x6, other arithmetic, grid_sums(): narrow = lambda *terms: add(*terms).astype(bf16)  11.6 us
    pallas_call x1, Pallas kernels, pick(): pl.pallas_call(lambda *refs: pick_kernel(count, *refs), grid_spec=pltpu.P...  9.49 us
    add x5, other arithmetic, grid_sums(): add = lambda *terms: sum((t.astype(f32) for t in terms))  5.8 us
  transfers between devices with their start and end apart: 26, of which 14 were waited for; matrix products, arithmetic and copies ran while one was open for 12% of the time, Pallas kernels for 21%

profile of v2, /device:TPU:0, one launch (start us, length us, event | category | flops | bytes accessed | tf_op | source)
XLA Modules:
  0.0 190.7 jit_solution(966493785033895182)
XLA Ops:
  0.7 0.7 reshape.65
  1.4 0.6 fusion.24.refs_0_
  2.0 9.5 %shard_map.114 = (bf16[6,64,1792]{2,1,0:T(8,128)(2,1)}, bf16[6,64,1024]{2,1,0:T(8,128)(2,1)}, bf16[6,64,1792]{2,1,0:T(8,128)(2,1)}, bf16[6,64,1024]{2,1,0:T(8,128)(2,1)}) custom-call(s32[12]{0:T(128)} %fusion.24.refs_0_, bf16[32,64,1792]{2,1,0:T(8,128)(2,1)} %bitcast.37, bf16[32,64,1024]{2,1,0:T(8,128)(2,1)} %refs_2_.10), custom_call_target="tpu_custom_call" | custom-call | tf_op jit(solution)/shard_map/pallas_call | solution.py:106
  11.9 4.3 %fusion.4.refs_1_ = bf16[768,1792]{1,0:T(8,128)(2,1)S(1)} fusion(bf16[768,1792]{1,0:T(8,128)(2,1)} %param.11, bf16[768,1792]{1,0:T(8,128)(2,1)} %param.10), kind=kLoop, calls=%fused_computation.6 | loop fusion | flops 11010048 | bytes 8257536 | tf_op jit(solution)/shard_map/convert_element_type | solution.py:259
  16.2 5.4 %shard_map.113 = (bf16[384,1024]{1,0:T(8,128)(2,1)}, bf16[384,1024]{1,0:T(8,128)(2,1)S(1)}) custom-call(s32[1]{0:T(128)} %bitcast.refs_0_, bf16[768,1792]{1,0:T(8,128)(2,1)S(1)} %fusion.4.refs_1_, bf16[1792,8192]{1,0:T(8,128)(2,1)} %refs_2_.17), custom_call_target="tpu_custom_call" | custom-call | tf_op jit(solution)/shard_map/pallas_call | solution.py:64
  21.5 2.6 %collective-permute-start.3 = (bf16[384,1024]{1,0:T(8,128)(2,1)}, bf16[384,1024]{1,0:T(8,128)(2,1)}, u32[]{:S(2)}, u32[]{:S(2)}) collective-permute-start(bf16[384,1024]{1,0:T(8,128)(2,1)} %get-tuple-element.58), channel_id=1, source_target_pairs={{0,1},{1,0},{2,3},{3,2},{4,5},{5,4},{6,7},{7,6},{8,9},{9,8},{10,11... | collective-permute-start | bytes 2359304 | tf_op jit(solution)/shard_map/ppermute | solution.py:28
  24.1 2.9 %fusion.8 = f32[6,8,8,128]{3,2,1,0:T(8,128)S(1)} fusion(bf16[6,128,1792]{2,1,0:T(8,128)(2,1)S(1)} %bitcast.36, bf16[6,64,1792]{2,1,0:T(8,128)(2,1)} %collective-permute-done, bf16[6,64,1792]{2,1,0:T(8,128)(2,1)} %get-tuple-element.61, pred[6]{0:T(512)(128)(4,1)S(1)} %fusion.25), kind=kOutput, calls=%fused_computation.26 | convolution fusion | flops 176848896 | bytes 5701638 | tf_op jit(solution)/shard_map/bcj,bej->bce/dot_general | solution.py:242
  27.0 1.6 collective-permute-start.1
  28.7 0.5 collective-permute-start.4
  29.2 4.9 %shard_map.115 = (f32[384,1024]{1,0:T(8,128)S(1)}, f32[384,1024]{1,0:T(8,128)S(1)}) custom-call(s32[1]{0:T(128)} %bitcast.refs_0_, bf16[768,1792]{1,0:T(8,128)(2,1)S(1)} %fusion.4.refs_1_, bf16[1792,8192]{1,0:T(8,128)(2,1)} %refs_2_.17), custom_call_target="tpu_custom_call" | custom-call | tf_op jit(solution)/shard_map/pallas_call | solution.py:64
  34.1 2.7 %collective-permute-start.2 = (f32[768,64]{0,1:T(8,128)S(1)}, f32[768,64]{0,1:T(8,128)S(1)}, u32[]{:S(2)}, u32[]{:S(2)}) collective-permute-start(f32[768,64]{0,1:T(8,128)S(1)} %add.134), channel_id=1, source_target_pairs={{0,4},{1,5},{2,6},{3,7},{4,0},{5,1},{6,2},{7,3},{8,12},{9,13},{10,... | collective-permute-start | bytes 589832 | tf_op jit(solution)/shard_map/ppermute | solution.py:28
  36.8 4.9 %shard_map.116 = (f32[384,1024]{1,0:T(8,128)S(1)}, f32[384,1024]{1,0:T(8,128)S(1)}) custom-call(s32[1]{0:T(128)} %bitcast.refs_0_, bf16[768,1792]{1,0:T(8,128)(2,1)S(1)} %fusion.4.refs_1_, bf16[1792,8192]{1,0:T(8,128)(2,1)} %refs_2_.17), custom_call_target="tpu_custom_call" | custom-call | tf_op jit(solution)/shard_map/pallas_call | solution.py:64
  41.7 4.1 %collective-permute-done.2 = f32[768,64]{0,1:T(8,128)S(1)} collective-permute-done((f32[768,64]{0,1:T(8,128)S(1)}, f32[768,64]{0,1:T(8,128)S(1)}, u32[]{:S(2)}, u32[]{:S(2)}) %collective-permute-start.2) | collective-permute-done | bytes 196640 | tf_op jit(solution)/shard_map/ppermute | solution.py:28
  45.8 0.7 add.135
  46.5 4.8 %shard_map.117 = (bf16[384,1024]{1,0:T(8,128)(2,1)S(1)}, bf16[384,1024]{1,0:T(8,128)(2,1)S(1)}) custom-call(s32[1]{0:T(128)} %bitcast.refs_0_, bf16[768,1792]{1,0:T(8,128)(2,1)S(1)} %fusion.4.refs_1_, bf16[1792,8192]{1,0:T(8,128)(2,1)} %refs_2_.17), custom_call_target="tpu_custom_call" | custom-call | tf_op jit(solution)/shard_map/pallas_call | solution.py:64
  51.3 1.4 add_convert_fusion.7
  52.7 2.6 %collective-permute-start.8 = (bf16[384,1024]{1,0:T(8,128)(2,1)S(1)}, bf16[384,1024]{1,0:T(8,128)(2,1)S(1)}, u32[]{:S(2)}, u32[]{:S(2)}) collective-permute-start(bf16[384,1024]{1,0:T(8,128)(2,1)S(1)} %add_convert_fusion.7), channel_id=1, source_target_pairs={{0,2},{1,3},{6,4},{7,5},{8,10},{9,11},{14,12},{15,13},{16,18},{17,... | collective-permute-start | bytes 2359304 | tf_op jit(solution)/shard_map/ppermute | solution.py:23
  55.3 0.6 collective-permute-start.7
  55.9 5.5 %shard_map.118 = (bf16[384,1024]{1,0:T(8,128)(2,1)S(1)}, bf16[384,1024]{1,0:T(8,128)(2,1)}) custom-call(s32[1]{0:T(128)} %bitcast.refs_0_, bf16[768,1792]{1,0:T(8,128)(2,1)S(1)} %fusion.4.refs_1_, bf16[1792,8192]{1,0:T(8,128)(2,1)} %refs_2_.17), custom_call_target="tpu_custom_call" | custom-call | tf_op jit(solution)/shard_map/pallas_call | solution.py:64
  61.7 0.6 copy-done.14
  62.3 2.1 %collective-permute-start.10 = (bf16[384,1024]{1,0:T(8,128)(2,1)S(1)}, bf16[384,1024]{1,0:T(8,128)(2,1)S(1)}, u32[]{:S(2)}, u32[]{:S(2)}) collective-permute-start(bf16[384,1024]{1,0:T(8,128)(2,1)S(1)} %add_convert_fusion.6), channel_id=1, source_target_pairs={{0,2},{1,3},{6,4},{7,5},{8,10},{9,11},{14,12},{15,13},{16,18},{17,... | collective-permute-start | bytes 2359304 | tf_op jit(solution)/shard_map/ppermute | solution.py:23
  64.4 1.6 collective-permute-start.9
  66.5 4.9 %shard_map.119 = (f32[384,1024]{1,0:T(8,128)S(1)}, f32[384,1024]{1,0:T(8,128)S(1)}) custom-call(s32[1]{0:T(128)} %bitcast.refs_0_, bf16[768,1792]{1,0:T(8,128)(2,1)S(1)} %fusion.4.refs_1_, bf16[1792,8192]{1,0:T(8,128)(2,1)} %refs_2_.17), custom_call_target="tpu_custom_call" | custom-call | tf_op jit(solution)/shard_map/pallas_call | solution.py:64
  71.4 1.8 collective-permute-done.8
  73.2 3.3 %collective-permute-done.7 = bf16[384,1024]{1,0:T(8,128)(2,1)S(1)} collective-permute-done((bf16[384,1024]{1,0:T(8,128)(2,1)S(1)}, bf16[384,1024]{1,0:T(8,128)(2,1)S(1)}, u32[]{:S(2)}, u32[]{:S(2)}) %collective-permute-start.7) | collective-permute-done | bytes 786464 | tf_op jit(solution)/shard_map/ppermute | solution.py:28
  76.4 1.3 add_convert_fusion.5
  77.7 4.8 %collective-permute-start.12 = (bf16[384,1024]{1,0:T(8,128)(2,1)}, bf16[384,1024]{1,0:T(8,128)(2,1)}, u32[]{:S(2)}, u32[]{:S(2)}) collective-permute-start(bf16[384,1024]{1,0:T(8,128)(2,1)} %add_convert_fusion.5), channel_id=1, source_target_pairs={{0,2},{1,3},{2,4},{3,5},{8,10},{9,11},{10,12},{11,13},{16,18},{17,... | collective-permute-start | bytes 2359304 | tf_op jit(solution)/shard_map/ppermute | solution.py:23
  82.5 1.6 collective-permute-start.13
  84.0 4.8 %shard_map.120 = (bf16[384,1024]{1,0:T(8,128)(2,1)S(1)}, bf16[384,1024]{1,0:T(8,128)(2,1)S(1)}) custom-call(s32[1]{0:T(128)} %bitcast.refs_0_, bf16[768,1792]{1,0:T(8,128)(2,1)S(1)} %fusion.4.refs_1_, bf16[1792,8192]{1,0:T(8,128)(2,1)} %refs_2_.17), custom_call_target="tpu_custom_call" | custom-call | tf_op jit(solution)/shard_map/pallas_call | solution.py:64
  88.8 1.2 collective-permute-done.10
  90.0 0.5 collective-permute-start.20
  90.6 2.7 %collective-permute-done.9 = bf16[384,1024]{1,0:T(8,128)(2,1)S(1)} collective-permute-done((bf16[384,1024]{1,0:T(8,128)(2,1)S(1)}, bf16[384,1024]{1,0:T(8,128)(2,1)S(1)}, u32[]{:S(2)}, u32[]{:S(2)}) %collective-permute-start.9) | collective-permute-done | bytes 786464 | tf_op jit(solution)/shard_map/ppermute | solution.py:28
  93.3 1.3 add_convert_fusion.4
  94.5 4.8 %collective-permute-start.18 = (bf16[384,1024]{1,0:T(8,128)(2,1)}, bf16[384,1024]{1,0:T(8,128)(2,1)}, u32[]{:S(2)}, u32[]{:S(2)}) collective-permute-start(bf16[384,1024]{1,0:T(8,128)(2,1)} %add_convert_fusion.4), channel_id=1, source_target_pairs={{0,2},{1,3},{2,4},{3,5},{8,10},{9,11},{10,12},{11,13},{16,18},{17,... | collective-permute-start | bytes 2359304 | tf_op jit(solution)/shard_map/ppermute | solution.py:23
  99.3 10.8 %collective-permute-done.14 = bf16[384,1024]{1,0:T(8,128)(2,1)S(1)} collective-permute-done((bf16[384,1024]{1,0:T(8,128)(2,1)S(1)}, bf16[384,1024]{1,0:T(8,128)(2,1)S(1)}, u32[]{:S(2)}, u32[]{:S(2)}) %collective-permute-start.14) | collective-permute-done | bytes 786464 | tf_op jit(solution)/shard_map/ppermute | solution.py:28
  110.1 0.9 copy-done.19
  111.0 1.6 collective-permute-start.19
  112.6 5.1 %shard_map.121 = (f32[384,1024]{1,0:T(8,128)S(1)}, f32[384,1024]{1,0:T(8,128)S(1)}) custom-call(s32[1]{0:T(128)} %bitcast.refs_0_, bf16[768,1792]{1,0:T(8,128)(2,1)S(1)} %fusion.4.refs_1_, bf16[1792,8192]{1,0:T(8,128)(2,1)} %refs_2_.17), custom_call_target="tpu_custom_call" | custom-call | tf_op jit(solution)/shard_map/pallas_call | solution.py:64
  117.8 2.0 %collective-permute-start.11 = (bf16[384,1024]{1,0:T(8,128)(2,1)S(1)}, bf16[384,1024]{1,0:T(8,128)(2,1)S(1)}, u32[]{:S(2)}, u32[]{:S(2)}) collective-permute-start(bf16[384,1024]{1,0:T(8,128)(2,1)S(1)} %copy-done.13), channel_id=1, source_target_pairs={{0,1},{1,0},{2,3},{3,2},{4,5},{5,4},{6,7},{7,6},{8,9},{9,8},{10,11... | collective-permute-start | bytes 2359304 | tf_op jit(solution)/shard_map/ppermute | solution.py:28
  119.8 3.8 %add_convert_fusion.2 = (bf16[384,1024]{1,0:T(8,128)(2,1)}, bf16[384,1024]{1,0:T(8,128)(2,1)}) fusion(bf16[384,1024]{1,0:T(8,128)(2,1)} %collective-permute-done.13, f32[384,1024]{1,0:T(8,128)S(1)} %copy-done.3, bf16[384,1024]{1,0:T(8,128)(2,1)} %collective-permute-done.3, f32[384,1024]{1,0:T(8,128)S(1)} %copy-done.11, bf16[384,1024]{1,0:T(8,128)(2,1)S(1)} %copy-done.20, ...), kind=kLoop, calls=%fused_computation.16 | loop fusion | flops 4325376 | bytes 7864321 | tf_op jit(solution)/shard_map/convert_element_type | solution.py:135
  123.6 3.5 %collective-permute-done.20 = bf16[384,1024]{1,0:T(8,128)(2,1)} collective-permute-done((bf16[384,1024]{1,0:T(8,128)(2,1)}, bf16[384,1024]{1,0:T(8,128)(2,1)}, u32[]{:S(2)}, u32[]{:S(2)}) %collective-permute-start.20) | collective-permute-done | bytes 786464 | tf_op jit(solution)/shard_map/ppermute | solution.py:28
  127.1 1.9 %collective-permute-start.5 = (f32[768,64]{0,1:T(8,128)S(1)}, f32[768,64]{0,1:T(8,128)S(1)}, u32[]{:S(2)}, u32[]{:S(2)}) collective-permute-start(f32[768,64]{0,1:T(8,128)S(1)} %copy-done.18), channel_id=1, source_target_pairs={{0,1},{1,0},{2,3},{3,2},{4,5},{5,4},{6,7},{7,6},{8,9},{9,8},{10,11... | collective-permute-start | bytes 589832 | tf_op jit(solution)/shard_map/ppermute | solution.py:28
  129.0 4.4 %collective-permute-start.15 = (bf16[384,1024]{1,0:T(8,128)(2,1)}, bf16[384,1024]{1,0:T(8,128)(2,1)}, u32[]{:S(2)}, u32[]{:S(2)}) collective-permute-start(bf16[384,1024]{1,0:T(8,128)(2,1)} %get-tuple-element.118), channel_id=1, source_target_pairs={{0,2},{1,3},{2,4},{3,5},{4,6},{5,7},{8,10},{9,11},{10,12},{11,13},... | collective-permute-start | bytes 2359304 | tf_op jit(solution)/shard_map/ppermute | solution.py:23
  133.4 1.3 collective-permute-start.16
  134.7 3.7 %add_convert_fusion.1 = (bf16[384,1024]{1,0:T(8,128)(2,1)}, bf16[384,1024]{1,0:T(8,128)(2,1)}) fusion(bf16[384,1024]{1,0:T(8,128)(2,1)} %collective-permute-done.18, f32[384,1024]{1,0:T(8,128)S(1)} %copy-done.9, bf16[384,1024]{1,0:T(8,128)(2,1)} %collective-permute-done.20, bf16[384,1024]{1,0:T(8,128)(2,1)} %collective-permute-done.19, ...), kind=kLoop, calls=%fused_computation.13 | loop fusion | flops 4325376 | bytes 7864321 | tf_op jit(solution)/shard_map/convert_element_type | solution.py:135
  138.9 9.1 %collective-permute-done.5 = f32[768,64]{0,1:T(8,128)S(1)} collective-permute-done((f32[768,64]{0,1:T(8,128)S(1)}, f32[768,64]{0,1:T(8,128)S(1)}, u32[]{:S(2)}, u32[]{:S(2)}) %collective-permute-start.5) | collective-permute-done | bytes 196640 | tf_op jit(solution)/shard_map/ppermute | solution.py:28
  148.0 4.8 %collective-permute-start.21 = (bf16[384,1024]{1,0:T(8,128)(2,1)}, bf16[384,1024]{1,0:T(8,128)(2,1)}, u32[]{:S(2)}, u32[]{:S(2)}) collective-permute-start(bf16[384,1024]{1,0:T(8,128)(2,1)} %get-tuple-element.119), channel_id=1, source_target_pairs={{0,2},{1,3},{2,4},{3,5},{4,6},{5,7},{8,10},{9,11},{10,12},{11,13},... | collective-permute-start | bytes 2359304 | tf_op jit(solution)/shard_map/ppermute | solution.py:23
  152.8 1.3 collective-permute-start.22
  154.1 0.9 add.138
  155.1 0.6 convolution_convert_fusion
  155.8 0.7 copy-done.7
  156.5 1.9 %convert_add_fusion.2 = f32[384,1024]{1,0:T(8,128)S(1)} fusion(bf16[384,1024]{1,0:T(8,128)(2,1)} %collective-permute-done.16, bf16[384,1024]{1,0:T(8,128)(2,1)} %collective-permute-done.15, f32[384,1024]{1,0:T(8,128)S(1)} %copy-done.7, bf16[384,1024]{1,0:T(8,128)(2,1)S(1)} %collective-permute-done.11), kind=kLoop, calls=%fused_computation.15 | loop fusion | flops 2359296 | bytes 5505024 | tf_op jit(solution)/shard_map/add | solution.py:134
  158.4 6.4 %collective-permute-done.17 = bf16[384,1024]{1,0:T(8,128)(2,1)} collective-permute-done((bf16[384,1024]{1,0:T(8,128)(2,1)S(1)}, bf16[384,1024]{1,0:T(8,128)(2,1)}, u32[]{:S(2)}, u32[]{:S(2)}) %collective-permute-start.17) | collective-permute-done | bytes 786464 | tf_op jit(solution)/shard_map/ppermute | solution.py:28
  164.8 3.8 %collective-permute-done.21 = bf16[384,1024]{1,0:T(8,128)(2,1)} collective-permute-done((bf16[384,1024]{1,0:T(8,128)(2,1)}, bf16[384,1024]{1,0:T(8,128)(2,1)}, u32[]{:S(2)}, u32[]{:S(2)}) %collective-permute-start.21) | collective-permute-done | bytes 786464 | tf_op jit(solution)/shard_map/ppermute | solution.py:23
  168.7 5.0 %collective-permute-done.22 = bf16[384,1024]{1,0:T(8,128)(2,1)} collective-permute-done((bf16[384,1024]{1,0:T(8,128)(2,1)}, bf16[384,1024]{1,0:T(8,128)(2,1)}, u32[]{:S(2)}, u32[]{:S(2)}) %collective-permute-start.22) | collective-permute-done | bytes 786464 | tf_op jit(solution)/shard_map/ppermute | solution.py:23
  173.7 2.2 %convert_add_fusion = f32[384,1024]{1,0:T(8,128)S(1)} fusion(bf16[384,1024]{1,0:T(8,128)(2,1)} %collective-permute-done.22, bf16[384,1024]{1,0:T(8,128)(2,1)} %collective-permute-done.21, f32[384,1024]{1,0:T(8,128)S(1)} %copy-done.5, bf16[384,1024]{1,0:T(8,128)(2,1)} %collective-permute-done.17), kind=kLoop, calls=%fused_computation.11 | loop fusion | flops 2359296 | bytes 5505024 | tf_op jit(solution)/shard_map/add | solution.py:134
  175.9 2.1 %multiply_reduce_fusion.1 = (f32[768]{0:T(1024)S(1)}, f32[768]{0:T(1024)S(1)}, bf16[768,1024]{1,0:T(8,128)(2,1)}) fusion(f32[384,1024]{1,0:T(8,128)S(1)} %convert_add_fusion, f32[384,1024]{1,0:T(8,128)S(1)} %convert_add_fusion.2, bf16[6,128,1024]{2,1,0:T(8,128)(2,1)S(1)} %convolution_convert_fusion, bf16[768,1024]{1,0:T(8,128)(2,1)S(1)} %copy-done.16, ...), kind=kLoop, calls=%fused_computation.9 | loop fusion | flops 7862784 | bytes 7874560 | tf_op jit(solution)/shard_map/reduce_sum | solution.py:279
  178.1 1.6 collective-permute-start.23
  179.6 2.1 %collective-permute-done.23 = f32[12,128]{1,0:T(8,128)S(1)} collective-permute-done((f32[12,128]{1,0:T(8,128)S(1)}, f32[12,128]{1,0:T(8,128)S(1)}, u32[]{:S(2)}, u32[]{:S(2)}) %collective-permute-start.23) | collective-permute-done | bytes 6176 | tf_op jit(solution)/shard_map/ppermute | solution.py:28
  181.8 0.7 collective-permute-start.24
  182.5 3.0 %collective-permute-done.24 = f32[12,128]{1,0:T(8,128)S(1)} collective-permute-done((f32[12,128]{1,0:T(8,128)S(1)}, f32[12,128]{1,0:T(8,128)S(1)}, u32[]{:S(2)}, u32[]{:S(2)}) %collective-permute-start.24) | collective-permute-done | bytes 6176 | tf_op jit(solution)/shard_map/ppermute | solution.py:28
  185.4 1.7 collective-permute-start.25
  187.1 2.8 %collective-permute-done.25 = f32[12,128]{1,0:T(8,128)S(1)} collective-permute-done((f32[12,128]{1,0:T(8,128)S(1)}, f32[12,128]{1,0:T(8,128)S(1)}, u32[]{:S(2)}, u32[]{:S(2)}) %collective-permute-start.25) | collective-permute-done | bytes 6176 | tf_op jit(solution)/shard_map/ppermute | solution.py:28
  190.0 0.7 fusion.19
  (77 shorter events, 2.0 us)
Async XLA Ops:
  11.5 12.6 %collective-permute-start = (bf16[6,64,1792]{2,1,0:T(8,128)(2,1)}, bf16[6,64,1792]{2,1,0:T(8,128)(2,1)}, u32[]{:S(2)}, u32[]{:S(2)}) collective-permute-start(bf16[6,64,1792]{2,1,0:T(8,128)(2,1)} %get-tuple-element.60), channel_id=1, source_target_pairs={{0,8},{8,0},{1,9},{9,1},{2,10},{10,2},{3,11},{11,3},{4,12},{12,4},... | collective-permute-start | bytes 4128776 | tf_op jit(solution)/shard_map/ppermute | solution.py:235
  21.5 29.7 %collective-permute-start.3 = (bf16[384,1024]{1,0:T(8,128)(2,1)}, bf16[384,1024]{1,0:T(8,128)(2,1)}, u32[]{:S(2)}, u32[]{:S(2)}) collective-permute-start(bf16[384,1024]{1,0:T(8,128)(2,1)} %get-tuple-element.58), channel_id=1, source_target_pairs={{0,1},{1,0},{2,3},{3,2},{4,5},{5,4},{6,7},{7,6},{8,9},{9,8},{10,11... | collective-permute-start | bytes 2359304 | tf_op jit(solution)/shard_map/ppermute | solution.py:28
  27.0 7.1 %collective-permute-start.1 = (f32[768,64]{0,1:T(8,128)S(1)}, f32[768,64]{0,1:T(8,128)S(1)}, u32[]{:S(2)}, u32[]{:S(2)}) collective-permute-start(f32[768,64]{0,1:T(8,128)S(1)} %bitcast.38), channel_id=1, source_target_pairs={{0,2},{1,3},{2,0},{3,1},{4,6},{5,7},{6,4},{7,5},{8,10},{9,11},{10,... | collective-permute-start | bytes 589832 | tf_op jit(solution)/shard_map/ppermute | solution.py:28
  28.7 32.8 %collective-permute-start.4 = (bf16[384,1024]{1,0:T(8,128)(2,1)S(1)}, bf16[384,1024]{1,0:T(8,128)(2,1)S(1)}, u32[]{:S(2)}, u32[]{:S(2)}) collective-permute-start(bf16[384,1024]{1,0:T(8,128)(2,1)S(1)} %get-tuple-element.77), channel_id=1, source_target_pairs={{0,1},{1,0},{2,3},{3,2},{4,5},{5,4},{6,7},{7,6},{8,9},{9,8},{10,11... | collective-permute-start | bytes 2359304 | tf_op jit(solution)/shard_map/ppermute | solution.py:28
  34.0 17.2 %copy-start.2 = (f32[384,1024]{1,0:T(8,128)}, f32[384,1024]{1,0:T(8,128)S(1)}, u32[]{:S(2)}) copy-start(f32[384,1024]{1,0:T(8,128)S(1)} %get-tuple-element.101) | copy-start | bytes 4718596
  34.1 27.4 %copy-start = (f32[384,1024]{1,0:T(8,128)}, f32[384,1024]{1,0:T(8,128)S(1)}, u32[]{:S(2)}) copy-start(f32[384,1024]{1,0:T(8,128)S(1)} %get-tuple-element.111) | copy-start | bytes 4718596
  34.1 11.6 %collective-permute-start.2 = (f32[768,64]{0,1:T(8,128)S(1)}, f32[768,64]{0,1:T(8,128)S(1)}, u32[]{:S(2)}, u32[]{:S(2)}) collective-permute-start(f32[768,64]{0,1:T(8,128)S(1)} %add.134), channel_id=1, source_target_pairs={{0,4},{1,5},{2,6},{3,7},{4,0},{5,1},{6,2},{7,3},{8,12},{9,13},{10,... | collective-permute-start | bytes 589832 | tf_op jit(solution)/shard_map/ppermute | solution.py:28
  52.7 20.5 %collective-permute-start.8 = (bf16[384,1024]{1,0:T(8,128)(2,1)S(1)}, bf16[384,1024]{1,0:T(8,128)(2,1)S(1)}, u32[]{:S(2)}, u32[]{:S(2)}) collective-permute-start(bf16[384,1024]{1,0:T(8,128)(2,1)S(1)} %add_convert_fusion.7), channel_id=1, source_target_pairs={{0,2},{1,3},{6,4},{7,5},{8,10},{9,11},{14,12},{15,13},{16,18},{17,... | collective-permute-start | bytes 2359304 | tf_op jit(solution)/shard_map/ppermute | solution.py:23
  55.3 21.1 %collective-permute-start.7 = (bf16[384,1024]{1,0:T(8,128)(2,1)S(1)}, bf16[384,1024]{1,0:T(8,128)(2,1)S(1)}, u32[]{:S(2)}, u32[]{:S(2)}) collective-permute-start(bf16[384,1024]{1,0:T(8,128)(2,1)S(1)} %get-tuple-element.71), channel_id=1, source_target_pairs={{0,1},{1,0},{2,3},{3,2},{4,5},{5,4},{6,7},{7,6},{8,9},{9,8},{10,11... | collective-permute-start | bytes 2359304 | tf_op jit(solution)/shard_map/ppermute | solution.py:28
  61.4 0.9 copy-start.14
  62.3 27.7 %collective-permute-start.10 = (bf16[384,1024]{1,0:T(8,128)(2,1)S(1)}, bf16[384,1024]{1,0:T(8,128)(2,1)S(1)}, u32[]{:S(2)}, u32[]{:S(2)}) collective-permute-start(bf16[384,1024]{1,0:T(8,128)(2,1)S(1)} %add_convert_fusion.6), channel_id=1, source_target_pairs={{0,2},{1,3},{6,4},{7,5},{8,10},{9,11},{14,12},{15,13},{16,18},{17,... | collective-permute-start | bytes 2359304 | tf_op jit(solution)/shard_map/ppermute | solution.py:23
  64.4 28.9 %collective-permute-start.9 = (bf16[384,1024]{1,0:T(8,128)(2,1)S(1)}, bf16[384,1024]{1,0:T(8,128)(2,1)S(1)}, u32[]{:S(2)}, u32[]{:S(2)}) collective-permute-start(bf16[384,1024]{1,0:T(8,128)(2,1)S(1)} %get-tuple-element.92), channel_id=1, source_target_pairs={{0,1},{1,0},{2,3},{3,2},{4,5},{5,4},{6,7},{7,6},{8,9},{9,8},{10,11... | collective-permute-start | bytes 2359304 | tf_op jit(solution)/shard_map/ppermute | solution.py:28
  66.0 44.1 %collective-permute-start.14 = (bf16[384,1024]{1,0:T(8,128)(2,1)S(1)}, bf16[384,1024]{1,0:T(8,128)(2,1)S(1)}, u32[]{:S(2)}, u32[]{:S(2)}) collective-permute-start(bf16[384,1024]{1,0:T(8,128)(2,1)S(1)} %get-tuple-element.75), channel_id=1, source_target_pairs={{0,1},{1,0},{2,3},{3,2},{4,5},{5,4},{6,7},{7,6},{8,9},{9,8},{10,11... | collective-permute-start | bytes 2359304 | tf_op jit(solution)/shard_map/ppermute | solution.py:28
  71.4 6.3 %copy-start.8 = (f32[384,1024]{1,0:T(8,128)}, f32[384,1024]{1,0:T(8,128)S(1)}, u32[]{:S(2)}) copy-start(f32[384,1024]{1,0:T(8,128)S(1)} %get-tuple-element.108) | copy-start | bytes 4718596
  71.4 6.3 %copy-start.10 = (f32[384,1024]{1,0:T(8,128)}, f32[384,1024]{1,0:T(8,128)S(1)}, u32[]{:S(2)}) copy-start(f32[384,1024]{1,0:T(8,128)S(1)} %get-tuple-element.98) | copy-start | bytes 4718596
  77.7 40.0 %collective-permute-start.12 = (bf16[384,1024]{1,0:T(8,128)(2,1)}, bf16[384,1024]{1,0:T(8,128)(2,1)}, u32[]{:S(2)}, u32[]{:S(2)}) collective-permute-start(bf16[384,1024]{1,0:T(8,128)(2,1)} %add_convert_fusion.5), channel_id=1, source_target_pairs={{0,2},{1,3},{2,4},{3,5},{8,10},{9,11},{10,12},{11,13},{16,18},{17,... | collective-permute-start | bytes 2359304 | tf_op jit(solution)/shard_map/ppermute | solution.py:23
  82.5 35.3 %collective-permute-start.13 = (bf16[384,1024]{1,0:T(8,128)(2,1)}, bf16[384,1024]{1,0:T(8,128)(2,1)}, u32[]{:S(2)}, u32[]{:S(2)}) collective-permute-start(bf16[384,1024]{1,0:T(8,128)(2,1)} %add_convert_fusion.5), channel_id=1, source_target_pairs={{6,4},{7,5},{4,2},{5,3},{14,12},{15,13},{12,10},{13,11},{22,20},{2... | collective-permute-start | bytes 2359304 | tf_op jit(solution)/shard_map/ppermute | solution.py:23
  88.8 5.7 %copy-start.12 = (bf16[384,1024]{1,0:T(8,128)(2,1)}, bf16[384,1024]{1,0:T(8,128)(2,1)S(1)}, u32[]{:S(2)}) copy-start(bf16[384,1024]{1,0:T(8,128)(2,1)S(1)} %get-tuple-element.90) | copy-start | bytes 2359300
  90.0 37.1 %collective-permute-start.20 = (bf16[384,1024]{1,0:T(8,128)(2,1)}, bf16[384,1024]{1,0:T(8,128)(2,1)}, u32[]{:S(2)}, u32[]{:S(2)}) collective-permute-start(bf16[384,1024]{1,0:T(8,128)(2,1)} %get-tuple-element.107), channel_id=1, source_target_pairs={{0,1},{1,0},{2,3},{3,2},{4,5},{5,4},{6,7},{7,6},{8,9},{9,8},{10,11... | collective-permute-start | bytes 2359304 | tf_op jit(solution)/shard_map/ppermute | solution.py:28
  94.5 34.5 %collective-permute-start.18 = (bf16[384,1024]{1,0:T(8,128)(2,1)}, bf16[384,1024]{1,0:T(8,128)(2,1)}, u32[]{:S(2)}, u32[]{:S(2)}) collective-permute-start(bf16[384,1024]{1,0:T(8,128)(2,1)} %add_convert_fusion.4), channel_id=1, source_target_pairs={{0,2},{1,3},{2,4},{3,5},{8,10},{9,11},{10,12},{11,13},{16,18},{17,... | collective-permute-start | bytes 2359304 | tf_op jit(solution)/shard_map/ppermute | solution.py:23
  110.1 0.9 copy-start.19
  111.0 22.4 %collective-permute-start.19 = (bf16[384,1024]{1,0:T(8,128)(2,1)}, bf16[384,1024]{1,0:T(8,128)(2,1)}, u32[]{:S(2)}, u32[]{:S(2)}) collective-permute-start(bf16[384,1024]{1,0:T(8,128)(2,1)} %add_convert_fusion.4), channel_id=1, source_target_pairs={{6,4},{7,5},{4,2},{5,3},{14,12},{15,13},{12,10},{13,11},{22,20},{2... | collective-permute-start | bytes 2359304 | tf_op jit(solution)/shard_map/ppermute | solution.py:23
  112.6 5.1 %copy-start.24 = (bf16[6,64,1024]{2,1,0:T(8,128)(2,1)S(1)}, bf16[6,64,1024]{2,1,0:T(8,128)(2,1)}, u32[]{:S(2)}) copy-start(bf16[6,64,1024]{2,1,0:T(8,128)(2,1)} %get-tuple-element.82) | copy-start | bytes 2359300
  112.6 5.2 %copy-start.13 = (bf16[384,1024]{1,0:T(8,128)(2,1)S(1)}, bf16[384,1024]{1,0:T(8,128)(2,1)}, u32[]{:S(2)}) copy-start(bf16[384,1024]{1,0:T(8,128)(2,1)} %copy-done.12) | copy-start | bytes 2359300
  112.6 7.2 %copy-start.3 = (f32[384,1024]{1,0:T(8,128)S(1)}, f32[384,1024]{1,0:T(8,128)}, u32[]{:S(2)}) copy-start(f32[384,1024]{1,0:T(8,128)} %copy-done.2) | copy-start | bytes 4718596
  112.6 7.2 %copy-start.11 = (f32[384,1024]{1,0:T(8,128)S(1)}, f32[384,1024]{1,0:T(8,128)}, u32[]{:S(2)}) copy-start(f32[384,1024]{1,0:T(8,128)} %copy-done.10) | copy-start | bytes 4718596
  112.6 7.2 %copy-start.20 = (bf16[384,1024]{1,0:T(8,128)(2,1)S(1)}, bf16[384,1024]{1,0:T(8,128)(2,1)}, u32[]{:S(2)}) copy-start(bf16[384,1024]{1,0:T(8,128)(2,1)} %copy-done.19) | copy-start | bytes 2359300
  117.6 6.0 %copy-start.4 = (f32[384,1024]{1,0:T(8,128)}, f32[384,1024]{1,0:T(8,128)S(1)}, u32[]{:S(2)}) copy-start(f32[384,1024]{1,0:T(8,128)S(1)} %get-tuple-element.104) | copy-start | bytes 4718596
  117.6 6.0 %copy-start.6 = (f32[384,1024]{1,0:T(8,128)}, f32[384,1024]{1,0:T(8,128)S(1)}, u32[]{:S(2)}) copy-start(f32[384,1024]{1,0:T(8,128)S(1)} %get-tuple-element.97) | copy-start | bytes 4718596
  117.7 20.7 %collective-permute-start.6 = (bf16[6,64,1024]{2,1,0:T(8,128)(2,1)S(1)}, bf16[6,64,1024]{2,1,0:T(8,128)(2,1)S(1)}, u32[]{:S(2)}, u32[]{:S(2)}) collective-permute-start(bf16[6,64,1024]{2,1,0:T(8,128)(2,1)S(1)} %copy-done.24), channel_id=1, source_target_pairs={{0,8},{8,0},{1,9},{9,1},{2,10},{10,2},{3,11},{11,3},{4,12},{12,4},... | collective-permute-start | bytes 2359304 | tf_op jit(solution)/shard_map/ppermute | solution.py:235
  117.8 35.1 %collective-permute-start.11 = (bf16[384,1024]{1,0:T(8,128)(2,1)S(1)}, bf16[384,1024]{1,0:T(8,128)(2,1)S(1)}, u32[]{:S(2)}, u32[]{:S(2)}) collective-permute-start(bf16[384,1024]{1,0:T(8,128)(2,1)S(1)} %copy-done.13), channel_id=1, source_target_pairs={{0,1},{1,0},{2,3},{3,2},{4,5},{5,4},{6,7},{7,6},{8,9},{9,8},{10,11... | collective-permute-start | bytes 2359304 | tf_op jit(solution)/shard_map/ppermute | solution.py:28
  119.8 7.3 %copy-start.18 = (f32[768,64]{0,1:T(8,128)S(1)}, f32[768,64]{0,1:T(8,128)}, u32[]{:S(2)}) copy-start(f32[768,64]{0,1:T(8,128)} %add.135) | copy-start | bytes 589828
  119.8 14.9 %copy-start.1 = (f32[384,1024]{1,0:T(8,128)S(1)}, f32[384,1024]{1,0:T(8,128)}, u32[]{:S(2)}) copy-start(f32[384,1024]{1,0:T(8,128)} %copy-done) | copy-start | bytes 4718596
  119.8 14.9 %copy-start.9 = (f32[384,1024]{1,0:T(8,128)S(1)}, f32[384,1024]{1,0:T(8,128)}, u32[]{:S(2)}) copy-start(f32[384,1024]{1,0:T(8,128)} %copy-done.8) | copy-start | bytes 4718596
  119.8 14.9 %copy-start.15 = (bf16[384,1024]{1,0:T(8,128)(2,1)S(1)}, bf16[384,1024]{1,0:T(8,128)(2,1)}, u32[]{:S(2)}) copy-start(bf16[384,1024]{1,0:T(8,128)(2,1)} %copy-done.14) | copy-start | bytes 2359300
  127.1 21.0 %collective-permute-start.5 = (f32[768,64]{0,1:T(8,128)S(1)}, f32[768,64]{0,1:T(8,128)S(1)}, u32[]{:S(2)}, u32[]{:S(2)}) collective-permute-start(f32[768,64]{0,1:T(8,128)S(1)} %copy-done.18), channel_id=1, source_target_pairs={{0,1},{1,0},{2,3},{3,2},{4,5},{5,4},{6,7},{7,6},{8,9},{9,8},{10,11... | collective-permute-start | bytes 589832 | tf_op jit(solution)/shard_map/ppermute | solution.py:28
  129.0 26.7 %collective-permute-start.15 = (bf16[384,1024]{1,0:T(8,128)(2,1)}, bf16[384,1024]{1,0:T(8,128)(2,1)}, u32[]{:S(2)}, u32[]{:S(2)}) collective-permute-start(bf16[384,1024]{1,0:T(8,128)(2,1)} %get-tuple-element.118), channel_id=1, source_target_pairs={{0,2},{1,3},{2,4},{3,5},{4,6},{5,7},{8,10},{9,11},{10,12},{11,13},... | collective-permute-start | bytes 2359304 | tf_op jit(solution)/shard_map/ppermute | solution.py:23
  133.4 22.4 %collective-permute-start.16 = (bf16[384,1024]{1,0:T(8,128)(2,1)}, bf16[384,1024]{1,0:T(8,128)(2,1)}, u32[]{:S(2)}, u32[]{:S(2)}) collective-permute-start(bf16[384,1024]{1,0:T(8,128)(2,1)} %get-tuple-element.117), channel_id=1, source_target_pairs={{6,4},{7,5},{4,2},{5,3},{2,0},{3,1},{14,12},{15,13},{12,10},{13,11... | collective-permute-start | bytes 2359304 | tf_op jit(solution)/shard_map/ppermute | solution.py:23
  134.7 20.4 %copy-start.17 = (bf16[6,64,1024]{2,1,0:T(8,128)(2,1)S(1)}, bf16[6,64,1024]{2,1,0:T(8,128)(2,1)}, u32[]{:S(2)}) copy-start(bf16[6,64,1024]{2,1,0:T(8,128)(2,1)} %get-tuple-element.83) | copy-start | bytes 2359300
  138.4 26.4 %collective-permute-start.17 = (bf16[384,1024]{1,0:T(8,128)(2,1)S(1)}, bf16[384,1024]{1,0:T(8,128)(2,1)}, u32[]{:S(2)}, u32[]{:S(2)}) collective-permute-start(bf16[384,1024]{1,0:T(8,128)(2,1)S(1)} %get-tuple-element.105), channel_id=1, source_target_pairs={{0,1},{1,0},{2,3},{3,2},{4,5},{5,4},{6,7},{7,6},{8,9},{9,8},{10,11... | collective-permute-start | bytes 2359304 | tf_op jit(solution)/shard_map/ppermute | solution.py:28
  148.0 6.1 %copy-start.21 = (f32[768,64]{0,1:T(8,128)}, f32[768,64]{0,1:T(8,128)S(1)}, u32[]{:S(2)}) copy-start(f32[768,64]{0,1:T(8,128)S(1)} %collective-permute-done.5) | copy-start | bytes 589828
  148.0 20.6 %collective-permute-start.21 = (bf16[384,1024]{1,0:T(8,128)(2,1)}, bf16[384,1024]{1,0:T(8,128)(2,1)}, u32[]{:S(2)}, u32[]{:S(2)}) collective-permute-start(bf16[384,1024]{1,0:T(8,128)(2,1)} %get-tuple-element.119), channel_id=1, source_target_pairs={{0,2},{1,3},{2,4},{3,5},{4,6},{5,7},{8,10},{9,11},{10,12},{11,13},... | collective-permute-start | bytes 2359304 | tf_op jit(solution)/shard_map/ppermute | solution.py:23
  152.8 20.8 %collective-permute-start.22 = (bf16[384,1024]{1,0:T(8,128)(2,1)}, bf16[384,1024]{1,0:T(8,128)(2,1)}, u32[]{:S(2)}, u32[]{:S(2)}) collective-permute-start(bf16[384,1024]{1,0:T(8,128)(2,1)} %get-tuple-element.120), channel_id=1, source_target_pairs={{6,4},{7,5},{4,2},{5,3},{2,0},{3,1},{14,12},{15,13},{12,10},{13,11... | collective-permute-start | bytes 2359304 | tf_op jit(solution)/shard_map/ppermute | solution.py:23
  155.1 1.4 copy-start.7
  155.8 17.9 %copy-start.5 = (f32[384,1024]{1,0:T(8,128)S(1)}, f32[384,1024]{1,0:T(8,128)}, u32[]{:S(2)}) copy-start(f32[384,1024]{1,0:T(8,128)} %copy-done.4) | copy-start | bytes 4718596
  173.7 2.2 %copy-start.16 = (bf16[768,1024]{1,0:T(8,128)(2,1)S(1)}, bf16[768,1024]{1,0:T(8,128)(2,1)}, u32[]{:S(2)}) copy-start(bf16[768,1024]{1,0:T(8,128)(2,1)} %param.15) | copy-start | bytes 4718596
  173.7 2.2 %dynamic-slice-start = ((f32[8192]{0:T(1024)}, s32[]{:T(128)}), f32[1024]{0:T(1024)S(1)}, s32[]{:S(2)}) async-start(f32[8192]{0:T(1024)} %param.16, s32[]{:T(128)} %select_n.73), calls=%async_computation | async-start | bytes 8704 | tf_op jit(solution)/shard_map/dynamic_slice | solution.py:276
  175.9 14.1 %copy-start.22 = (s32[6]{0:T(128)S(1)}, s32[6]{0:T(128)}, u32[]{:S(2)}) copy-start(s32[6]{0:T(128)} %param.19) | copy-start | bytes 76
  175.9 14.1 %copy-start.23 = (s32[6]{0:T(128)S(1)}, s32[6]{0:T(128)}, u32[]{:S(2)}) copy-start(s32[6]{0:T(128)} %param.18) | copy-start | bytes 76
  178.1 3.7 %collective-permute-start.23 = (f32[12,128]{1,0:T(8,128)S(1)}, f32[12,128]{1,0:T(8,128)S(1)}, u32[]{:S(2)}, u32[]{:S(2)}) collective-permute-start(f32[12,128]{1,0:T(8,128)S(1)} %reshape.68), channel_id=1, source_target_pairs={{0,1},{1,0},{2,3},{3,2},{4,5},{5,4},{6,7},{7,6},{8,9},{9,8},{10,11... | collective-permute-start | bytes 18440 | tf_op jit(solution)/shard_map/ppermute | solution.py:28
  181.8 3.7 %collective-permute-start.24 = (f32[12,128]{1,0:T(8,128)S(1)}, f32[12,128]{1,0:T(8,128)S(1)}, u32[]{:S(2)}, u32[]{:S(2)}) collective-permute-start(f32[12,128]{1,0:T(8,128)S(1)} %add.160), channel_id=1, source_target_pairs={{0,2},{1,3},{2,0},{3,1},{4,6},{5,7},{6,4},{7,5},{8,10},{9,11},{10,... | collective-permute-start | bytes 18440 | tf_op jit(solution)/shard_map/ppermute | solution.py:28
  185.4 4.5 %collective-permute-start.25 = (f32[12,128]{1,0:T(8,128)S(1)}, f32[12,128]{1,0:T(8,128)S(1)}, u32[]{:S(2)}, u32[]{:S(2)}) collective-permute-start(f32[12,128]{1,0:T(8,128)S(1)} %add.161), channel_id=1, source_target_pairs={{0,4},{1,5},{2,6},{3,7},{4,0},{5,1},{6,2},{7,3},{8,12},{9,13},{10,... | collective-permute-start | bytes 18440 | tf_op jit(solution)/shard_map/ppermute | solution.py:28

commit v3 on v1

v3 whole, which is shorter than its diff:
```python
import jax
import jax.numpy as jnp
from jax import lax
from jax.experimental import pallas as pl
from jax.experimental.pallas import tpu as pltpu
from jax.sharding import PartitionSpec as P

BLOCK = 128
EPSILON = 1e-05

f32 = jnp.float32
bf16 = jnp.bfloat16

LINE = 4
PAIR = 2
ORDER = ((3, 2, 1, 0), (0, 3, 2, 1), (1, 0, 3, 2), (0, 1, 2, 3))
PIECES = 2
TILE = 512

ANYWHERE = pl.BlockSpec(memory_space=pl.ANY)
NO_COST = pl.CostEstimate(flops=0, bytes_accessed=0, transcendentals=0)


def along_line(value, hops):
    pairs = [(a * PAIR + y, b * PAIR + y) for a, b in hops for y in range(PAIR)]
    return lax.ppermute(value, "tensor", pairs)


def across(value, bit):
    size = LINE * PAIR
    return lax.ppermute(value, "tensor", [(t, t ^ bit) for t in range(size)])


def product_kernel(count, further, index_ref, rows_ref, weights_ref, *refs):
    result = jnp.dot(rows_ref[...], weights_ref[...], preferred_element_type=f32)
    size = result.shape[0] // count
    for n, ref in enumerate(refs[-count:]):
        ref[:size] = result[n * size : (n + 1) * size].astype(ref.dtype)
        if further:
            ref[size:] = refs[0][...].astype(ref.dtype)


def product(hidden, weights, tensor_index, turn, own, kind, width, earlier, piece, count, further=None):
    rows, depth = hidden.shape
    steps = width // TILE
    rows = rows if piece is None else rows // PIECES
    size = rows // count
    more = 0 if further is None else further.shape[0]

    def block(j, index):
        z, y = index[0] >> 1, index[0] & 1
        goal = ORDER[LINE - 1][turn]
        for other in range(LINE - 1):
            goal = jnp.where(z == other, ORDER[other][turn], goal)
        return (goal * PAIR + (y if own else 1 - y)) * steps + j

    return pl.pallas_call(
        lambda *refs: product_kernel(count, more, *refs),
        grid_spec=pltpu.PrefetchScalarGridSpec(
            num_scalar_prefetch=1,
            grid=(steps,),
            in_specs=[
                pl.BlockSpec((rows, depth), lambda j, index: (piece or 0, 0)),
                pl.BlockSpec((depth, TILE), lambda j, index: (0, block(j, index))),
            ]
            + [pl.BlockSpec((more, TILE), lambda j, index: (0, j))] * (more > 0)
            + [ANYWHERE] * len(earlier),
            out_specs=[pl.BlockSpec((size + more, TILE), lambda j, index: (0, j))] * count,
        ),
        out_shape=[pltpu.HBM((size + more, width), kind)] * count,
        compiler_params=pltpu.CompilerParams(vmem_limit_bytes=40 * 1024 * 1024),
        cost_estimate=NO_COST,
    )(tensor_index.reshape(1), hidden, weights, *([further] if more else []), *earlier)


def pick_kernel(ids_ref, *refs):
    refs[-1][...] = refs[0][...]


def pick(ids, factors, earlier=()):
    block = (1,) + factors.shape[1:]
    return pl.pallas_call(
        pick_kernel,
        grid_spec=pltpu.PrefetchScalarGridSpec(
            num_scalar_prefetch=1,
            grid=ids.shape,
            in_specs=[pl.BlockSpec(block, lambda n, ids: (ids[n], 0, 0))] + [ANYWHERE] * len(earlier),
            out_specs=pl.BlockSpec(block, lambda n, ids: (n, 0, 0)),
        ),
        out_shape=pltpu.HBM(ids.shape + factors.shape[1:], factors.dtype),
        cost_estimate=NO_COST,
    )(ids, factors, *earlier)


def exchange_sum(value, wire):
    for bit in (1, 2, 4):
        value = value + across(value.astype(wire), bit).astype(f32)
    return value


UP = ((0, 1), (1, 2), (2, 3))
DOWN = ((3, 2), (2, 1), (1, 0))


class Sequence:
    def __init__(self):
        self.last = None

    def __call__(self, stage, *values):
        if self.last is not None:
            values = lax.optimization_barrier((self.last,) + values)[1:]
        result = stage(*values)
        self.last = jax.tree.leaves(result)[0]
        return result


def grid_sums(hidden, weights, tensor_index, width, low_rank_terms):
    z = tensor_index >> 1
    low, last_z = z < LINE // 2, z == LINE - 1
    pieces = range(PIECES)
    then = Sequence()
    arrived, mine, first, second, third = {}, {}, {}, {}, {}
    add = lambda *terms: sum(t.astype(f32) for t in terms)
    narrow = lambda *terms: add(*terms).astype(bf16)
    size = hidden.shape[0] // PIECES

    def products(k, own, piece, count, further):
        kind = f32 if own else bf16
        out = then(
            lambda h, *more: product(h, weights, tensor_index, k, own, kind, width, (), piece, count, *more),
            hidden,
            *further,
        )
        for p, value in enumerate(out) if piece is None else [(piece, out[0])]:
            if own:
                mine[p, k] = value
            else:
                arrived[p, k] = across(value, 1)

    def theirs(k, *further, piece=None, count=PIECES):
        products(k, False, piece, 1 if piece is not None else count, further)

    def ours(k, piece=None, count=PIECES):
        products(k, True, piece, 1 if piece is not None else count, ())

    def sent(value, further):
        return value if further is None else jnp.concatenate([value, further.astype(bf16)], 0)

    def hop_1(p, further=None):
        value = sent(then(narrow, mine[p, 0], arrived[p, 0][:size]), further)
        first[p] = along_line(value, [UP[0], DOWN[0]])

    def hop_2(p, further=None):
        value = sent(then(narrow, mine[p, 1], arrived[p, 1], first[p][:size]), further)
        second[p] = (along_line(value, UP[:2]), along_line(value, DOWN[:2]))

    def hop_3(p, further):
        def stage(up, down, own, came_own, other, came_other):
            here, there = add(own, came_own), add(other, came_other)
            return narrow(here, up[:size]), narrow(jnp.where(last_z, here, there), down[:size])

        up, down = then(stage, *second[p], mine[p, 2], arrived[p, 2], mine[p, 0], arrived[p, 0][:size])
        third[p] = (along_line(sent(up, further), UP), along_line(sent(down, further), DOWN))

    wanted, low_rank_of = low_rank_terms(hidden)
    hidden = lax.optimization_barrier((wanted, hidden))[1]
    theirs(0, piece=0)
    low_rank, second_factors = low_rank_of()
    low_rank = low_rank.reshape(-1, width)
    theirs(0, low_rank, piece=1)
    ours(0)
    theirs(1, piece=0)
    hop_1(0)
    ours(1)
    theirs(1, piece=1)
    low_rank = add(low_rank, arrived[1, 0][size:])
    hop_1(1, low_rank)
    theirs(2, piece=0)
    ours(2)
    hop_2(0)
    theirs(2, piece=1)
    low_rank = add(low_rank, first[1][size:])
    hop_2(1, low_rank)
    theirs(3, count=1)
    ours(3, count=1)
    hop_3(0, None)
    up, down = second[1]
    low_rank = narrow(low_rank, jnp.where(low, down[size:], up[size:]))
    hop_3(1, low_rank)
    settled = then(add, *third[0])
    own_part = then(add, mine[0, 3], arrived[0, 3])
    up, down = third[1] = then(lambda *t: t, *third[1])
    low_rank = jnp.where(z == 0, down[size:], jnp.where(last_z, up[size:], low_rank))
    moved = jnp.concatenate([settled, add(up[:size], down[:size])], 0)
    base_part = own_part + moved
    return base_part, low_rank.reshape(hidden.shape[0], -1), second_factors


def shards(
    gate_preactivation,
    up_preactivation,
    base_down_matrix,
    adapter_first_factor,
    adapter_second_factor,
    residual,
    scoring_head_matrix,
    block_adapter_index,
    block_span_start,
    block_span_end,
):
    rows_local, hidden_width = gate_preactivation.shape
    slice_width = residual.shape[1]
    model_width = scoring_head_matrix.shape[0]
    blocks = rows_local // BLOCK
    adapters_here = adapter_first_factor.shape[0]
    data_index = lax.axis_index("dp")
    data_size = lax.axis_size("dp")
    tensor_index = lax.axis_index("tensor")
    on_grid = lax.axis_size("tensor") == LINE * PAIR

    ids = block_adapter_index.reshape(data_size, blocks)
    owner = lax.dynamic_index_in_dim(ids, data_index, 0, keepdims=False) // adapters_here
    first_turned = jnp.swapaxes(adapter_first_factor, 1, 2)
    steps = [step for step in range(1, data_size)] + [0]
    turned = jnp.concatenate(
        [lax.dynamic_slice_in_dim(ids, (data_index + step) % data_size, 1)[0] for step in steps]
    )
    turned = jnp.clip(turned - data_index * adapters_here, 0, adapters_here - 1)
    away = blocks * (data_size - 1)

    def low_rank_terms(rows):
        wanted_first = pick(turned[:away], first_turned)

        def terms(*earlier):
            wanted_second = pick(turned[:away], adapter_second_factor, earlier)
            first_factors = pick(turned[away:], first_turned, earlier)
            second_factors = pick(turned[away:], adapter_second_factor, earlier)
            for n, step in enumerate(steps[:-1]):
                hop = [(d, (d + step) % data_size) for d in range(data_size)]
                take = (owner == (data_index - step) % data_size)[:, None, None]

                def fetched(wanted, kept):
                    came = lax.ppermute(wanted[n * blocks : (n + 1) * blocks], "dp", hop)
                    return jnp.where(take, came, kept)

                first_factors = fetched(wanted_first, first_factors)
                second_factors = fetched(wanted_second, second_factors)
            product = jnp.einsum(
                "bcj,bej->bce",
                rows.reshape(blocks, BLOCK, hidden_width),
                first_factors,
                preferred_element_type=f32,
            ).reshape(rows_local, -1)
            return product, second_factors

        return wanted_first, terms

    def adapter_delta(low_rank, second_factors):
        return jnp.einsum(
            "bcn,bnt->bct",
            low_rank.astype(bf16).reshape(blocks, BLOCK, -1),
            second_factors,
            preferred_element_type=f32,
        ).reshape(rows_local, slice_width).astype(bf16)

    hidden = (
        jax.nn.silu(gate_preactivation.astype(f32)) * up_preactivation.astype(f32)
    ).astype(bf16)
    if on_grid:
        base_part, low_rank, second_factors = grid_sums(
            hidden, base_down_matrix, tensor_index, slice_width, low_rank_terms
        )
        delta = adapter_delta(low_rank, second_factors)
    else:
        low_rank, second_factors = low_rank_terms(hidden)[1]()
        delta = adapter_delta(lax.psum(low_rank, "tensor"), second_factors)
        base_part = lax.psum_scatter(
            jnp.dot(hidden, base_down_matrix, preferred_element_type=f32),
            "tensor",
            scatter_dimension=1,
            tiled=True,
        )
    combined = residual.astype(f32) + delta.astype(f32) + base_part
    layer_out = combined.astype(bf16)
    head = lax.dynamic_slice_in_dim(
        scoring_head_matrix, tensor_index * slice_width, slice_width
    )
    stats = jnp.stack([jnp.sum(combined * combined, 1), jnp.sum(combined * head[None, :], 1)])
    stats = stats.reshape(2 * blocks, BLOCK)
    stats = exchange_sum(stats, f32) if on_grid else lax.psum(stats, "tensor")
    square_sum, head_sum = stats[:blocks], stats[blocks:]
    scores = head_sum * lax.rsqrt(square_sum / model_width + EPSILON)
    position = jnp.arange(BLOCK, dtype=jnp.int32)
    inside = (position[None, :] >= block_span_start[:, None]) & (
        position[None, :] < block_span_end[:, None]
    )
    span_scores = jnp.sum(jnp.where(inside, scores, f32(0.0)), 1)
    return (layer_out, span_scores)


def solution(mesh):
    return jax.shard_map(
        shards,
        mesh=mesh,
        in_specs=(
            P(("groups", "dp"), "tensor"),
            P(("groups", "dp"), "tensor"),
            P("tensor", None),
            P("dp", "tensor", None),
            P("dp", None, "tensor"),
            P(("groups", "dp"), "tensor"),
            P(),
            P("groups"),
            P(("groups", "dp")),
            P(("groups", "dp")),
        ),
        out_specs=(P(("groups", "dp"), "tensor"), P(("groups", "dp"))),
        check_vma=False,
    )
```

time: 221 us -> 180 us (0.81)
  Pallas kernels: 0 us -> 72.9 us
  waiting for transfers between devices: 86.5 us -> 22.2 us
  matrix products: 55 us -> 4.59 us
  local copies, waits for them, and re-layouts: 18.6 us -> 3.99 us
  starting transfers between devices: 35.7 us -> 47.3 us
  other arithmetic: 21.6 us -> 26.5 us
  between operations: 3.45 us -> 1.07 us
    pallas_call x0 -> x15, Pallas kernels: none -> 72.9 us  [the longest x11 53.6 us: product(): pl.pallas_call(lambda *refs: product_kernel(count, more, *refs), grid_spe...]
    ppermute x10, waiting for transfers between devices: 71.1 us -> 18.6 us  [across(): return lax.ppermute(value, 'tensor', [(t, t ^ bit) for t in range(size)])]
    dot_general x10 -> x2, matrix products: 55 us -> 4.59 us  [the longest x1 2.69 us: terms(): jnp.einsum('bcj,bej->bce', rows.reshape(blocks, BLOCK, hidden_width), fir...]
    gather x4 -> x0, local copies, waits for them, and re-layouts: 17.1 us -> none  [held(): return factors[at]]
    ppermute x5 -> x10, waiting for transfers between devices: 15.4 us -> 3.69 us  [along_line(): return lax.ppermute(value, 'tensor', pairs)]
    ppermute x5 -> x10, starting transfers between devices: 22.7 us -> 30.5 us  [along_line(): return lax.ppermute(value, 'tensor', pairs)]
    add x0 -> x3, other arithmetic: none -> 5.08 us  [grid_sums(): add = lambda *terms: sum((t.astype(f32) for t in terms))]
    ppermute x10, starting transfers between devices: 13 us -> 15.9 us  [across(): return lax.ppermute(value, 'tensor', [(t, t ^ bit) for t in range(size)])]
  transfers between devices with their start and end apart: 17 -> 22, of which waited for: 9 -> 6; matrix products, arithmetic and copies ran while one was open for 35% -> 15% of each run, Pallas kernels for 0% -> 38%
where the time goes in v3:
time: 180 us; the launch traced here: 179 us
  Pallas kernels  72.9 us (41%)
  starting transfers between devices  47.3 us (26%)
  other arithmetic  26.5 us (15%)
  waiting for transfers between devices  22.2 us (12%)
  matrix products  4.59 us (3%)
  local copies, waits for them, and re-layouts  3.99 us (2%)
    pallas_call x11, Pallas kernels, product(): pl.pallas_call(lambda *refs: product_kernel(count, more, *refs), grid_spe...  53.6 us
    ppermute x10, starting transfers between devices, along_line(): return lax.ppermute(value, 'tensor', pairs)  30.5 us
    pallas_call x4, Pallas kernels, pick(): pl.pallas_call(pick_kernel, grid_spec=pltpu.PrefetchScalarGridSpec(num_sc...  19.3 us
    ppermute x10, waiting for transfers between devices, across(): return lax.ppermute(value, 'tensor', [(t, t ^ bit) for t in range(size)])  18.6 us
    ppermute x10, starting transfers between devices, across(): return lax.ppermute(value, 'tensor', [(t, t ^ bit) for t in range(size)])  15.9 us
    convert_element_type x7, other arithmetic, grid_sums(): narrow = lambda *terms: add(*terms).astype(bf16)  10.6 us
    add x3, other arithmetic, grid_sums(): add = lambda *terms: sum((t.astype(f32) for t in terms))  5.08 us
    convert_element_type x1, other arithmetic, shards(): hidden = (jax.nn.silu(gate_preactivation.astype(f32)) * up_preactivation....  4.27 us
  transfers between devices with their start and end apart: 22, of which 6 were waited for; matrix products, arithmetic and copies ran while one was open for 15% of the time, Pallas kernels for 38%

profile of v3, /device:TPU:0, one launch (start us, length us, event | category | flops | bytes accessed | tf_op | source)
XLA Modules:
  0.0 178.6 jit_solution(629451727546652060)
XLA Ops:
  0.7 0.7 reshape.63
  1.5 0.6 fusion.25
  2.1 4.7 %shard_map.113 = bf16[6,64,1792]{2,1,0:T(8,128)(2,1)} custom-call(s32[6]{0:T(128)} %get-tuple-element.106.ids_ref, bf16[32,64,1792]{2,1,0:T(8,128)(2,1)} %bitcast.20), custom_call_target="tpu_custom_call" | custom-call | tf_op jit(solution)/shard_map/pallas_call | solution.py:82
  6.9 0.9 collective-permute-start
  7.8 4.3 %fusion.4.refs_1_ = bf16[768,1792]{1,0:T(8,128)(2,1)S(1)} fusion(bf16[768,1792]{1,0:T(8,128)(2,1)} %param.11, bf16[768,1792]{1,0:T(8,128)(2,1)} %param.10), kind=kLoop, calls=%fused_computation.6 | loop fusion | flops 11010048 | bytes 8257536 | tf_op jit(solution)/shard_map/convert_element_type | solution.py:268
  12.0 4.1 %shard_map.114 = bf16[384,1024]{1,0:T(8,128)(2,1)} custom-call(s32[1]{0:T(128)} %bitcast.refs_0_, bf16[768,1792]{1,0:T(8,128)(2,1)S(1)} %fusion.4.refs_1_, bf16[1792,8192]{1,0:T(8,128)(2,1)} %refs_2_.21), custom_call_target="tpu_custom_call" | custom-call | tf_op jit(solution)/shard_map/pallas_call | solution.py:57
  16.1 2.3 %collective-permute-start.1 = (bf16[384,1024]{1,0:T(8,128)(2,1)}, bf16[384,1024]{1,0:T(8,128)(2,1)}, u32[]{:S(2)}, u32[]{:S(2)}) collective-permute-start(bf16[384,1024]{1,0:T(8,128)(2,1)} %shard_map.114), channel_id=1, source_target_pairs={{0,1},{1,0},{2,3},{3,2},{4,5},{5,4},{6,7},{7,6},{8,9},{9,8},{10,11... | collective-permute-start | bytes 2359304 | tf_op jit(solution)/shard_map/ppermute | solution.py:31
  18.5 5.2 %shard_map.115 = bf16[6,64,1792]{2,1,0:T(8,128)(2,1)} custom-call(s32[6]{0:T(128)} %get-tuple-element.105.ids_ref, bf16[32,64,1792]{2,1,0:T(8,128)(2,1)} %bitcast.21), custom_call_target="tpu_custom_call" | custom-call | tf_op jit(solution)/shard_map/pallas_call | solution.py:82
  23.6 2.7 %fusion.6 = f32[6,128,64]{2,1,0:T(8,128)S(1)} fusion(bf16[6,128,1792]{2,1,0:T(8,128)(2,1)S(1)} %bitcast.19, bf16[6,64,1792]{2,1,0:T(8,128)(2,1)} %collective-permute-done, bf16[6,64,1792]{2,1,0:T(8,128)(2,1)} %shard_map.115, pred[6]{0:T(512)(128)(4,1)S(1)} %fusion.23), kind=kOutput, calls=%fused_computation.26 | convolution fusion | flops 176848896 | bytes 5701638 | tf_op jit(solution)/shard_map/bcj,bej->bce/dot_general | solution.py:248
  26.3 0.2 reshape_reshape.6.refs_3_
  26.5 4.1 %shard_map.116 = bf16[432,1024]{1,0:T(8,128)(2,1)} custom-call(s32[1]{0:T(128)} %bitcast.refs_0_, bf16[768,1792]{1,0:T(8,128)(2,1)S(1)} %fusion.4.refs_1_, bf16[1792,8192]{1,0:T(8,128)(2,1)} %refs_2_.21, f32[48,1024]{1,0:T(8,128)S(1)} %reshape_reshape.6.refs_3_), custom_call_target="tpu_custom_call" | custom-call | tf_op jit(solution)/shard_map/pallas_call | solution.py:57
  30.6 5.8 %shard_map.117 = (f32[384,1024]{1,0:T(8,128)}, f32[384,1024]{1,0:T(8,128)}) custom-call(s32[1]{0:T(128)} %bitcast.refs_0_, bf16[768,1792]{1,0:T(8,128)(2,1)S(1)} %fusion.4.refs_1_, bf16[1792,8192]{1,0:T(8,128)(2,1)} %refs_2_.21), custom_call_target="tpu_custom_call" | custom-call | tf_op jit(solution)/shard_map/pallas_call | solution.py:57
  36.3 4.2 %shard_map.118 = bf16[384,1024]{1,0:T(8,128)(2,1)} custom-call(s32[1]{0:T(128)} %bitcast.refs_0_, bf16[768,1792]{1,0:T(8,128)(2,1)S(1)} %fusion.4.refs_1_, bf16[1792,8192]{1,0:T(8,128)(2,1)} %refs_2_.21), custom_call_target="tpu_custom_call" | custom-call | tf_op jit(solution)/shard_map/pallas_call | solution.py:57
  40.6 2.0 %collective-permute-start.3 = (bf16[384,1024]{1,0:T(8,128)(2,1)}, bf16[384,1024]{1,0:T(8,128)(2,1)S(1)}, u32[]{:S(2)}, u32[]{:S(2)}) collective-permute-start(bf16[384,1024]{1,0:T(8,128)(2,1)} %shard_map.118), channel_id=1, source_target_pairs={{0,1},{1,0},{2,3},{3,2},{4,5},{5,4},{6,7},{7,6},{8,9},{9,8},{10,11... | collective-permute-start | bytes 2359304 | tf_op jit(solution)/shard_map/ppermute | solution.py:31
  42.6 1.4 add_convert_fusion.7
  44.0 3.5 %collective-permute-start.4 = (bf16[384,1024]{1,0:T(8,128)(2,1)S(1)}, bf16[384,1024]{1,0:T(8,128)(2,1)S(1)}, u32[]{:S(2)}, u32[]{:S(2)}) collective-permute-start(bf16[384,1024]{1,0:T(8,128)(2,1)S(1)} %add_convert_fusion.7), channel_id=1, source_target_pairs={{0,2},{1,3},{6,4},{7,5},{8,10},{9,11},{14,12},{15,13},{16,18},{17,... | collective-permute-start | bytes 2359304 | tf_op jit(solution)/shard_map/ppermute | solution.py:26
  47.5 5.8 %shard_map.119 = (f32[384,1024]{1,0:T(8,128)}, f32[384,1024]{1,0:T(8,128)}) custom-call(s32[1]{0:T(128)} %bitcast.refs_0_, bf16[768,1792]{1,0:T(8,128)(2,1)S(1)} %fusion.4.refs_1_, bf16[1792,8192]{1,0:T(8,128)(2,1)} %refs_2_.21), custom_call_target="tpu_custom_call" | custom-call | tf_op jit(solution)/shard_map/pallas_call | solution.py:57
  53.3 4.1 %shard_map.120 = bf16[384,1024]{1,0:T(8,128)(2,1)} custom-call(s32[1]{0:T(128)} %bitcast.refs_0_, bf16[768,1792]{1,0:T(8,128)(2,1)S(1)} %fusion.4.refs_1_, bf16[1792,8192]{1,0:T(8,128)(2,1)} %refs_2_.21), custom_call_target="tpu_custom_call" | custom-call | tf_op jit(solution)/shard_map/pallas_call | solution.py:57
  57.5 1.9 %copy-done.3 = f32[384,1024]{1,0:T(8,128)S(1)} copy-done((f32[384,1024]{1,0:T(8,128)S(1)}, f32[384,1024]{1,0:T(8,128)}, u32[]{:S(2)}) %copy-start.3) | copy-done | bytes 1572888
  59.4 0.3 add_convert_fusion.6
  59.8 1.5 collective-permute-start.6
  61.3 1.6 collective-permute-start.5
  62.9 4.0 %shard_map.121 = bf16[384,1024]{1,0:T(8,128)(2,1)} custom-call(s32[1]{0:T(128)} %bitcast.refs_0_, bf16[768,1792]{1,0:T(8,128)(2,1)S(1)} %fusion.4.refs_1_, bf16[1792,8192]{1,0:T(8,128)(2,1)} %refs_2_.21), custom_call_target="tpu_custom_call" | custom-call | tf_op jit(solution)/shard_map/pallas_call | solution.py:57
  66.9 5.9 %shard_map.122 = (f32[384,1024]{1,0:T(8,128)}, f32[384,1024]{1,0:T(8,128)}) custom-call(s32[1]{0:T(128)} %bitcast.refs_0_, bf16[768,1792]{1,0:T(8,128)(2,1)S(1)} %fusion.4.refs_1_, bf16[1792,8192]{1,0:T(8,128)(2,1)} %refs_2_.21), custom_call_target="tpu_custom_call" | custom-call | tf_op jit(solution)/shard_map/pallas_call | solution.py:57
  72.8 1.3 add_convert_fusion.5
  74.1 4.9 %collective-permute-start.7 = (bf16[384,1024]{1,0:T(8,128)(2,1)}, bf16[384,1024]{1,0:T(8,128)(2,1)}, u32[]{:S(2)}, u32[]{:S(2)}) collective-permute-start(bf16[384,1024]{1,0:T(8,128)(2,1)} %add_convert_fusion.5), channel_id=1, source_target_pairs={{0,2},{1,3},{2,4},{3,5},{8,10},{9,11},{10,12},{11,13},{16,18},{17,... | collective-permute-start | bytes 2359304 | tf_op jit(solution)/shard_map/ppermute | solution.py:26
  79.0 1.5 collective-permute-start.8
  80.6 1.5 collective-permute-start.9
  82.1 4.1 %shard_map.123 = bf16[384,1024]{1,0:T(8,128)(2,1)} custom-call(s32[1]{0:T(128)} %bitcast.refs_0_, bf16[768,1792]{1,0:T(8,128)(2,1)S(1)} %fusion.4.refs_1_, bf16[1792,8192]{1,0:T(8,128)(2,1)} %refs_2_.21), custom_call_target="tpu_custom_call" | custom-call | tf_op jit(solution)/shard_map/pallas_call | solution.py:57
  86.3 3.4 %collective-permute-done.5 = bf16[384,1024]{1,0:T(8,128)(2,1)S(1)} collective-permute-done((bf16[384,1024]{1,0:T(8,128)(2,1)S(1)}, bf16[384,1024]{1,0:T(8,128)(2,1)S(1)}, u32[]{:S(2)}, u32[]{:S(2)}) %collective-permute-start.5) | collective-permute-done | bytes 786464 | tf_op jit(solution)/shard_map/ppermute | solution.py:31
  89.6 0.4 add_convert_fusion.4
  90.1 1.0 pad_maximum_fusion.3
  91.1 5.0 %collective-permute-start.10 = (bf16[432,1024]{1,0:T(8,128)(2,1)}, bf16[432,1024]{1,0:T(8,128)(2,1)}, u32[]{:S(2)}, u32[]{:S(2)}) collective-permute-start(bf16[432,1024]{1,0:T(8,128)(2,1)} %pad_maximum_fusion.3), channel_id=1, source_target_pairs={{0,2},{1,3},{2,4},{3,5},{8,10},{9,11},{10,12},{11,13},{16,18},{17,... | collective-permute-start | bytes 2654216 | tf_op jit(solution)/shard_map/ppermute | solution.py:26
  96.1 1.6 collective-permute-start.11
  97.7 3.7 %collective-permute-done.7 = bf16[384,1024]{1,0:T(8,128)(2,1)} collective-permute-done((bf16[384,1024]{1,0:T(8,128)(2,1)}, bf16[384,1024]{1,0:T(8,128)(2,1)}, u32[]{:S(2)}, u32[]{:S(2)}) %collective-permute-start.7) | collective-permute-done | bytes 786464 | tf_op jit(solution)/shard_map/ppermute | solution.py:26
  101.4 5.6 %shard_map.124 = bf16[768,1024]{1,0:T(8,128)(2,1)} custom-call(s32[1]{0:T(128)} %bitcast.refs_0_, bf16[768,1792]{1,0:T(8,128)(2,1)S(1)} %fusion.4.refs_1_, bf16[1792,8192]{1,0:T(8,128)(2,1)} %refs_2_.21), custom_call_target="tpu_custom_call" | custom-call | tf_op jit(solution)/shard_map/pallas_call | solution.py:57
  106.9 6.0 %shard_map.125 = f32[768,1024]{1,0:T(8,128)} custom-call(s32[1]{0:T(128)} %bitcast.refs_0_, bf16[768,1792]{1,0:T(8,128)(2,1)S(1)} %fusion.4.refs_1_, bf16[1792,8192]{1,0:T(8,128)(2,1)} %refs_2_.21), custom_call_target="tpu_custom_call" | custom-call | tf_op jit(solution)/shard_map/pallas_call | solution.py:57
  113.0 2.0 %collective-permute-start.15 = (bf16[768,1024]{1,0:T(8,128)(2,1)}, bf16[768,1024]{1,0:T(8,128)(2,1)}, u32[]{:S(2)}, u32[]{:S(2)}) collective-permute-start(bf16[768,1024]{1,0:T(8,128)(2,1)} %shard_map.124), channel_id=1, source_target_pairs={{0,1},{1,0},{2,3},{3,2},{4,5},{5,4},{6,7},{7,6},{8,9},{9,8},{10,11... | collective-permute-start | bytes 4718600 | tf_op jit(solution)/shard_map/ppermute | solution.py:31
  115.0 3.7 %add_convert_fusion.1 = (bf16[384,1024]{1,0:T(8,128)(2,1)S(1)}, bf16[384,1024]{1,0:T(8,128)(2,1)}) fusion(bf16[384,1024]{1,0:T(8,128)(2,1)} %collective-permute-done.8, f32[384,1024]{1,0:T(8,128)S(1)} %copy-done.6, bf16[384,1024]{1,0:T(8,128)(2,1)} %collective-permute-done.1, f32[384,1024]{1,0:T(8,128)S(1)} %copy-done.13, ...), kind=kLoop, calls=%fused_computation.17 | loop fusion | flops 4325376 | bytes 7864321 | tf_op jit(solution)/shard_map/convert_element_type | solution.py:124
  118.8 4.4 %collective-permute-start.13 = (bf16[384,1024]{1,0:T(8,128)(2,1)}, bf16[384,1024]{1,0:T(8,128)(2,1)S(1)}, u32[]{:S(2)}, u32[]{:S(2)}) collective-permute-start(bf16[384,1024]{1,0:T(8,128)(2,1)} %get-tuple-element.100), channel_id=1, source_target_pairs={{0,2},{1,3},{2,4},{3,5},{4,6},{5,7},{8,10},{9,11},{10,12},{11,13},... | collective-permute-start | bytes 2359304 | tf_op jit(solution)/shard_map/ppermute | solution.py:26
  123.2 1.3 collective-permute-start.14
  124.5 1.1 add_convert_fusion.8
  125.7 2.5 %add_convert_fusion = (bf16[384,1024]{1,0:T(8,128)(2,1)S(1)}, bf16[384,1024]{1,0:T(8,128)(2,1)S(1)}) fusion(f32[384,1024]{1,0:T(8,128)S(1)} %copy-done.4, bf16[384,1024]{1,0:T(8,128)(2,1)S(1)} %copy-done.2, f32[384,1024]{1,0:T(8,128)S(1)} %copy-done.12, bf16[384,1024]{1,0:T(8,128)(2,1)} %collective-permute-done.12, ...), kind=kLoop, calls=%fused_computation.15 | loop fusion | flops 4325376 | bytes 7864321 | tf_op jit(solution)/shard_map/convert_element_type | solution.py:124
  128.1 1.4 pad_maximum_fusion
  129.6 5.5 %collective-permute-start.16 = (bf16[432,1024]{1,0:T(8,128)(2,1)}, bf16[432,1024]{1,0:T(8,128)(2,1)}, u32[]{:S(2)}, u32[]{:S(2)}) collective-permute-start(bf16[432,1024]{1,0:T(8,128)(2,1)} %get-tuple-element.102), channel_id=1, source_target_pairs={{0,2},{1,3},{2,4},{3,5},{4,6},{5,7},{8,10},{9,11},{10,12},{11,13},... | collective-permute-start | bytes 2654216 | tf_op jit(solution)/shard_map/ppermute | solution.py:26
  135.0 1.3 collective-permute-start.17
  136.3 4.5 %shard_map.126 = bf16[6,64,1024]{2,1,0:T(8,128)(2,1)} custom-call(s32[6]{0:T(128)} %get-tuple-element.106.ids_ref, bf16[32,64,1024]{2,1,0:T(8,128)(2,1)} %refs_0_.3), custom_call_target="tpu_custom_call" | custom-call | tf_op jit(solution)/shard_map/pallas_call | solution.py:82
  140.8 4.9 %shard_map.127 = bf16[6,64,1024]{2,1,0:T(8,128)(2,1)} custom-call(s32[6]{0:T(128)} %get-tuple-element.105.ids_ref, bf16[32,64,1024]{2,1,0:T(8,128)(2,1)} %refs_0_.3), custom_call_target="tpu_custom_call" | custom-call | tf_op jit(solution)/shard_map/pallas_call | solution.py:82
  145.7 1.4 convert_add_fusion.3
  147.2 9.6 %collective-permute-done.15 = bf16[768,1024]{1,0:T(8,128)(2,1)} collective-permute-done((bf16[768,1024]{1,0:T(8,128)(2,1)}, bf16[768,1024]{1,0:T(8,128)(2,1)}, u32[]{:S(2)}, u32[]{:S(2)}) %collective-permute-start.15) | collective-permute-done | bytes 1572896 | tf_op jit(solution)/shard_map/ppermute | solution.py:31
  156.8 1.9 %convert_add_fusion.1 = f32[768,1024]{1,0:T(8,128)S(1)} fusion(f32[768,1024]{1,0:T(8,128)S(1)} %copy-done, bf16[768,1024]{1,0:T(8,128)(2,1)} %collective-permute-done.15), kind=kLoop, calls=%fused_computation.12 | loop fusion | flops 1572864 | bytes 7864320 | tf_op jit(solution)/shard_map/add | solution.py:123
  158.8 1.0 select_select_fusion
  159.7 0.2 reshape_reshape.7
  159.9 1.7 convert_add_fusion.2
  161.7 1.9 %convolution_convert_fusion = bf16[6,128,1024]{2,1,0:T(8,128)(2,1)S(1)} fusion(bf16[6,128,64]{2,1,0:T(8,128)(2,1)S(1)} %reshape_reshape.7, bf16[6,64,1024]{2,1,0:T(8,128)(2,1)} %collective-permute-done.18, bf16[6,64,1024]{2,1,0:T(8,128)(2,1)S(1)} %copy-done.8, pred[6]{0:T(512)(128)(4,1)S(1)} %fusion.23), kind=kOutput, calls=%fused_computation.13 | convolution fusion | flops 101842944 | bytes 3244038 | tf_op jit(solution)/shard_map/bcn,bnt->bct/dot_general | solution.py:259
  163.6 0.1 copy-done.11
  163.8 2.1 %multiply_reduce_fusion.1 = (f32[768]{0:T(1024)S(1)}, f32[768]{0:T(1024)S(1)}, bf16[768,1024]{1,0:T(8,128)(2,1)}) fusion(f32[1024]{0:T(1024)S(1)} %dynamic-slice-done, f32[768,1024]{1,0:T(8,128)S(1)} %convert_add_fusion.1, f32[384,1024]{1,0:T(8,128)S(1)} %convert_add_fusion.2, f32[384,1024]{1,0:T(8,128)S(1)} %copy-done.7, ...), kind=kLoop, calls=%fused_computation.11 | loop fusion | flops 8649216 | bytes 11020288 | tf_op jit(solution)/shard_map/reduce_sum | solution.py:288
  165.9 1.8 %collective-permute-start.19 = (f32[12,128]{1,0:T(8,128)S(1)}, f32[12,128]{1,0:T(8,128)S(1)}, u32[]{:S(2)}, u32[]{:S(2)}) collective-permute-start(f32[12,128]{1,0:T(8,128)S(1)} %reshape.65), channel_id=1, source_target_pairs={{0,1},{1,0},{2,3},{3,2},{4,5},{5,4},{6,7},{7,6},{8,9},{9,8},{10,11... | collective-permute-start | bytes 18440 | tf_op jit(solution)/shard_map/ppermute | solution.py:31
  167.7 1.9 %collective-permute-done.19 = f32[12,128]{1,0:T(8,128)S(1)} collective-permute-done((f32[12,128]{1,0:T(8,128)S(1)}, f32[12,128]{1,0:T(8,128)S(1)}, u32[]{:S(2)}, u32[]{:S(2)}) %collective-permute-start.19) | collective-permute-done | bytes 6176 | tf_op jit(solution)/shard_map/ppermute | solution.py:31
  169.7 1.8 %collective-permute-start.20 = (f32[12,128]{1,0:T(8,128)S(1)}, f32[12,128]{1,0:T(8,128)S(1)}, u32[]{:S(2)}, u32[]{:S(2)}) collective-permute-start(f32[12,128]{1,0:T(8,128)S(1)} %add.152), channel_id=1, source_target_pairs={{0,2},{1,3},{2,0},{3,1},{4,6},{5,7},{6,4},{7,5},{8,10},{9,11},{10,... | collective-permute-start | bytes 18440 | tf_op jit(solution)/shard_map/ppermute | solution.py:31
  171.5 1.9 %collective-permute-done.20 = f32[12,128]{1,0:T(8,128)S(1)} collective-permute-done((f32[12,128]{1,0:T(8,128)S(1)}, f32[12,128]{1,0:T(8,128)S(1)}, u32[]{:S(2)}, u32[]{:S(2)}) %collective-permute-start.20) | collective-permute-done | bytes 6176 | tf_op jit(solution)/shard_map/ppermute | solution.py:31
  173.3 2.8 %collective-permute-start.21 = (f32[12,128]{1,0:T(8,128)S(1)}, f32[12,128]{1,0:T(8,128)S(1)}, u32[]{:S(2)}, u32[]{:S(2)}) collective-permute-start(f32[12,128]{1,0:T(8,128)S(1)} %add.153), channel_id=1, source_target_pairs={{0,4},{1,5},{2,6},{3,7},{4,0},{5,1},{6,2},{7,3},{8,12},{9,13},{10,... | collective-permute-start | bytes 18440 | tf_op jit(solution)/shard_map/ppermute | solution.py:31
  176.1 1.7 collective-permute-done.21
  177.9 0.7 fusion.17
  (72 shorter events, 0.5 us)
Async XLA Ops:
  6.9 16.8 %collective-permute-start = (bf16[6,64,1792]{2,1,0:T(8,128)(2,1)}, bf16[6,64,1792]{2,1,0:T(8,128)(2,1)}, u32[]{:S(2)}, u32[]{:S(2)}) collective-permute-start(bf16[6,64,1792]{2,1,0:T(8,128)(2,1)} %shard_map.113), channel_id=1, source_target_pairs={{0,8},{8,0},{1,9},{9,1},{2,10},{10,2},{3,11},{11,3},{4,12},{12,4},... | collective-permute-start | bytes 4128776 | tf_op jit(solution)/shard_map/ppermute | solution.py:243
  16.1 26.5 %collective-permute-start.1 = (bf16[384,1024]{1,0:T(8,128)(2,1)}, bf16[384,1024]{1,0:T(8,128)(2,1)}, u32[]{:S(2)}, u32[]{:S(2)}) collective-permute-start(bf16[384,1024]{1,0:T(8,128)(2,1)} %shard_map.114), channel_id=1, source_target_pairs={{0,1},{1,0},{2,3},{3,2},{4,5},{5,4},{6,7},{7,6},{8,9},{9,8},{10,11... | collective-permute-start | bytes 2359304 | tf_op jit(solution)/shard_map/ppermute | solution.py:31
  30.6 26.8 %collective-permute-start.2 = (bf16[432,1024]{1,0:T(8,128)(2,1)}, bf16[432,1024]{1,0:T(8,128)(2,1)S(1)}, u32[]{:S(2)}, u32[]{:S(2)}) collective-permute-start(bf16[432,1024]{1,0:T(8,128)(2,1)} %shard_map.116), channel_id=1, source_target_pairs={{0,1},{1,0},{2,3},{3,2},{4,5},{5,4},{6,7},{7,6},{8,9},{9,8},{10,11... | collective-permute-start | bytes 2654216 | tf_op jit(solution)/shard_map/ppermute | solution.py:31
  36.3 6.2 %copy-start.5 = (f32[384,1024]{1,0:T(8,128)S(1)}, f32[384,1024]{1,0:T(8,128)}, u32[]{:S(2)}) copy-start(f32[384,1024]{1,0:T(8,128)} %get-tuple-element.82) | copy-start | bytes 4718596
  40.6 32.2 %collective-permute-start.3 = (bf16[384,1024]{1,0:T(8,128)(2,1)}, bf16[384,1024]{1,0:T(8,128)(2,1)S(1)}, u32[]{:S(2)}, u32[]{:S(2)}) collective-permute-start(bf16[384,1024]{1,0:T(8,128)(2,1)} %shard_map.118), channel_id=1, source_target_pairs={{0,1},{1,0},{2,3},{3,2},{4,5},{5,4},{6,7},{7,6},{8,9},{9,8},{10,11... | collective-permute-start | bytes 2359304 | tf_op jit(solution)/shard_map/ppermute | solution.py:31
  44.0 28.8 %collective-permute-start.4 = (bf16[384,1024]{1,0:T(8,128)(2,1)S(1)}, bf16[384,1024]{1,0:T(8,128)(2,1)S(1)}, u32[]{:S(2)}, u32[]{:S(2)}) collective-permute-start(bf16[384,1024]{1,0:T(8,128)(2,1)S(1)} %add_convert_fusion.7), channel_id=1, source_target_pairs={{0,2},{1,3},{6,4},{7,5},{8,10},{9,11},{14,12},{15,13},{16,18},{17,... | collective-permute-start | bytes 2359304 | tf_op jit(solution)/shard_map/ppermute | solution.py:26
  57.4 2.0 %copy-start.3 = (f32[384,1024]{1,0:T(8,128)S(1)}, f32[384,1024]{1,0:T(8,128)}, u32[]{:S(2)}) copy-start(f32[384,1024]{1,0:T(8,128)} %get-tuple-element.89) | copy-start | bytes 4718596
  57.4 32.7 %copy-start.14 = (bf16[432,1024]{1,0:T(8,128)(2,1)}, bf16[432,1024]{1,0:T(8,128)(2,1)S(1)}, u32[]{:S(2)}) copy-start(bf16[432,1024]{1,0:T(8,128)(2,1)S(1)} %collective-permute-done.2) | copy-start | bytes 2654212
  57.5 2.2 %copy-start.1 = (bf16[384,1024]{1,0:T(8,128)(2,1)}, bf16[384,1024]{1,0:T(8,128)(2,1)S(1)}, u32[]{:S(2)}) copy-start(bf16[384,1024]{1,0:T(8,128)(2,1)S(1)} %slice.67) | copy-start | bytes 2359300
  59.7 1.6 copy-start.16
  59.8 26.4 %collective-permute-start.6 = (bf16[432,1024]{1,0:T(8,128)(2,1)S(1)}, bf16[432,1024]{1,0:T(8,128)(2,1)S(1)}, u32[]{:S(2)}, u32[]{:S(2)}) collective-permute-start(bf16[432,1024]{1,0:T(8,128)(2,1)S(1)} %pad_maximum_fusion.2), channel_id=1, source_target_pairs={{0,2},{1,3},{6,4},{7,5},{8,10},{9,11},{14,12},{15,13},{16,18},{17,... | collective-permute-start | bytes 2654216 | tf_op jit(solution)/shard_map/ppermute | solution.py:26
  61.3 28.4 %collective-permute-start.5 = (bf16[384,1024]{1,0:T(8,128)(2,1)S(1)}, bf16[384,1024]{1,0:T(8,128)(2,1)S(1)}, u32[]{:S(2)}, u32[]{:S(2)}) collective-permute-start(bf16[384,1024]{1,0:T(8,128)(2,1)S(1)} %copy-done.16), channel_id=1, source_target_pairs={{0,1},{1,0},{2,3},{3,2},{4,5},{5,4},{6,7},{7,6},{8,9},{9,8},{10,11... | collective-permute-start | bytes 2359304 | tf_op jit(solution)/shard_map/ppermute | solution.py:31
  66.9 5.9 %copy-start.10 = (f32[384,1024]{1,0:T(8,128)S(1)}, f32[384,1024]{1,0:T(8,128)}, u32[]{:S(2)}) copy-start(f32[384,1024]{1,0:T(8,128)} %get-tuple-element.65) | copy-start | bytes 4718596
  74.1 27.3 %collective-permute-start.7 = (bf16[384,1024]{1,0:T(8,128)(2,1)}, bf16[384,1024]{1,0:T(8,128)(2,1)}, u32[]{:S(2)}, u32[]{:S(2)}) collective-permute-start(bf16[384,1024]{1,0:T(8,128)(2,1)} %add_convert_fusion.5), channel_id=1, source_target_pairs={{0,2},{1,3},{2,4},{3,5},{8,10},{9,11},{10,12},{11,13},{16,18},{17,... | collective-permute-start | bytes 2359304 | tf_op jit(solution)/shard_map/ppermute | solution.py:26
  79.0 33.9 %collective-permute-start.8 = (bf16[384,1024]{1,0:T(8,128)(2,1)}, bf16[384,1024]{1,0:T(8,128)(2,1)}, u32[]{:S(2)}, u32[]{:S(2)}) collective-permute-start(bf16[384,1024]{1,0:T(8,128)(2,1)} %add_convert_fusion.5), channel_id=1, source_target_pairs={{6,4},{7,5},{4,2},{5,3},{14,12},{15,13},{12,10},{13,11},{22,20},{2... | collective-permute-start | bytes 2359304 | tf_op jit(solution)/shard_map/ppermute | solution.py:26
  80.6 34.4 %collective-permute-start.9 = (bf16[384,1024]{1,0:T(8,128)(2,1)}, bf16[384,1024]{1,0:T(8,128)(2,1)}, u32[]{:S(2)}, u32[]{:S(2)}) collective-permute-start(bf16[384,1024]{1,0:T(8,128)(2,1)} %shard_map.121), channel_id=1, source_target_pairs={{0,1},{1,0},{2,3},{3,2},{4,5},{5,4},{6,7},{7,6},{8,9},{9,8},{10,11... | collective-permute-start | bytes 2359304 | tf_op jit(solution)/shard_map/ppermute | solution.py:31
  86.2 3.5 %copy-start.9 = (f32[384,1024]{1,0:T(8,128)S(1)}, f32[384,1024]{1,0:T(8,128)}, u32[]{:S(2)}) copy-start(f32[384,1024]{1,0:T(8,128)} %get-tuple-element.70) | copy-start | bytes 4718596
  86.2 3.9 %copy-start.15 = (bf16[432,1024]{1,0:T(8,128)(2,1)}, bf16[432,1024]{1,0:T(8,128)(2,1)S(1)}, u32[]{:S(2)}) copy-start(bf16[432,1024]{1,0:T(8,128)(2,1)S(1)} %collective-permute-done.6) | copy-start | bytes 2654212
  91.1 32.1 %collective-permute-start.10 = (bf16[432,1024]{1,0:T(8,128)(2,1)}, bf16[432,1024]{1,0:T(8,128)(2,1)}, u32[]{:S(2)}, u32[]{:S(2)}) collective-permute-start(bf16[432,1024]{1,0:T(8,128)(2,1)} %pad_maximum_fusion.3), channel_id=1, source_target_pairs={{0,2},{1,3},{2,4},{3,5},{8,10},{9,11},{10,12},{11,13},{16,18},{17,... | collective-permute-start | bytes 2654216 | tf_op jit(solution)/shard_map/ppermute | solution.py:26
  96.1 28.4 %collective-permute-start.11 = (bf16[432,1024]{1,0:T(8,128)(2,1)}, bf16[432,1024]{1,0:T(8,128)(2,1)}, u32[]{:S(2)}, u32[]{:S(2)}) collective-permute-start(bf16[432,1024]{1,0:T(8,128)(2,1)} %pad_maximum_fusion.3), channel_id=1, source_target_pairs={{6,4},{7,5},{4,2},{5,3},{14,12},{15,13},{12,10},{13,11},{22,20},{2... | collective-permute-start | bytes 2654216 | tf_op jit(solution)/shard_map/ppermute | solution.py:26
  101.4 24.3 %collective-permute-start.12 = (bf16[384,1024]{1,0:T(8,128)(2,1)}, bf16[384,1024]{1,0:T(8,128)(2,1)}, u32[]{:S(2)}, u32[]{:S(2)}) collective-permute-start(bf16[384,1024]{1,0:T(8,128)(2,1)} %shard_map.123), channel_id=1, source_target_pairs={{0,1},{1,0},{2,3},{3,2},{4,5},{5,4},{6,7},{7,6},{8,9},{9,8},{10,11... | collective-permute-start | bytes 2359304 | tf_op jit(solution)/shard_map/ppermute | solution.py:31
  106.9 8.1 %copy-start.6 = (f32[384,1024]{1,0:T(8,128)S(1)}, f32[384,1024]{1,0:T(8,128)}, u32[]{:S(2)}) copy-start(f32[384,1024]{1,0:T(8,128)} %get-tuple-element.82) | copy-start | bytes 4718596
  106.9 8.1 %copy-start.13 = (f32[384,1024]{1,0:T(8,128)S(1)}, f32[384,1024]{1,0:T(8,128)}, u32[]{:S(2)}) copy-start(f32[384,1024]{1,0:T(8,128)} %get-tuple-element.75) | copy-start | bytes 4718596
  113.0 12.7 %copy-start.2 = (bf16[384,1024]{1,0:T(8,128)(2,1)S(1)}, bf16[384,1024]{1,0:T(8,128)(2,1)}, u32[]{:S(2)}) copy-start(bf16[384,1024]{1,0:T(8,128)(2,1)} %copy-done.1) | copy-start | bytes 2359300
  113.0 43.8 %collective-permute-start.15 = (bf16[768,1024]{1,0:T(8,128)(2,1)}, bf16[768,1024]{1,0:T(8,128)(2,1)}, u32[]{:S(2)}, u32[]{:S(2)}) collective-permute-start(bf16[768,1024]{1,0:T(8,128)(2,1)} %shard_map.124), channel_id=1, source_target_pairs={{0,1},{1,0},{2,3},{3,2},{4,5},{5,4},{6,7},{7,6},{8,9},{9,8},{10,11... | collective-permute-start | bytes 4718600 | tf_op jit(solution)/shard_map/ppermute | solution.py:31
  115.0 10.6 %copy-start.4 = (f32[384,1024]{1,0:T(8,128)S(1)}, f32[384,1024]{1,0:T(8,128)}, u32[]{:S(2)}) copy-start(f32[384,1024]{1,0:T(8,128)} %get-tuple-element.89) | copy-start | bytes 4718596
  115.0 10.6 %copy-start.12 = (f32[384,1024]{1,0:T(8,128)S(1)}, f32[384,1024]{1,0:T(8,128)}, u32[]{:S(2)}) copy-start(f32[384,1024]{1,0:T(8,128)} %get-tuple-element.79) | copy-start | bytes 4718596
  118.8 26.9 %collective-permute-start.13 = (bf16[384,1024]{1,0:T(8,128)(2,1)}, bf16[384,1024]{1,0:T(8,128)(2,1)S(1)}, u32[]{:S(2)}, u32[]{:S(2)}) collective-permute-start(bf16[384,1024]{1,0:T(8,128)(2,1)} %get-tuple-element.100), channel_id=1, source_target_pairs={{0,2},{1,3},{2,4},{3,5},{4,6},{5,7},{8,10},{9,11},{10,12},{11,13},... | collective-permute-start | bytes 2359304 | tf_op jit(solution)/shard_map/ppermute | solution.py:26
  123.2 22.5 %collective-permute-start.14 = (bf16[384,1024]{1,0:T(8,128)(2,1)S(1)}, bf16[384,1024]{1,0:T(8,128)(2,1)S(1)}, u32[]{:S(2)}, u32[]{:S(2)}) collective-permute-start(bf16[384,1024]{1,0:T(8,128)(2,1)S(1)} %get-tuple-element.99), channel_id=1, source_target_pairs={{6,4},{7,5},{4,2},{5,3},{2,0},{3,1},{14,12},{15,13},{12,10},{13,11... | collective-permute-start | bytes 2359304 | tf_op jit(solution)/shard_map/ppermute | solution.py:26
  129.6 29.2 %collective-permute-start.16 = (bf16[432,1024]{1,0:T(8,128)(2,1)}, bf16[432,1024]{1,0:T(8,128)(2,1)}, u32[]{:S(2)}, u32[]{:S(2)}) collective-permute-start(bf16[432,1024]{1,0:T(8,128)(2,1)} %get-tuple-element.102), channel_id=1, source_target_pairs={{0,2},{1,3},{2,4},{3,5},{4,6},{5,7},{8,10},{9,11},{10,12},{11,13},... | collective-permute-start | bytes 2654216 | tf_op jit(solution)/shard_map/ppermute | solution.py:26
  135.0 23.7 %collective-permute-start.17 = (bf16[432,1024]{1,0:T(8,128)(2,1)}, bf16[432,1024]{1,0:T(8,128)(2,1)}, u32[]{:S(2)}, u32[]{:S(2)}) collective-permute-start(bf16[432,1024]{1,0:T(8,128)(2,1)} %get-tuple-element.101), channel_id=1, source_target_pairs={{6,4},{7,5},{4,2},{5,3},{2,0},{3,1},{14,12},{15,13},{12,10},{13,11... | collective-permute-start | bytes 2654216 | tf_op jit(solution)/shard_map/ppermute | solution.py:26
  145.7 11.1 %copy-start = (f32[768,1024]{1,0:T(8,128)S(1)}, f32[768,1024]{1,0:T(8,128)}, u32[]{:S(2)}) copy-start(f32[768,1024]{1,0:T(8,128)} %shard_map.125) | copy-start | bytes 9437188
  145.7 16.0 %collective-permute-start.18 = (bf16[6,64,1024]{2,1,0:T(8,128)(2,1)}, bf16[6,64,1024]{2,1,0:T(8,128)(2,1)}, u32[]{:S(2)}, u32[]{:S(2)}) collective-permute-start(bf16[6,64,1024]{2,1,0:T(8,128)(2,1)} %shard_map.126), channel_id=1, source_target_pairs={{0,8},{8,0},{1,9},{9,1},{2,10},{10,2},{3,11},{11,3},{4,12},{12,4},... | collective-permute-start | bytes 2359304 | tf_op jit(solution)/shard_map/ppermute | solution.py:243
  159.9 1.8 %copy-start.8 = (bf16[6,64,1024]{2,1,0:T(8,128)(2,1)S(1)}, bf16[6,64,1024]{2,1,0:T(8,128)(2,1)}, u32[]{:S(2)}) copy-start(bf16[6,64,1024]{2,1,0:T(8,128)(2,1)} %shard_map.127) | copy-start | bytes 2359300
  161.6 2.0 %copy-start.7 = (f32[384,1024]{1,0:T(8,128)S(1)}, f32[384,1024]{1,0:T(8,128)}, u32[]{:S(2)}) copy-start(f32[384,1024]{1,0:T(8,128)} %convert_add_fusion.3) | copy-start | bytes 4718596
  161.6 2.1 %copy-start.11 = (bf16[768,1024]{1,0:T(8,128)(2,1)S(1)}, bf16[768,1024]{1,0:T(8,128)(2,1)}, u32[]{:S(2)}) copy-start(bf16[768,1024]{1,0:T(8,128)(2,1)} %param.15) | copy-start | bytes 4718596
  161.7 2.1 %dynamic-slice-start = ((f32[8192]{0:T(1024)}, s32[]{:T(128)}), f32[1024]{0:T(1024)S(1)}, s32[]{:S(2)}) async-start(f32[8192]{0:T(1024)} %param.16, s32[]{:T(128)} %select_n.99), calls=%async_computation | async-start | bytes 8704 | tf_op jit(solution)/shard_map/dynamic_slice | solution.py:285
  163.8 14.1 %copy-start.17 = (s32[6]{0:T(128)S(1)}, s32[6]{0:T(128)}, u32[]{:S(2)}) copy-start(s32[6]{0:T(128)} %param.19) | copy-start | bytes 76
  163.8 14.1 %copy-start.18 = (s32[6]{0:T(128)S(1)}, s32[6]{0:T(128)}, u32[]{:S(2)}) copy-start(s32[6]{0:T(128)} %param.18) | copy-start | bytes 76
  165.9 3.7 %collective-permute-start.19 = (f32[12,128]{1,0:T(8,128)S(1)}, f32[12,128]{1,0:T(8,128)S(1)}, u32[]{:S(2)}, u32[]{:S(2)}) collective-permute-start(f32[12,128]{1,0:T(8,128)S(1)} %reshape.65), channel_id=1, source_target_pairs={{0,1},{1,0},{2,3},{3,2},{4,5},{5,4},{6,7},{7,6},{8,9},{9,8},{10,11... | collective-permute-start | bytes 18440 | tf_op jit(solution)/shard_map/ppermute | solution.py:31
  169.7 3.7 %collective-permute-start.20 = (f32[12,128]{1,0:T(8,128)S(1)}, f32[12,128]{1,0:T(8,128)S(1)}, u32[]{:S(2)}, u32[]{:S(2)}) collective-permute-start(f32[12,128]{1,0:T(8,128)S(1)} %add.152), channel_id=1, source_target_pairs={{0,2},{1,3},{2,0},{3,1},{4,6},{5,7},{6,4},{7,5},{8,10},{9,11},{10,... | collective-permute-start | bytes 18440 | tf_op jit(solution)/shard_map/ppermute | solution.py:31
  173.3 4.5 %collective-permute-start.21 = (f32[12,128]{1,0:T(8,128)S(1)}, f32[12,128]{1,0:T(8,128)S(1)}, u32[]{:S(2)}, u32[]{:S(2)}) collective-permute-start(f32[12,128]{1,0:T(8,128)S(1)} %add.153), channel_id=1, source_target_pairs={{0,4},{1,5},{2,6},{3,7},{4,0},{5,1},{6,2},{7,3},{8,12},{9,13},{10,... | collective-permute-start | bytes 18440 | tf_op jit(solution)/shard_map/ppermute | solution.py:31

commit v4 on v3

v4 whole, which is shorter than its diff:
```python
import jax
import jax.numpy as jnp
from jax import lax
from jax.experimental import pallas as pl
from jax.experimental.pallas import tpu as pltpu
from jax.sharding import PartitionSpec as P

BLOCK = 128
EPSILON = 1e-05

f32 = jnp.float32
bf16 = jnp.bfloat16

LINE = 4
PAIR = 2
ORDER = ((3, 2, 1, 0), (0, 3, 2, 1), (1, 0, 3, 2), (0, 1, 2, 3))
PIECES = 2
TILE = 512

ANYWHERE = pl.BlockSpec(memory_space=pl.ANY)
NO_COST = pl.CostEstimate(flops=0, bytes_accessed=0, transcendentals=0)


def along_line(value, hops):
    pairs = [(a * PAIR + y, b * PAIR + y) for a, b in hops for y in range(PAIR)]
    return lax.ppermute(value, "tensor", pairs)


def across(value, bit):
    size = LINE * PAIR
    return lax.ppermute(value, "tensor", [(t, t ^ bit) for t in range(size)])


def product_kernel(count, index_ref, rows_ref, weights_ref, *refs):
    result = jnp.dot(rows_ref[...], weights_ref[...], preferred_element_type=f32)
    size = result.shape[0] // count
    for n, ref in enumerate(refs[-count:]):
        ref[...] = result[n * size : (n + 1) * size].astype(ref.dtype)


def product(hidden, weights, tensor_index, turn, own, kind, width, piece, count):
    rows, depth = hidden.shape
    steps = width // TILE
    rows = rows if piece is None else rows // PIECES
    size = rows // count

    def block(j, index):
        z, y = index[0] >> 1, index[0] & 1
        goal = ORDER[LINE - 1][turn]
        for other in range(LINE - 1):
            goal = jnp.where(z == other, ORDER[other][turn], goal)
        return (goal * PAIR + (y if own else 1 - y)) * steps + j

    return pl.pallas_call(
        lambda *refs: product_kernel(count, *refs),
        grid_spec=pltpu.PrefetchScalarGridSpec(
            num_scalar_prefetch=1,
            grid=(steps,),
            in_specs=[
                pl.BlockSpec((rows, depth), lambda j, index: (piece or 0, 0)),
                pl.BlockSpec((depth, TILE), lambda j, index: (0, block(j, index))),
            ],
            out_specs=[pl.BlockSpec((size, TILE), lambda j, index: (0, j))] * count,
        ),
        out_shape=[pltpu.HBM((size, width), kind)] * count,
        compiler_params=pltpu.CompilerParams(vmem_limit_bytes=40 * 1024 * 1024),
        cost_estimate=NO_COST,
    )(tensor_index.reshape(1), hidden, weights)


def pick_kernel(ids_ref, *refs):
    count = len(refs) // 2
    for n in range(count):
        refs[n - count][...] = refs[n][...]


def pick(ids, factors, sets, earlier=()):
    block = (1,) + factors.shape[1:]
    count = ids.shape[0] // sets
    spec = lambda s: pl.BlockSpec(block, lambda n, ids: (ids[s * count + n], 0, 0))
    return pl.pallas_call(
        pick_kernel,
        grid_spec=pltpu.PrefetchScalarGridSpec(
            num_scalar_prefetch=1,
            grid=(count,),
            in_specs=[spec(s) for s in range(sets)] + [ANYWHERE] * len(earlier),
            out_specs=[pl.BlockSpec(block, lambda n, ids: (n, 0, 0))] * sets,
        ),
        out_shape=[pltpu.HBM((count,) + factors.shape[1:], factors.dtype)] * sets,
        cost_estimate=NO_COST,
    )(ids, *[factors] * sets, *earlier)


def exchange_sum(value):
    a, b, c = [across(value, bit) for bit in (1, 2, 3)]
    value = (value + a) + (b + c)
    return value + across(value, 4)


UP = ((0, 1), (1, 2), (2, 3))
DOWN = ((3, 2), (2, 1), (1, 0))


class Sequence:
    def __init__(self):
        self.last = None

    def __call__(self, stage, *values):
        if self.last is not None:
            values = lax.optimization_barrier((self.last,) + values)[1:]
        result = stage(*values)
        self.last = jax.tree.leaves(result)[0]
        return result


def grid_sums(hidden, weights, residual, tensor_index, low_rank_terms, adapter_delta):
    width = residual.shape[1]
    z = tensor_index >> 1
    low, last_z = z < LINE // 2, z == LINE - 1
    then = Sequence()
    arrived, mine, first, second, third = {}, {}, {}, {}, {}
    add = lambda *terms: sum(t.astype(f32) for t in terms)
    narrow = lambda *terms: add(*terms).astype(bf16)
    size = hidden.shape[0] // PIECES

    def products(k, own, piece, count):
        kind = f32 if own else bf16
        return then(
            lambda h: product(h, weights, tensor_index, k, own, kind, width, piece, count), hidden
        )

    def theirs(k, piece=0, whole=False):
        value = products(k, False, None if whole else piece, 1)[0]
        arrived[piece, k] = across(value, 1)

    def ours(k):
        for p, value in enumerate(products(k, True, None, PIECES)):
            mine[p, k] = value

    def sent(value, further):
        return value if further is None else jnp.concatenate([value, further.astype(bf16)], 0)

    def hop_1(p, further=None):
        value = sent(then(narrow, mine[p, 0], arrived[p, 0][:size]), further)
        first[p] = along_line(value, [UP[0], DOWN[0]])

    def hop_2(p, further=None):
        value = sent(then(narrow, mine[p, 1], arrived[p, 1], first[p][:size]), further)
        second[p] = (along_line(value, UP[:2]), along_line(value, DOWN[:2]))

    def hop_3(p, further):
        def stage(up, down, own, came_own, other, came_other):
            here, there = add(own, came_own), add(other, came_other)
            return narrow(here, up[:size]), narrow(jnp.where(last_z, here, there), down[:size])

        up, down = then(stage, *second[p], mine[p, 2], arrived[p, 2], mine[p, 0], arrived[p, 0][:size])
        third[p] = (along_line(sent(up, further), UP), along_line(sent(down, further), DOWN))

    theirs(0, 0)
    low_rank_of, second_factors_of = low_rank_terms(then.last)
    value = products(0, False, 1, 1)[0]
    low_rank = low_rank_of(hidden).reshape(-1, width)
    arrived[1, 0] = across(then(sent, value, low_rank), 1)
    ours(0)
    theirs(1, 0)
    hop_1(0)
    ours(1)
    theirs(1, 1)
    low_rank = add(low_rank, arrived[1, 0][size:])
    hop_1(1, low_rank)
    theirs(2, 0)
    ours(2)
    hop_2(0)
    theirs(2, 1)
    low_rank = add(low_rank, first[1][size:])
    hop_2(1, low_rank)
    hop_3(0, None)
    theirs(3, whole=True)
    ours(3)
    up, down = second[1]
    low_rank = narrow(low_rank, jnp.where(low, down[size:], up[size:]))
    hop_3(1, low_rank)
    second_factors = second_factors_of(mine[0, 3])
    settled = then(add, *third[0], mine[0, 3], residual[:size])
    up, down = third[1] = then(lambda *t: t, *third[1])
    low_rank = jnp.where(z == 0, down[size:], jnp.where(last_z, up[size:], low_rank))
    delta = adapter_delta(low_rank.reshape(hidden.shape[0], -1), second_factors)

    def stage(settled, up, down, own, kept, delta):
        return jnp.concatenate([settled, add(up[:size], down[:size], own, kept)], 0) + delta.astype(f32)

    settled = then(stage, settled, up, down, mine[1, 3], residual[size:], delta)
    return add(*lax.optimization_barrier((settled, arrived[0, 3])))


def shards(
    gate_preactivation,
    up_preactivation,
    base_down_matrix,
    adapter_first_factor,
    adapter_second_factor,
    residual,
    scoring_head_matrix,
    block_adapter_index,
    block_span_start,
    block_span_end,
):
    rows_local, hidden_width = gate_preactivation.shape
    slice_width = residual.shape[1]
    model_width = scoring_head_matrix.shape[0]
    blocks = rows_local // BLOCK
    adapters_here = adapter_first_factor.shape[0]
    data_index = lax.axis_index("dp")
    data_size = lax.axis_size("dp")
    tensor_index = lax.axis_index("tensor")
    on_grid = lax.axis_size("tensor") == LINE * PAIR

    ids = block_adapter_index.reshape(data_size, blocks)
    owner = lax.dynamic_index_in_dim(ids, data_index, 0, keepdims=False) // adapters_here
    first_turned = jnp.swapaxes(adapter_first_factor, 1, 2)
    steps = [step for step in range(1, data_size)] + [0]
    turned = jnp.concatenate(
        [lax.dynamic_slice_in_dim(ids, (data_index + step) % data_size, 1)[0] for step in steps]
    )
    turned = jnp.clip(turned - data_index * adapters_here, 0, adapters_here - 1)

    def fetched(factors, earlier):
        *wanted, kept = pick(turned, factors, data_size, earlier)
        for n, step in enumerate(steps[:-1]):
            hop = [(d, (d + step) % data_size) for d in range(data_size)]
            take = (owner == (data_index - step) % data_size)[:, None, None]
            kept = jnp.where(take, lax.ppermute(wanted[n], "dp", hop), kept)
        return kept

    def low_rank_terms(*earlier):
        first_factors = fetched(first_turned, earlier)

        def terms(rows):
            return jnp.einsum(
                "bcj,bej->bce",
                rows.reshape(blocks, BLOCK, hidden_width),
                first_factors,
                preferred_element_type=f32,
            ).reshape(rows_local, -1)

        return terms, lambda *earlier: fetched(adapter_second_factor, earlier)

    def adapter_delta(low_rank, second_factors):
        return jnp.einsum(
            "bcn,bnt->bct",
            low_rank.astype(bf16).reshape(blocks, BLOCK, -1),
            second_factors,
            preferred_element_type=f32,
        ).reshape(rows_local, slice_width).astype(bf16)

    hidden = (
        jax.nn.silu(gate_preactivation.astype(f32)) * up_preactivation.astype(f32)
    ).astype(bf16)
    if on_grid:
        combined = grid_sums(
            hidden, base_down_matrix, residual, tensor_index, low_rank_terms, adapter_delta
        )
    else:
        low_rank_of, second_factors_of = low_rank_terms()
        delta = adapter_delta(lax.psum(low_rank_of(hidden), "tensor"), second_factors_of())
        base_part = lax.psum_scatter(
            jnp.dot(hidden, base_down_matrix, preferred_element_type=f32),
            "tensor",
            scatter_dimension=1,
            tiled=True,
        )
        combined = residual.astype(f32) + delta.astype(f32) + base_part
    layer_out = combined.astype(bf16)
    head = lax.dynamic_slice_in_dim(
        scoring_head_matrix, tensor_index * slice_width, slice_width
    )
    stats = jnp.stack([jnp.sum(combined * combined, 1), jnp.sum(combined * head[None, :], 1)])
    stats = stats.reshape(2 * blocks, BLOCK)
    stats = exchange_sum(stats) if on_grid else lax.psum(stats, "tensor")
    square_sum, head_sum = stats[:blocks], stats[blocks:]
    scores = head_sum * lax.rsqrt(square_sum / model_width + EPSILON)
    position = jnp.arange(BLOCK, dtype=jnp.int32)
    inside = (position[None, :] >= block_span_start[:, None]) & (
        position[None, :] < block_span_end[:, None]
    )
    span_scores = jnp.sum(jnp.where(inside, scores, f32(0.0)), 1)
    return (layer_out, span_scores)


def solution(mesh):
    return jax.shard_map(
        shards,
        mesh=mesh,
        in_specs=(
            P(("groups", "dp"), "tensor"),
            P(("groups", "dp"), "tensor"),
            P("tensor", None),
            P("dp", "tensor", None),
            P("dp", None, "tensor"),
            P(("groups", "dp"), "tensor"),
            P(),
            P("groups"),
            P(("groups", "dp")),
            P(("groups", "dp")),
        ),
        out_specs=(P(("groups", "dp"), "tensor"), P(("groups", "dp"))),
        check_vma=False,
    )
```

time: 180 us -> 201 us (1.12)
  waiting for transfers between devices: 22.2 us -> 46.5 us
  Pallas kernels: 72.9 us -> 64.7 us
  starting transfers between devices: 47.3 us -> 51.3 us
  other arithmetic: 26.5 us -> 29.5 us
    ppermute x10, waiting for transfers between devices: 3.69 us -> 18.7 us  [along_line(): return lax.ppermute(value, 'tensor', pairs)]
    ppermute x10 -> x11, waiting for transfers between devices: 18.6 us -> 27.8 us  [across(): return lax.ppermute(value, 'tensor', [(t, t ^ bit) for t in range(size)])]
    pallas_call x4 -> x2, Pallas kernels: 19.3 us -> 11.1 us  [pick(): pl.pallas_call(pick_kernel, grid_spec=pltpu.PrefetchScalarGridSpec(num_sc...]
    ppermute x10, starting transfers between devices: 30.5 us -> 32.9 us  [along_line(): return lax.ppermute(value, 'tensor', pairs)]
    ppermute x10 -> x11, starting transfers between devices: 15.9 us -> 18.3 us  [across(): return lax.ppermute(value, 'tensor', [(t, t ^ bit) for t in range(size)])]
    add x3 -> x2, other arithmetic: 5.08 us -> 3.78 us  [grid_sums(): add = lambda *terms: sum((t.astype(f32) for t in terms))]
  transfers between devices with their start and end apart: 22 -> 23, of which waited for: 6 -> 12; matrix products, arithmetic and copies ran while one was open for 15% -> 13% of each run, Pallas kernels for 38% -> 27%
where the time goes in v4:
time: 201 us; the launch traced here: 200 us
  Pallas kernels  64.7 us (32%)
  starting transfers between devices  51.3 us (26%)
  waiting for transfers between devices  46.5 us (23%)
  other arithmetic  29.5 us (15%)
  matrix products  4.79 us (2%)
  local copies, waits for them, and re-layouts  2.28 us (1%)
    pallas_call x11, Pallas kernels, product(): pl.pallas_call(lambda *refs: product_kernel(count, *refs), grid_spec=pltp...  53.6 us
    ppermute x10, starting transfers between devices, along_line(): return lax.ppermute(value, 'tensor', pairs)  32.9 us
    ppermute x11, waiting for transfers between devices, across(): return lax.ppermute(value, 'tensor', [(t, t ^ bit) for t in range(size)])  27.8 us
    ppermute x10, waiting for transfers between devices, along_line(): return lax.ppermute(value, 'tensor', pairs)  18.7 us
    ppermute x11, starting transfers between devices, across(): return lax.ppermute(value, 'tensor', [(t, t ^ bit) for t in range(size)])  18.3 us
    convert_element_type x7, other arithmetic, grid_sums(): narrow = lambda *terms: add(*terms).astype(bf16)  11.8 us
    pallas_call x2, Pallas kernels, pick(): pl.pallas_call(pick_kernel, grid_spec=pltpu.PrefetchScalarGridSpec(num_sc...  11.1 us
    convert_element_type x1, other arithmetic, shards(): hidden = (jax.nn.silu(gate_preactivation.astype(f32)) * up_preactivation....  4.27 us
  transfers between devices with their start and end apart: 23, of which 12 were waited for; matrix products, arithmetic and copies ran while one was open for 13% of the time, Pallas kernels for 27%

profile of v4, /device:TPU:0, one launch (start us, length us, event | category | flops | bytes accessed | tf_op | source)
XLA Modules:
  0.0 200.1 jit_solution(12206186432374809355)
XLA Ops:
  0.7 0.7 reshape.62
  1.4 4.3 %fusion.4.refs_1_ = bf16[768,1792]{1,0:T(8,128)(2,1)S(1)} fusion(bf16[768,1792]{1,0:T(8,128)(2,1)} %param.11, bf16[768,1792]{1,0:T(8,128)(2,1)} %param.10), kind=kLoop, calls=%fused_computation.6 | loop fusion | flops 11010048 | bytes 8257536 | tf_op jit(solution)/shard_map/convert_element_type | solution.py:258
  5.7 4.1 %shard_map.113.refs_2_ = bf16[384,1024]{1,0:T(8,128)(2,1)} custom-call(s32[1]{0:T(128)} %bitcast.refs_0_, bf16[768,1792]{1,0:T(8,128)(2,1)S(1)} %fusion.4.refs_1_, bf16[1792,8192]{1,0:T(8,128)(2,1)} %refs_2_.21), custom_call_target="tpu_custom_call" | custom-call | tf_op jit(solution)/shard_map/pallas_call | solution.py:54
  9.8 0.7 fusion.22.ids_ref
  10.4 5.7 %shard_map.115 = (bf16[6,64,1792]{2,1,0:T(8,128)(2,1)}, bf16[6,64,1792]{2,1,0:T(8,128)(2,1)}) custom-call(s32[12]{0:T(128)} %fusion.22.ids_ref, bf16[32,64,1792]{2,1,0:T(8,128)(2,1)} %bitcast.17, bf16[32,64,1792]{2,1,0:T(8,128)(2,1)} %bitcast.18, bf16[384,1024]{1,0:T(8,128)(2,1)} %shard_map.113.refs_2_), custom_call_target="tpu_custom_call" | custom-call | tf_op jit(solution)/shard_map/pallas_call | solution.py:81
  16.1 3.0 %collective-permute-start.1 = (bf16[384,1024]{1,0:T(8,128)(2,1)}, bf16[384,1024]{1,0:T(8,128)(2,1)}, u32[]{:S(2)}, u32[]{:S(2)}) collective-permute-start(bf16[384,1024]{1,0:T(8,128)(2,1)} %shard_map.113.refs_2_), channel_id=1, source_target_pairs={{0,1},{1,0},{2,3},{3,2},{4,5},{5,4},{6,7},{7,6},{8,9},{9,8},{10,11... | collective-permute-start | bytes 2359304 | tf_op jit(solution)/shard_map/ppermute | solution.py:31
  19.1 4.1 %shard_map.114 = bf16[384,1024]{1,0:T(8,128)(2,1)} custom-call(s32[1]{0:T(128)} %bitcast.refs_0_, bf16[768,1792]{1,0:T(8,128)(2,1)S(1)} %fusion.4.refs_1_, bf16[1792,8192]{1,0:T(8,128)(2,1)} %refs_2_.21), custom_call_target="tpu_custom_call" | custom-call | tf_op jit(solution)/shard_map/pallas_call | solution.py:54
  23.2 2.7 %fusion.5 = f32[6,128,64]{2,1,0:T(8,128)S(1)} fusion(bf16[6,128,1792]{2,1,0:T(8,128)(2,1)S(1)} %bitcast.16, bf16[6,64,1792]{2,1,0:T(8,128)(2,1)} %collective-permute-done, bf16[6,64,1792]{2,1,0:T(8,128)(2,1)} %get-tuple-element.64, pred[6]{0:T(512)(128)(4,1)S(1)} %fusion.23), kind=kOutput, calls=%fused_computation.24 | convolution fusion | flops 176848896 | bytes 5701638 | tf_op jit(solution)/shard_map/bcj,bej->bce/dot_general | solution.py:239
  26.1 1.3 pad_maximum_fusion.2
  27.5 5.7 %shard_map.116 = (f32[384,1024]{1,0:T(8,128)}, f32[384,1024]{1,0:T(8,128)}) custom-call(s32[1]{0:T(128)} %bitcast.refs_0_, bf16[768,1792]{1,0:T(8,128)(2,1)S(1)} %fusion.4.refs_1_, bf16[1792,8192]{1,0:T(8,128)(2,1)} %refs_2_.21), custom_call_target="tpu_custom_call" | custom-call | tf_op jit(solution)/shard_map/pallas_call | solution.py:54
  33.2 4.2 %shard_map.117 = bf16[384,1024]{1,0:T(8,128)(2,1)} custom-call(s32[1]{0:T(128)} %bitcast.refs_0_, bf16[768,1792]{1,0:T(8,128)(2,1)S(1)} %fusion.4.refs_1_, bf16[1792,8192]{1,0:T(8,128)(2,1)} %refs_2_.21), custom_call_target="tpu_custom_call" | custom-call | tf_op jit(solution)/shard_map/pallas_call | solution.py:54
  37.4 2.0 collective-permute-start.3
  39.4 1.4 add_convert_fusion.7
  40.8 3.5 %collective-permute-start.4 = (bf16[384,1024]{1,0:T(8,128)(2,1)S(1)}, bf16[384,1024]{1,0:T(8,128)(2,1)S(1)}, u32[]{:S(2)}, u32[]{:S(2)}) collective-permute-start(bf16[384,1024]{1,0:T(8,128)(2,1)S(1)} %add_convert_fusion.7), channel_id=1, source_target_pairs={{0,2},{1,3},{6,4},{7,5},{8,10},{9,11},{14,12},{15,13},{16,18},{17,... | collective-permute-start | bytes 2359304 | tf_op jit(solution)/shard_map/ppermute | solution.py:26
  44.3 5.8 %shard_map.118 = (f32[384,1024]{1,0:T(8,128)}, f32[384,1024]{1,0:T(8,128)}) custom-call(s32[1]{0:T(128)} %bitcast.refs_0_, bf16[768,1792]{1,0:T(8,128)(2,1)S(1)} %fusion.4.refs_1_, bf16[1792,8192]{1,0:T(8,128)(2,1)} %refs_2_.21), custom_call_target="tpu_custom_call" | custom-call | tf_op jit(solution)/shard_map/pallas_call | solution.py:54
  50.1 4.1 %shard_map.119 = bf16[384,1024]{1,0:T(8,128)(2,1)} custom-call(s32[1]{0:T(128)} %bitcast.refs_0_, bf16[768,1792]{1,0:T(8,128)(2,1)S(1)} %fusion.4.refs_1_, bf16[1792,8192]{1,0:T(8,128)(2,1)} %refs_2_.21), custom_call_target="tpu_custom_call" | custom-call | tf_op jit(solution)/shard_map/pallas_call | solution.py:54
  54.2 2.5 %collective-permute-done.2 = bf16[432,1024]{1,0:T(8,128)(2,1)S(1)} collective-permute-done((bf16[432,1024]{1,0:T(8,128)(2,1)S(1)}, bf16[432,1024]{1,0:T(8,128)(2,1)S(1)}, u32[]{:S(2)}, u32[]{:S(2)}) %collective-permute-start.2) | collective-permute-done | bytes 884768 | tf_op jit(solution)/shard_map/ppermute | solution.py:31
  57.0 0.9 copy-done.5
  58.0 4.1 %collective-permute-start.6 = (bf16[432,1024]{1,0:T(8,128)(2,1)S(1)}, bf16[432,1024]{1,0:T(8,128)(2,1)S(1)}, u32[]{:S(2)}, u32[]{:S(2)}) collective-permute-start(bf16[432,1024]{1,0:T(8,128)(2,1)S(1)} %pad_maximum_fusion.3), channel_id=1, source_target_pairs={{0,2},{1,3},{6,4},{7,5},{8,10},{9,11},{14,12},{15,13},{16,18},{17,... | collective-permute-start | bytes 2654216 | tf_op jit(solution)/shard_map/ppermute | solution.py:26
  62.1 1.6 collective-permute-start.5
  63.7 4.1 %shard_map.120 = bf16[384,1024]{1,0:T(8,128)(2,1)} custom-call(s32[1]{0:T(128)} %bitcast.refs_0_, bf16[768,1792]{1,0:T(8,128)(2,1)S(1)} %fusion.4.refs_1_, bf16[1792,8192]{1,0:T(8,128)(2,1)} %refs_2_.21), custom_call_target="tpu_custom_call" | custom-call | tf_op jit(solution)/shard_map/pallas_call | solution.py:54
  67.8 6.0 %shard_map.121 = (f32[384,1024]{1,0:T(8,128)}, f32[384,1024]{1,0:T(8,128)}) custom-call(s32[1]{0:T(128)} %bitcast.refs_0_, bf16[768,1792]{1,0:T(8,128)(2,1)S(1)} %fusion.4.refs_1_, bf16[1792,8192]{1,0:T(8,128)(2,1)} %refs_2_.21), custom_call_target="tpu_custom_call" | custom-call | tf_op jit(solution)/shard_map/pallas_call | solution.py:54
  73.8 1.3 add_convert_fusion.5
  75.1 4.5 %collective-permute-start.7 = (bf16[384,1024]{1,0:T(8,128)(2,1)}, bf16[384,1024]{1,0:T(8,128)(2,1)}, u32[]{:S(2)}, u32[]{:S(2)}) collective-permute-start(bf16[384,1024]{1,0:T(8,128)(2,1)} %add_convert_fusion.5), channel_id=1, source_target_pairs={{0,2},{1,3},{2,4},{3,5},{8,10},{9,11},{10,12},{11,13},{16,18},{17,... | collective-permute-start | bytes 2359304 | tf_op jit(solution)/shard_map/ppermute | solution.py:26
  79.7 1.6 collective-permute-start.8
  81.2 1.5 collective-permute-start.9
  82.7 4.0 %shard_map.122 = bf16[384,1024]{1,0:T(8,128)(2,1)} custom-call(s32[1]{0:T(128)} %bitcast.refs_0_, bf16[768,1792]{1,0:T(8,128)(2,1)S(1)} %fusion.4.refs_1_, bf16[1792,8192]{1,0:T(8,128)(2,1)} %refs_2_.21), custom_call_target="tpu_custom_call" | custom-call | tf_op jit(solution)/shard_map/pallas_call | solution.py:54
  86.8 3.6 %collective-permute-done.5 = bf16[384,1024]{1,0:T(8,128)(2,1)S(1)} collective-permute-done((bf16[384,1024]{1,0:T(8,128)(2,1)S(1)}, bf16[384,1024]{1,0:T(8,128)(2,1)S(1)}, u32[]{:S(2)}, u32[]{:S(2)}) %collective-permute-start.5) | collective-permute-done | bytes 786464 | tf_op jit(solution)/shard_map/ppermute | solution.py:31
  90.4 0.4 add_convert_fusion.4
  90.9 1.0 pad_maximum_fusion.4
  91.8 4.8 %collective-permute-start.10 = (bf16[432,1024]{1,0:T(8,128)(2,1)}, bf16[432,1024]{1,0:T(8,128)(2,1)}, u32[]{:S(2)}, u32[]{:S(2)}) collective-permute-start(bf16[432,1024]{1,0:T(8,128)(2,1)} %pad_maximum_fusion.4), channel_id=1, source_target_pairs={{0,2},{1,3},{2,4},{3,5},{8,10},{9,11},{10,12},{11,13},{16,18},{17,... | collective-permute-start | bytes 2654216 | tf_op jit(solution)/shard_map/ppermute | solution.py:26
  96.6 1.6 collective-permute-start.11
  98.2 0.9 collective-permute-done.7
  99.1 1.5 collective-permute-start.12
  100.6 6.7 %collective-permute-done.9 = bf16[384,1024]{1,0:T(8,128)(2,1)} collective-permute-done((bf16[384,1024]{1,0:T(8,128)(2,1)}, bf16[384,1024]{1,0:T(8,128)(2,1)}, u32[]{:S(2)}, u32[]{:S(2)}) %collective-permute-start.9) | collective-permute-done | bytes 786464 | tf_op jit(solution)/shard_map/ppermute | solution.py:31
  107.4 4.9 %add_convert_fusion.1 = (bf16[384,1024]{1,0:T(8,128)(2,1)}, bf16[384,1024]{1,0:T(8,128)(2,1)}) fusion(bf16[384,1024]{1,0:T(8,128)(2,1)} %collective-permute-done.8, f32[384,1024]{1,0:T(8,128)} %get-tuple-element.99, bf16[384,1024]{1,0:T(8,128)(2,1)} %collective-permute-done.1, f32[384,1024]{1,0:T(8,128)} %get-tuple-element.89, ...), kind=kLoop, calls=%fused_computation.15 | loop fusion | flops 4325376 | bytes 7864321 | tf_op jit(solution)/shard_map/convert_element_type | solution.py:123
  112.2 4.8 %collective-permute-start.13 = (bf16[384,1024]{1,0:T(8,128)(2,1)}, bf16[384,1024]{1,0:T(8,128)(2,1)}, u32[]{:S(2)}, u32[]{:S(2)}) collective-permute-start(bf16[384,1024]{1,0:T(8,128)(2,1)} %get-tuple-element.128), channel_id=1, source_target_pairs={{0,2},{1,3},{2,4},{3,5},{4,6},{5,7},{8,10},{9,11},{10,12},{11,13},... | collective-permute-start | bytes 2359304 | tf_op jit(solution)/shard_map/ppermute | solution.py:26
  117.0 5.6 %shard_map.123 = bf16[768,1024]{1,0:T(8,128)(2,1)} custom-call(s32[1]{0:T(128)} %bitcast.refs_0_, bf16[768,1792]{1,0:T(8,128)(2,1)S(1)} %fusion.4.refs_1_, bf16[1792,8192]{1,0:T(8,128)(2,1)} %refs_2_.21), custom_call_target="tpu_custom_call" | custom-call | tf_op jit(solution)/shard_map/pallas_call | solution.py:54
  122.6 6.0 %shard_map.124 = (f32[384,1024]{1,0:T(8,128)}, f32[384,1024]{1,0:T(8,128)}) custom-call(s32[1]{0:T(128)} %bitcast.refs_0_, bf16[768,1792]{1,0:T(8,128)(2,1)S(1)} %fusion.4.refs_1_, bf16[1792,8192]{1,0:T(8,128)(2,1)} %refs_2_.21), custom_call_target="tpu_custom_call" | custom-call | tf_op jit(solution)/shard_map/pallas_call | solution.py:54
  128.6 1.3 collective-permute-start.14
  130.0 2.5 %add_convert_fusion = (bf16[384,1024]{1,0:T(8,128)(2,1)S(1)}, bf16[384,1024]{1,0:T(8,128)(2,1)S(1)}) fusion(f32[384,1024]{1,0:T(8,128)S(1)} %copy-done.2, bf16[384,1024]{1,0:T(8,128)(2,1)S(1)} %slice.65, f32[384,1024]{1,0:T(8,128)S(1)} %copy-done.11, bf16[384,1024]{1,0:T(8,128)(2,1)} %collective-permute-done.12, ...), kind=kLoop, calls=%fused_computation.13 | loop fusion | flops 4325376 | bytes 7864321 | tf_op jit(solution)/shard_map/convert_element_type | solution.py:123
  132.5 1.1 add_convert_fusion.8
  133.6 1.1 pad_maximum_fusion
  134.7 5.5 %collective-permute-start.15 = (bf16[432,1024]{1,0:T(8,128)(2,1)}, bf16[432,1024]{1,0:T(8,128)(2,1)}, u32[]{:S(2)}, u32[]{:S(2)}) collective-permute-start(bf16[432,1024]{1,0:T(8,128)(2,1)} %get-tuple-element.132), channel_id=1, source_target_pairs={{0,2},{1,3},{2,4},{3,5},{4,6},{5,7},{8,10},{9,11},{10,12},{11,13},... | collective-permute-start | bytes 2654216 | tf_op jit(solution)/shard_map/ppermute | solution.py:26
  140.1 1.3 collective-permute-start.16
  141.5 5.4 %shard_map.125 = (bf16[6,64,1024]{2,1,0:T(8,128)(2,1)}, bf16[6,64,1024]{2,1,0:T(8,128)(2,1)}) custom-call(s32[12]{0:T(128)} %fusion.22.ids_ref, bf16[32,64,1024]{2,1,0:T(8,128)(2,1)} %refs_1_.1, bf16[32,64,1024]{2,1,0:T(8,128)(2,1)} %refs_1_.1, f32[384,1024]{1,0:T(8,128)} %get-tuple-element.104.refs_2_), custom_call_target="tpu_custom_call" | custom-call | tf_op jit(solution)/shard_map/pallas_call | solution.py:81
  147.0 1.6 collective-permute-start.18
  148.6 2.7 %collective-permute-done.14 = bf16[384,1024]{1,0:T(8,128)(2,1)} collective-permute-done((bf16[384,1024]{1,0:T(8,128)(2,1)}, bf16[384,1024]{1,0:T(8,128)(2,1)}, u32[]{:S(2)}, u32[]{:S(2)}) %collective-permute-start.14) | collective-permute-done | bytes 786464 | tf_op jit(solution)/shard_map/ppermute | solution.py:26
  151.3 1.9 convert_add_fusion.2
  153.2 4.1 %collective-permute-done.15 = bf16[432,1024]{1,0:T(8,128)(2,1)} collective-permute-done((bf16[432,1024]{1,0:T(8,128)(2,1)}, bf16[432,1024]{1,0:T(8,128)(2,1)}, u32[]{:S(2)}, u32[]{:S(2)}) %collective-permute-start.15) | collective-permute-done | bytes 884768 | tf_op jit(solution)/shard_map/ppermute | solution.py:26
  157.3 10.9 %collective-permute-done.16 = bf16[432,1024]{1,0:T(8,128)(2,1)} collective-permute-done((bf16[432,1024]{1,0:T(8,128)(2,1)S(1)}, bf16[432,1024]{1,0:T(8,128)(2,1)}, u32[]{:S(2)}, u32[]{:S(2)}) %collective-permute-start.16) | collective-permute-done | bytes 884768 | tf_op jit(solution)/shard_map/ppermute | solution.py:26
  168.3 1.0 select_select_fusion
  169.4 2.1 %convolution_convert_fusion = bf16[6,128,1024]{2,1,0:T(8,128)(2,1)S(1)} fusion(bf16[6,128,64]{2,1,0:T(8,128)(2,1)S(1)} %reshape_reshape.7, bf16[6,64,1024]{2,1,0:T(8,128)(2,1)} %collective-permute-done.17, bf16[6,64,1024]{2,1,0:T(8,128)(2,1)} %get-tuple-element.113, pred[6]{0:T(512)(128)(4,1)S(1)} %fusion.23), kind=kOutput, calls=%fused_computation.11 | convolution fusion | flops 101842944 | bytes 3244038 | tf_op jit(solution)/shard_map/bcn,bnt->bct/dot_general | solution.py:249
  171.5 1.9 convert_add_fusion.1
  173.5 0.6 maximum_add_fusion
  174.1 10.0 %collective-permute-done.18 = bf16[768,1024]{1,0:T(8,128)(2,1)} collective-permute-done((bf16[768,1024]{1,0:T(8,128)(2,1)}, bf16[768,1024]{1,0:T(8,128)(2,1)}, u32[]{:S(2)}, u32[]{:S(2)}) %collective-permute-start.18) | collective-permute-done | bytes 1572896 | tf_op jit(solution)/shard_map/ppermute | solution.py:31
  184.2 3.2 %multiply_reduce_fusion.1 = (f32[768]{0:T(1024)S(1)}, f32[768]{0:T(1024)S(1)}, bf16[768,1024]{1,0:T(8,128)(2,1)}) fusion(f32[768,1024]{1,0:T(8,128)S(1)} %maximum_add_fusion, bf16[768,1024]{1,0:T(8,128)(2,1)} %collective-permute-done.18, f32[1024]{0:T(1024)S(1)} %dynamic-slice-done), kind=kLoop, calls=%fused_computation.9 | loop fusion | flops 5503488 | bytes 6301696 | tf_op jit(solution)/shard_map/reduce_sum | solution.py:277
  187.4 2.7 %collective-permute-start.20 = (f32[12,128]{1,0:T(8,128)S(1)}, f32[12,128]{1,0:T(8,128)S(1)}, u32[]{:S(2)}, u32[]{:S(2)}) collective-permute-start(f32[12,128]{1,0:T(8,128)S(1)} %reshape.63), channel_id=1, source_target_pairs={{0,2},{1,3},{2,0},{3,1},{4,6},{5,7},{6,4},{7,5},{8,10},{9,11},{10,... | collective-permute-start | bytes 18440 | tf_op jit(solution)/shard_map/ppermute | solution.py:31
  190.1 1.0 collective-permute-start.21
  191.2 0.5 collective-permute-start.19
  191.8 2.9 %collective-permute-done.21 = f32[12,128]{1,0:T(8,128)S(1)} collective-permute-done((f32[12,128]{1,0:T(8,128)S(1)}, f32[12,128]{1,0:T(8,128)S(1)}, u32[]{:S(2)}, u32[]{:S(2)}) %collective-permute-start.21) | collective-permute-done | bytes 6176 | tf_op jit(solution)/shard_map/ppermute | solution.py:31
  194.8 2.8 %collective-permute-start.22 = (f32[12,128]{1,0:T(8,128)S(1)}, f32[12,128]{1,0:T(8,128)S(1)}, u32[]{:S(2)}, u32[]{:S(2)}) collective-permute-start(f32[12,128]{1,0:T(8,128)S(1)} %add_add_fusion), channel_id=1, source_target_pairs={{0,4},{1,5},{2,6},{3,7},{4,0},{5,1},{6,2},{7,3},{8,12},{9,13},{10,... | collective-permute-start | bytes 18440 | tf_op jit(solution)/shard_map/ppermute | solution.py:31
  197.6 1.8 collective-permute-done.22
  199.4 0.7 fusion.17
  (69 shorter events, 1.5 us)
Async XLA Ops:
  16.1 7.1 %collective-permute-start = (bf16[6,64,1792]{2,1,0:T(8,128)(2,1)}, bf16[6,64,1792]{2,1,0:T(8,128)(2,1)}, u32[]{:S(2)}, u32[]{:S(2)}) collective-permute-start(bf16[6,64,1792]{2,1,0:T(8,128)(2,1)} %get-tuple-element.63), channel_id=1, source_target_pairs={{0,8},{8,0},{1,9},{9,1},{2,10},{10,2},{3,11},{11,3},{4,12},{12,4},... | collective-permute-start | bytes 4128776 | tf_op jit(solution)/shard_map/ppermute | solution.py:232
  16.1 23.2 %collective-permute-start.1 = (bf16[384,1024]{1,0:T(8,128)(2,1)}, bf16[384,1024]{1,0:T(8,128)(2,1)}, u32[]{:S(2)}, u32[]{:S(2)}) collective-permute-start(bf16[384,1024]{1,0:T(8,128)(2,1)} %shard_map.113.refs_2_), channel_id=1, source_target_pairs={{0,1},{1,0},{2,3},{3,2},{4,5},{5,4},{6,7},{7,6},{8,9},{9,8},{10,11... | collective-permute-start | bytes 2359304 | tf_op jit(solution)/shard_map/ppermute | solution.py:31
  26.1 7.1 %copy-start.4 = (f32[48,1024]{1,0:T(8,128)}, f32[48,1024]{1,0:T(8,128)S(1)}, u32[]{:S(2)}) copy-start(f32[48,1024]{1,0:T(8,128)S(1)} %reshape_reshape.6) | copy-start | bytes 589828
  27.4 29.3 %collective-permute-start.2 = (bf16[432,1024]{1,0:T(8,128)(2,1)S(1)}, bf16[432,1024]{1,0:T(8,128)(2,1)S(1)}, u32[]{:S(2)}, u32[]{:S(2)}) collective-permute-start(bf16[432,1024]{1,0:T(8,128)(2,1)S(1)} %pad_maximum_fusion.2), channel_id=1, source_target_pairs={{0,1},{1,0},{2,3},{3,2},{4,5},{5,4},{6,7},{7,6},{8,9},{9,8},{10,11... | collective-permute-start | bytes 2654216 | tf_op jit(solution)/shard_map/ppermute | solution.py:31
  33.2 6.2 %copy-start.3 = (f32[384,1024]{1,0:T(8,128)S(1)}, f32[384,1024]{1,0:T(8,128)}, u32[]{:S(2)}) copy-start(f32[384,1024]{1,0:T(8,128)} %get-tuple-element.99) | copy-start | bytes 4718596
  37.4 36.4 %collective-permute-start.3 = (bf16[384,1024]{1,0:T(8,128)(2,1)}, bf16[384,1024]{1,0:T(8,128)(2,1)S(1)}, u32[]{:S(2)}, u32[]{:S(2)}) collective-permute-start(bf16[384,1024]{1,0:T(8,128)(2,1)} %shard_map.117), channel_id=1, source_target_pairs={{0,1},{1,0},{2,3},{3,2},{4,5},{5,4},{6,7},{7,6},{8,9},{9,8},{10,11... | collective-permute-start | bytes 2359304 | tf_op jit(solution)/shard_map/ppermute | solution.py:31
  40.8 33.0 %collective-permute-start.4 = (bf16[384,1024]{1,0:T(8,128)(2,1)S(1)}, bf16[384,1024]{1,0:T(8,128)(2,1)S(1)}, u32[]{:S(2)}, u32[]{:S(2)}) collective-permute-start(bf16[384,1024]{1,0:T(8,128)(2,1)S(1)} %add_convert_fusion.7), channel_id=1, source_target_pairs={{0,2},{1,3},{6,4},{7,5},{8,10},{9,11},{14,12},{15,13},{16,18},{17,... | collective-permute-start | bytes 2359304 | tf_op jit(solution)/shard_map/ppermute | solution.py:26
  54.2 2.6 %copy-start.1 = (f32[384,1024]{1,0:T(8,128)S(1)}, f32[384,1024]{1,0:T(8,128)}, u32[]{:S(2)}) copy-start(f32[384,1024]{1,0:T(8,128)} %get-tuple-element.106) | copy-start | bytes 4718596
  56.7 34.1 %copy-start.12 = (bf16[432,1024]{1,0:T(8,128)(2,1)}, bf16[432,1024]{1,0:T(8,128)(2,1)S(1)}, u32[]{:S(2)}) copy-start(bf16[432,1024]{1,0:T(8,128)(2,1)S(1)} %collective-permute-done.2) | copy-start | bytes 2654212
  56.8 1.2 copy-start.5
  57.9 4.2 %copy-start.14 = (bf16[384,1024]{1,0:T(8,128)(2,1)S(1)}, bf16[384,1024]{1,0:T(8,128)(2,1)}, u32[]{:S(2)}) copy-start(bf16[384,1024]{1,0:T(8,128)(2,1)} %shard_map.119) | copy-start | bytes 2359300
  58.0 28.7 %collective-permute-start.6 = (bf16[432,1024]{1,0:T(8,128)(2,1)S(1)}, bf16[432,1024]{1,0:T(8,128)(2,1)S(1)}, u32[]{:S(2)}, u32[]{:S(2)}) collective-permute-start(bf16[432,1024]{1,0:T(8,128)(2,1)S(1)} %pad_maximum_fusion.3), channel_id=1, source_target_pairs={{0,2},{1,3},{6,4},{7,5},{8,10},{9,11},{14,12},{15,13},{16,18},{17,... | collective-permute-start | bytes 2654216 | tf_op jit(solution)/shard_map/ppermute | solution.py:26
  62.1 28.3 %collective-permute-start.5 = (bf16[384,1024]{1,0:T(8,128)(2,1)S(1)}, bf16[384,1024]{1,0:T(8,128)(2,1)S(1)}, u32[]{:S(2)}, u32[]{:S(2)}) collective-permute-start(bf16[384,1024]{1,0:T(8,128)(2,1)S(1)} %copy-done.14), channel_id=1, source_target_pairs={{0,1},{1,0},{2,3},{3,2},{4,5},{5,4},{6,7},{7,6},{8,9},{9,8},{10,11... | collective-permute-start | bytes 2359304 | tf_op jit(solution)/shard_map/ppermute | solution.py:31
  67.8 6.0 %copy-start.10 = (f32[384,1024]{1,0:T(8,128)S(1)}, f32[384,1024]{1,0:T(8,128)}, u32[]{:S(2)}) copy-start(f32[384,1024]{1,0:T(8,128)} %get-tuple-element.81) | copy-start | bytes 4718596
  75.1 24.0 %collective-permute-start.7 = (bf16[384,1024]{1,0:T(8,128)(2,1)}, bf16[384,1024]{1,0:T(8,128)(2,1)}, u32[]{:S(2)}, u32[]{:S(2)}) collective-permute-start(bf16[384,1024]{1,0:T(8,128)(2,1)} %add_convert_fusion.5), channel_id=1, source_target_pairs={{0,2},{1,3},{2,4},{3,5},{8,10},{9,11},{10,12},{11,13},{16,18},{17,... | collective-permute-start | bytes 2359304 | tf_op jit(solution)/shard_map/ppermute | solution.py:26
  79.7 21.0 %collective-permute-start.8 = (bf16[384,1024]{1,0:T(8,128)(2,1)}, bf16[384,1024]{1,0:T(8,128)(2,1)}, u32[]{:S(2)}, u32[]{:S(2)}) collective-permute-start(bf16[384,1024]{1,0:T(8,128)(2,1)} %add_convert_fusion.5), channel_id=1, source_target_pairs={{6,4},{7,5},{4,2},{5,3},{14,12},{15,13},{12,10},{13,11},{22,20},{2... | collective-permute-start | bytes 2359304 | tf_op jit(solution)/shard_map/ppermute | solution.py:26
  81.2 26.1 %collective-permute-start.9 = (bf16[384,1024]{1,0:T(8,128)(2,1)}, bf16[384,1024]{1,0:T(8,128)(2,1)}, u32[]{:S(2)}, u32[]{:S(2)}) collective-permute-start(bf16[384,1024]{1,0:T(8,128)(2,1)} %shard_map.120), channel_id=1, source_target_pairs={{0,1},{1,0},{2,3},{3,2},{4,5},{5,4},{6,7},{7,6},{8,9},{9,8},{10,11... | collective-permute-start | bytes 2359304 | tf_op jit(solution)/shard_map/ppermute | solution.py:31
  86.8 3.7 %copy-start.9 = (f32[384,1024]{1,0:T(8,128)S(1)}, f32[384,1024]{1,0:T(8,128)}, u32[]{:S(2)}) copy-start(f32[384,1024]{1,0:T(8,128)} %get-tuple-element.86) | copy-start | bytes 4718596
  86.8 4.0 %copy-start.13 = (bf16[432,1024]{1,0:T(8,128)(2,1)}, bf16[432,1024]{1,0:T(8,128)(2,1)S(1)}, u32[]{:S(2)}) copy-start(bf16[432,1024]{1,0:T(8,128)(2,1)S(1)} %collective-permute-done.6) | copy-start | bytes 2654212
  91.8 38.1 %collective-permute-start.10 = (bf16[432,1024]{1,0:T(8,128)(2,1)}, bf16[432,1024]{1,0:T(8,128)(2,1)}, u32[]{:S(2)}, u32[]{:S(2)}) collective-permute-start(bf16[432,1024]{1,0:T(8,128)(2,1)} %pad_maximum_fusion.4), channel_id=1, source_target_pairs={{0,2},{1,3},{2,4},{3,5},{8,10},{9,11},{10,12},{11,13},{16,18},{17,... | collective-permute-start | bytes 2654216 | tf_op jit(solution)/shard_map/ppermute | solution.py:26
  96.6 33.3 %collective-permute-start.11 = (bf16[432,1024]{1,0:T(8,128)(2,1)}, bf16[432,1024]{1,0:T(8,128)(2,1)}, u32[]{:S(2)}, u32[]{:S(2)}) collective-permute-start(bf16[432,1024]{1,0:T(8,128)(2,1)} %pad_maximum_fusion.4), channel_id=1, source_target_pairs={{6,4},{7,5},{4,2},{5,3},{14,12},{15,13},{12,10},{13,11},{22,20},{2... | collective-permute-start | bytes 2654216 | tf_op jit(solution)/shard_map/ppermute | solution.py:26
  99.1 30.8 %collective-permute-start.12 = (bf16[384,1024]{1,0:T(8,128)(2,1)}, bf16[384,1024]{1,0:T(8,128)(2,1)}, u32[]{:S(2)}, u32[]{:S(2)}) collective-permute-start(bf16[384,1024]{1,0:T(8,128)(2,1)} %shard_map.122), channel_id=1, source_target_pairs={{0,1},{1,0},{2,3},{3,2},{4,5},{5,4},{6,7},{7,6},{8,9},{9,8},{10,11... | collective-permute-start | bytes 2359304 | tf_op jit(solution)/shard_map/ppermute | solution.py:31
  112.2 34.8 %collective-permute-start.13 = (bf16[384,1024]{1,0:T(8,128)(2,1)}, bf16[384,1024]{1,0:T(8,128)(2,1)}, u32[]{:S(2)}, u32[]{:S(2)}) collective-permute-start(bf16[384,1024]{1,0:T(8,128)(2,1)} %get-tuple-element.128), channel_id=1, source_target_pairs={{0,2},{1,3},{2,4},{3,5},{4,6},{5,7},{8,10},{9,11},{10,12},{11,13},... | collective-permute-start | bytes 2359304 | tf_op jit(solution)/shard_map/ppermute | solution.py:26
  122.6 7.3 %copy-start.2 = (f32[384,1024]{1,0:T(8,128)S(1)}, f32[384,1024]{1,0:T(8,128)}, u32[]{:S(2)}) copy-start(f32[384,1024]{1,0:T(8,128)} %get-tuple-element.106) | copy-start | bytes 4718596
  122.6 7.3 %copy-start.11 = (f32[384,1024]{1,0:T(8,128)S(1)}, f32[384,1024]{1,0:T(8,128)}, u32[]{:S(2)}) copy-start(f32[384,1024]{1,0:T(8,128)} %get-tuple-element.96) | copy-start | bytes 4718596
  128.6 22.7 %collective-permute-start.14 = (bf16[384,1024]{1,0:T(8,128)(2,1)}, bf16[384,1024]{1,0:T(8,128)(2,1)}, u32[]{:S(2)}, u32[]{:S(2)}) collective-permute-start(bf16[384,1024]{1,0:T(8,128)(2,1)} %get-tuple-element.127), channel_id=1, source_target_pairs={{6,4},{7,5},{4,2},{5,3},{2,0},{3,1},{14,12},{15,13},{12,10},{13,11... | collective-permute-start | bytes 2359304 | tf_op jit(solution)/shard_map/ppermute | solution.py:26
  130.0 2.5 %copy-start.6 = (f32[48,1024]{1,0:T(8,128)S(1)}, f32[48,1024]{1,0:T(8,128)}, u32[]{:S(2)}) copy-start(f32[48,1024]{1,0:T(8,128)} %copy-done.4) | copy-start | bytes 589828
  134.7 22.7 %collective-permute-start.15 = (bf16[432,1024]{1,0:T(8,128)(2,1)}, bf16[432,1024]{1,0:T(8,128)(2,1)}, u32[]{:S(2)}, u32[]{:S(2)}) collective-permute-start(bf16[432,1024]{1,0:T(8,128)(2,1)} %get-tuple-element.132), channel_id=1, source_target_pairs={{0,2},{1,3},{2,4},{3,5},{4,6},{5,7},{8,10},{9,11},{10,12},{11,13},... | collective-permute-start | bytes 2654216 | tf_op jit(solution)/shard_map/ppermute | solution.py:26
  140.1 28.1 %collective-permute-start.16 = (bf16[432,1024]{1,0:T(8,128)(2,1)S(1)}, bf16[432,1024]{1,0:T(8,128)(2,1)}, u32[]{:S(2)}, u32[]{:S(2)}) collective-permute-start(bf16[432,1024]{1,0:T(8,128)(2,1)S(1)} %get-tuple-element.131), channel_id=1, source_target_pairs={{6,4},{7,5},{4,2},{5,3},{2,0},{3,1},{14,12},{15,13},{12,10},{13,11... | collective-permute-start | bytes 2654216 | tf_op jit(solution)/shard_map/ppermute | solution.py:26
  141.4 5.4 %copy-start.7 = (bf16[768,1024]{1,0:T(8,128)(2,1)S(1)}, bf16[768,1024]{1,0:T(8,128)(2,1)}, u32[]{:S(2)}) copy-start(bf16[768,1024]{1,0:T(8,128)(2,1)} %param.15) | copy-start | bytes 4718596
  146.8 4.5 %copy-start = (f32[384,1024]{1,0:T(8,128)S(1)}, f32[384,1024]{1,0:T(8,128)}, u32[]{:S(2)}) copy-start(f32[384,1024]{1,0:T(8,128)} %get-tuple-element.104.refs_2_) | copy-start | bytes 4718596
  146.8 22.6 %collective-permute-start.17 = (bf16[6,64,1024]{2,1,0:T(8,128)(2,1)}, bf16[6,64,1024]{2,1,0:T(8,128)(2,1)}, u32[]{:S(2)}, u32[]{:S(2)}) collective-permute-start(bf16[6,64,1024]{2,1,0:T(8,128)(2,1)} %get-tuple-element.112), channel_id=1, source_target_pairs={{0,8},{8,0},{1,9},{9,1},{2,10},{10,2},{3,11},{11,3},{4,12},{12,4},... | collective-permute-start | bytes 2359304 | tf_op jit(solution)/shard_map/ppermute | solution.py:232
  147.0 37.2 %collective-permute-start.18 = (bf16[768,1024]{1,0:T(8,128)(2,1)}, bf16[768,1024]{1,0:T(8,128)(2,1)}, u32[]{:S(2)}, u32[]{:S(2)}) collective-permute-start(bf16[768,1024]{1,0:T(8,128)(2,1)} %shard_map.123), channel_id=1, source_target_pairs={{0,1},{1,0},{2,3},{3,2},{4,5},{5,4},{6,7},{7,6},{8,9},{9,8},{10,11... | collective-permute-start | bytes 4718600 | tf_op jit(solution)/shard_map/ppermute | solution.py:31
  169.4 2.1 %copy-start.8 = (f32[384,1024]{1,0:T(8,128)S(1)}, f32[384,1024]{1,0:T(8,128)}, u32[]{:S(2)}) copy-start(f32[384,1024]{1,0:T(8,128)} %get-tuple-element.117) | copy-start | bytes 4718596
  173.4 10.7 %dynamic-slice-start = ((f32[8192]{0:T(1024)}, s32[]{:T(128)}), f32[1024]{0:T(1024)S(1)}, s32[]{:S(2)}) async-start(f32[8192]{0:T(1024)} %param.16, s32[]{:T(128)} %select_n.101), calls=%async_computation | async-start | bytes 8704 | tf_op jit(solution)/shard_map/dynamic_slice | solution.py:274
  174.1 25.3 %copy-start.15 = (s32[6]{0:T(128)S(1)}, s32[6]{0:T(128)}, u32[]{:S(2)}) copy-start(s32[6]{0:T(128)} %param.19) | copy-start | bytes 76
  174.1 25.3 %copy-start.16 = (s32[6]{0:T(128)S(1)}, s32[6]{0:T(128)}, u32[]{:S(2)}) copy-start(s32[6]{0:T(128)} %param.18) | copy-start | bytes 76
  187.4 4.3 %collective-permute-start.20 = (f32[12,128]{1,0:T(8,128)S(1)}, f32[12,128]{1,0:T(8,128)S(1)}, u32[]{:S(2)}, u32[]{:S(2)}) collective-permute-start(f32[12,128]{1,0:T(8,128)S(1)} %reshape.63), channel_id=1, source_target_pairs={{0,2},{1,3},{2,0},{3,1},{4,6},{5,7},{6,4},{7,5},{8,10},{9,11},{10,... | collective-permute-start | bytes 18440 | tf_op jit(solution)/shard_map/ppermute | solution.py:31
  190.1 4.5 %collective-permute-start.21 = (f32[12,128]{1,0:T(8,128)S(1)}, f32[12,128]{1,0:T(8,128)S(1)}, u32[]{:S(2)}, u32[]{:S(2)}) collective-permute-start(f32[12,128]{1,0:T(8,128)S(1)} %reshape.63), channel_id=1, source_target_pairs={{0,3},{1,2},{2,1},{3,0},{4,7},{5,6},{6,5},{7,4},{8,11},{9,10},{10,... | collective-permute-start | bytes 18440 | tf_op jit(solution)/shard_map/ppermute | solution.py:31
  191.2 3.7 %collective-permute-start.19 = (f32[12,128]{1,0:T(8,128)S(1)}, f32[12,128]{1,0:T(8,128)S(1)}, u32[]{:S(2)}, u32[]{:S(2)}) collective-permute-start(f32[12,128]{1,0:T(8,128)S(1)} %reshape.63), channel_id=1, source_target_pairs={{0,1},{1,0},{2,3},{3,2},{4,5},{5,4},{6,7},{7,6},{8,9},{9,8},{10,11... | collective-permute-start | bytes 18440 | tf_op jit(solution)/shard_map/ppermute | solution.py:31
  194.8 4.5 %collective-permute-start.22 = (f32[12,128]{1,0:T(8,128)S(1)}, f32[12,128]{1,0:T(8,128)S(1)}, u32[]{:S(2)}, u32[]{:S(2)}) collective-permute-start(f32[12,128]{1,0:T(8,128)S(1)} %add_add_fusion), channel_id=1, source_target_pairs={{0,4},{1,5},{2,6},{3,7},{4,0},{5,1},{6,2},{7,3},{8,12},{9,13},{10,... | collective-permute-start | bytes 18440 | tf_op jit(solution)/shard_map/ppermute | solution.py:31

commit v5 on v3

--- a/solution.py
+++ b/solution.py
@@ -31,20 +31,23 @@
     return lax.ppermute(value, "tensor", [(t, t ^ bit) for t in range(size)])
 
 
-def product_kernel(count, further, index_ref, rows_ref, weights_ref, *refs):
-    result = jnp.dot(rows_ref[...], weights_ref[...], preferred_element_type=f32)
-    size = result.shape[0] // count
-    for n, ref in enumerate(refs[-count:]):
-        ref[:size] = result[n * size : (n + 1) * size].astype(ref.dtype)
+def product_kernel(inputs, count, further, index_ref, weights_ref, *refs):
+    outs = refs[-count:]
+    for n, rows_ref in enumerate(refs[:inputs]):
+        result = jnp.dot(rows_ref[...], weights_ref[...], preferred_element_type=f32)
+        size = result.shape[0]
+        at = 0 if count == inputs else n * size
+        ref = outs[n if count == inputs else 0]
+        ref[at : at + size] = result.astype(ref.dtype)
         if further:
-            ref[size:] = refs[0][...].astype(ref.dtype)
+            ref[size:] = refs[inputs][...].astype(ref.dtype)
 
 
 def product(hidden, weights, tensor_index, turn, own, kind, width, earlier, piece, count, further=None):
-    rows, depth = hidden.shape
+    inputs = hidden if piece is None else hidden[piece : piece + 1]
+    rows, depth = inputs[0].shape
     steps = width // TILE
-    rows = rows if piece is None else rows // PIECES
-    size = rows // count
+    size = rows * len(inputs) // count
     more = 0 if further is None else further.shape[0]
 
     def block(j, index):
@@ -55,14 +58,14 @@
         return (goal * PAIR + (y if own else 1 - y)) * steps + j
 
     return pl.pallas_call(
-        lambda *refs: product_kernel(count, more, *refs),
+        lambda *refs: product_kernel(len(inputs), count, more, *refs),
         grid_spec=pltpu.PrefetchScalarGridSpec(
             num_scalar_prefetch=1,
             grid=(steps,),
             in_specs=[
-                pl.BlockSpec((rows, depth), lambda j, index: (piece or 0, 0)),
                 pl.BlockSpec((depth, TILE), lambda j, index: (0, block(j, index))),
             ]
+            + [pl.BlockSpec((rows, depth), lambda j, index: (0, 0))] * len(inputs)
             + [pl.BlockSpec((more, TILE), lambda j, index: (0, j))] * (more > 0)
             + [ANYWHERE] * len(earlier),
             out_specs=[pl.BlockSpec((size + more, TILE), lambda j, index: (0, j))] * count,
@@ -70,24 +73,34 @@
         out_shape=[pltpu.HBM((size + more, width), kind)] * count,
         compiler_params=pltpu.CompilerParams(vmem_limit_bytes=40 * 1024 * 1024),
         cost_estimate=NO_COST,
-    )(tensor_index.reshape(1), hidden, weights, *([further] if more else []), *earlier)
-
-
-def pick_kernel(ids_ref, *refs):
-    refs[-1][...] = refs[0][...]
+    )(tensor_index.reshape(1), weights, *inputs, *([further] if more else []), *earlier)
+
+
+def pick_kernel(ids_ref, factors_ref, *refs):
+    out_ref, semaphores = refs[-2:]
+    copies = [
+        pltpu.make_async_copy(factors_ref.at[ids_ref[n]], out_ref.at[n], semaphores.at[n])
+        for n in range(out_ref.shape[0])
+    ]
+    for copy in copies:
+        copy.start()
+    for copy in copies:
+        copy.wait()
 
 
 def pick(ids, factors, earlier=()):
-    block = (1,) + factors.shape[1:]
+    shape = ids.shape + factors.shape[1:]
     return pl.pallas_call(
         pick_kernel,
         grid_spec=pltpu.PrefetchScalarGridSpec(
             num_scalar_prefetch=1,
-            grid=ids.shape,
-            in_specs=[pl.BlockSpec(block, lambda n, ids: (ids[n], 0, 0))] + [ANYWHERE] * len(earlier),
-            out_specs=pl.BlockSpec(block, lambda n, ids: (n, 0, 0)),
+            grid=(1,),
+            in_specs=[pl.BlockSpec(memory_space=pltpu.HBM)] + [ANYWHERE] * len(earlier),
+            out_specs=pl.BlockSpec(shape, lambda i, ids: (0, 0, 0)),
+            scratch_shapes=[pltpu.SemaphoreType.DMA(ids.shape)],
         ),
-        out_shape=pltpu.HBM(ids.shape + factors.shape[1:], factors.dtype),
+        out_shape=pltpu.HBM(shape, factors.dtype),
+        compiler_params=pltpu.CompilerParams(vmem_limit_bytes=60 * 1024 * 1024),
         cost_estimate=NO_COST,
     )(ids, factors, *earlier)
 
@@ -122,13 +135,13 @@
     arrived, mine, first, second, third = {}, {}, {}, {}, {}
     add = lambda *terms: sum(t.astype(f32) for t in terms)
     narrow = lambda *terms: add(*terms).astype(bf16)
-    size = hidden.shape[0] // PIECES
+    size = hidden[0].shape[0]
 
     def products(k, own, piece, count, further):
         kind = f32 if own else bf16
         out = then(
-            lambda h, *more: product(h, weights, tensor_index, k, own, kind, width, (), piece, count, *more),
-            hidden,
+            lambda w, *more: product(hidden, w, tensor_index, k, own, kind, width, (), piece, count, *more),
+            weights,
             *further,
         )
         for p, value in enumerate(out) if piece is None else [(piece, out[0])]:
@@ -163,7 +176,7 @@
         third[p] = (along_line(sent(up, further), UP), along_line(sent(down, further), DOWN))
 
     wanted, low_rank_of = low_rank_terms(hidden)
-    hidden = lax.optimization_barrier((wanted, hidden))[1]
+    hidden[0] = lax.optimization_barrier((wanted, hidden[0]))[1]
     theirs(0, piece=0)
     low_rank, second_factors = low_rank_of()
     low_rank = low_rank.reshape(-1, width)
@@ -193,7 +206,7 @@
     low_rank = jnp.where(z == 0, down[size:], jnp.where(last_z, up[size:], low_rank))
     moved = jnp.concatenate([settled, add(up[:size], down[:size])], 0)
     base_part = own_part + moved
-    return base_part, low_rank.reshape(hidden.shape[0], -1), second_factors
+    return base_part, low_rank.reshape(PIECES * size, -1), second_factors
 
 
 def shards(
@@ -245,13 +258,17 @@
 
                 first_factors = fetched(wanted_first, first_factors)
                 second_factors = fetched(wanted_second, second_factors)
-            product = jnp.einsum(
-                "bcj,bej->bce",
-                rows.reshape(blocks, BLOCK, hidden_width),
-                first_factors,
-                preferred_element_type=f32,
-            ).reshape(rows_local, -1)
-            return product, second_factors
+            each = blocks // len(rows)
+            product = [
+                jnp.einsum(
+                    "bcj,bej->bce",
+                    part.reshape(each, BLOCK, hidden_width),
+                    first_factors[n * each : (n + 1) * each],
+                    preferred_element_type=f32,
+                ).reshape(each * BLOCK, -1)
+                for n, part in enumerate(rows)
+            ]
+            return jnp.concatenate(product, 0), second_factors
 
         return wanted_first, terms
 
@@ -263,16 +280,22 @@
             preferred_element_type=f32,
         ).reshape(rows_local, slice_width).astype(bf16)
 
-    hidden = (
-        jax.nn.silu(gate_preactivation.astype(f32)) * up_preactivation.astype(f32)
-    ).astype(bf16)
+    def hidden_of(gate, up):
+        return (jax.nn.silu(gate.astype(f32)) * up.astype(f32)).astype(bf16)
+
     if on_grid:
+        half = rows_local // PIECES
+        hidden = [
+            hidden_of(gate_preactivation[n * half : (n + 1) * half], up_preactivation[n * half : (n + 1) * half])
+            for n in range(PIECES)
+        ]
         base_part, low_rank, second_factors = grid_sums(
             hidden, base_down_matrix, tensor_index, slice_width, low_rank_terms
         )
         delta = adapter_delta(low_rank, second_factors)
     else:
-        low_rank, second_factors = low_rank_terms(hidden)[1]()
+        hidden = hidden_of(gate_preactivation, up_preactivation)
+        low_rank, second_factors = low_rank_terms([hidden])[1]()
         delta = adapter_delta(lax.psum(low_rank, "tensor"), second_factors)
         base_part = lax.psum_scatter(
             jnp.dot(hidden, base_down_matrix, preferred_element_type=f32),

time: 180 us -> 177 us (0.983)
  Pallas kernels: 72.9 us -> 65.1 us
  waiting for transfers between devices: 22.2 us -> 26.8 us
    pallas_call x4, Pallas kernels: 19.3 us -> 12 us  [pick(): pl.pallas_call(pick_kernel, grid_spec=pltpu.PrefetchScalarGridSpec(num_sc...]
    ppermute x10, waiting for transfers between devices: 18.6 us -> 21.2 us  [across(): return lax.ppermute(value, 'tensor', [(t, t ^ bit) for t in range(size)])]
    select_n x0 -> x1, other arithmetic: none -> 1.96 us  [fetched(): return jnp.where(take, came, kept)]
    ppermute x10, waiting for transfers between devices: 3.69 us -> 5.56 us  [along_line(): return lax.ppermute(value, 'tensor', pairs)]
  transfers between devices with their start and end apart: 22 -> 22, of which waited for: 6 -> 9; matrix products, arithmetic and copies ran while one was open for 15% -> 15% of each run, Pallas kernels for 38% -> 35%
where the time goes in v5:
time: 177 us; the launch traced here: 176 us
  Pallas kernels  65.1 us (37%)
  starting transfers between devices  48.5 us (27%)
  other arithmetic  27.6 us (16%)
  waiting for transfers between devices  26.8 us (15%)
  local copies, waits for them, and re-layouts  4.03 us (2%)
  matrix products  3.06 us (2%)
    pallas_call x11, Pallas kernels, product(): pl.pallas_call(lambda *refs: product_kernel(len(inputs), count, more, *re...  53.1 us
    ppermute x10, starting transfers between devices, along_line(): return lax.ppermute(value, 'tensor', pairs)  31.8 us
    ppermute x10, waiting for transfers between devices, across(): return lax.ppermute(value, 'tensor', [(t, t ^ bit) for t in range(size)])  21.2 us
    ppermute x10, starting transfers between devices, across(): return lax.ppermute(value, 'tensor', [(t, t ^ bit) for t in range(size)])  16.1 us
    pallas_call x4, Pallas kernels, pick(): pl.pallas_call(pick_kernel, grid_spec=pltpu.PrefetchScalarGridSpec(num_sc...  12 us
    convert_element_type x7, other arithmetic, grid_sums(): narrow = lambda *terms: add(*terms).astype(bf16)  10.6 us
    ppermute x10, waiting for transfers between devices, along_line(): return lax.ppermute(value, 'tensor', pairs)  5.56 us
    add x3, other arithmetic, grid_sums(): add = lambda *terms: sum((t.astype(f32) for t in terms))  5.09 us
  transfers between devices with their start and end apart: 22, of which 9 were waited for; matrix products, arithmetic and copies ran while one was open for 15% of the time, Pallas kernels for 35%

profile of v5, /device:TPU:0, one launch (start us, length us, event | category | flops | bytes accessed | tf_op | source)
XLA Modules:
  0.0 176.3 jit_solution(5116324388676542155)
XLA Ops:
  0.7 0.7 reshape.75
  1.5 0.6 fusion.29
  2.1 3.2 %shard_map.113 = bf16[6,64,1792]{2,1,0:T(8,128)(2,1)} custom-call(s32[6]{0:T(128)} %get-tuple-element.108.ids_ref, bf16[32,64,1792]{2,1,0:T(8,128)(2,1)} %bitcast.31), custom_call_target="tpu_custom_call" | custom-call | tf_op jit(solution)/shard_map/pallas_call | solution.py:93
  5.3 0.5 collective-permute-start
  5.9 3.4 %fusion.9 = (bf16[384,1792]{1,0:T(8,128)(2,1)S(1)}, bf16[384,1792]{1,0:T(8,128)(2,1)S(1)}) fusion(bf16[768,1792]{1,0:T(8,128)(2,1)} %param.11, bf16[768,1792]{1,0:T(8,128)(2,1)} %param.10), kind=kLoop, calls=%fused_computation.18 | loop fusion | flops 11010048 | bytes 8257536 | tf_op jit(solution)/shard_map/convert_element_type | solution.py:284
  9.3 4.1 %shard_map.114 = bf16[384,1024]{1,0:T(8,128)(2,1)} custom-call(s32[1]{0:T(128)} %bitcast.refs_0_, bf16[1792,8192]{1,0:T(8,128)(2,1)} %refs_1_.11, bf16[384,1792]{1,0:T(8,128)(2,1)S(1)} %get-tuple-element.48.refs_2_), custom_call_target="tpu_custom_call" | custom-call | tf_op jit(solution)/shard_map/pallas_call | solution.py:60
  13.4 2.5 %collective-permute-start.1 = (bf16[384,1024]{1,0:T(8,128)(2,1)}, bf16[384,1024]{1,0:T(8,128)(2,1)}, u32[]{:S(2)}, u32[]{:S(2)}) collective-permute-start(bf16[384,1024]{1,0:T(8,128)(2,1)} %shard_map.114), channel_id=1, source_target_pairs={{0,1},{1,0},{2,3},{3,2},{4,5},{5,4},{6,7},{7,6},{8,9},{9,8},{10,11... | collective-permute-start | bytes 2359304 | tf_op jit(solution)/shard_map/ppermute | solution.py:31
  15.9 3.2 %shard_map.115 = bf16[6,64,1792]{2,1,0:T(8,128)(2,1)} custom-call(s32[6]{0:T(128)} %get-tuple-element.107.ids_ref, bf16[32,64,1792]{2,1,0:T(8,128)(2,1)} %bitcast.32), custom_call_target="tpu_custom_call" | custom-call | tf_op jit(solution)/shard_map/pallas_call | solution.py:93
  19.2 2.0 %broadcast_select_fusion = bf16[6,64,1792]{2,1,0:T(8,128)(2,1)S(1)} fusion(bf16[6,64,1792]{2,1,0:T(8,128)(2,1)} %collective-permute-done, bf16[6,64,1792]{2,1,0:T(8,128)(2,1)} %shard_map.115, pred[6]{0:T(512)(128)(4,1)S(1)} %fusion.27), kind=kLoop, calls=%fused_computation.33 | loop fusion | flops 688128 | bytes 4128774 | tf_op jit(solution)/shard_map/jit(_where)/select_n | solution.py:257
  21.1 0.6 convolution_bitcast_fusion
  21.7 0.6 convolution_bitcast_fusion.1
  22.7 4.1 %shard_map.116 = bf16[432,1024]{1,0:T(8,128)(2,1)} custom-call(s32[1]{0:T(128)} %bitcast.refs_0_, bf16[1792,8192]{1,0:T(8,128)(2,1)} %refs_1_.11, bf16[384,1792]{1,0:T(8,128)(2,1)S(1)} %get-tuple-element.97.refs_2_.refs_3_, f32[48,1024]{1,0:T(8,128)S(1)} %reshape.80.refs_3_), custom_call_target="tpu_custom_call" | custom-call | tf_op jit(solution)/shard_map/pallas_call | solution.py:60
  26.8 5.6 %shard_map.117 = (f32[384,1024]{1,0:T(8,128)}, f32[384,1024]{1,0:T(8,128)}) custom-call(s32[1]{0:T(128)} %bitcast.refs_0_, bf16[1792,8192]{1,0:T(8,128)(2,1)} %refs_1_.11, bf16[384,1792]{1,0:T(8,128)(2,1)S(1)} %get-tuple-element.48.refs_2_, bf16[384,1792]{1,0:T(8,128)(2,1)S(1)} %get-tuple-element.97.refs_2_.refs_3_), custom_call_target="tpu_custom_call" | custom-call | tf_op jit(solution)/shard_map/pallas_call | solution.py:60
  32.4 4.2 %shard_map.118 = bf16[384,1024]{1,0:T(8,128)(2,1)} custom-call(s32[1]{0:T(128)} %bitcast.refs_0_, bf16[1792,8192]{1,0:T(8,128)(2,1)} %refs_1_.11, bf16[384,1792]{1,0:T(8,128)(2,1)S(1)} %get-tuple-element.48.refs_2_), custom_call_target="tpu_custom_call" | custom-call | tf_op jit(solution)/shard_map/pallas_call | solution.py:60
  36.6 2.0 %collective-permute-start.3 = (bf16[384,1024]{1,0:T(8,128)(2,1)}, bf16[384,1024]{1,0:T(8,128)(2,1)S(1)}, u32[]{:S(2)}, u32[]{:S(2)}) collective-permute-start(bf16[384,1024]{1,0:T(8,128)(2,1)} %shard_map.118), channel_id=1, source_target_pairs={{0,1},{1,0},{2,3},{3,2},{4,5},{5,4},{6,7},{7,6},{8,9},{9,8},{10,11... | collective-permute-start | bytes 2359304 | tf_op jit(solution)/shard_map/ppermute | solution.py:31
  38.6 1.4 add_convert_fusion.7
  40.0 3.5 %collective-permute-start.4 = (bf16[384,1024]{1,0:T(8,128)(2,1)S(1)}, bf16[384,1024]{1,0:T(8,128)(2,1)S(1)}, u32[]{:S(2)}, u32[]{:S(2)}) collective-permute-start(bf16[384,1024]{1,0:T(8,128)(2,1)S(1)} %add_convert_fusion.7), channel_id=1, source_target_pairs={{0,2},{1,3},{6,4},{7,5},{8,10},{9,11},{14,12},{15,13},{16,18},{17,... | collective-permute-start | bytes 2359304 | tf_op jit(solution)/shard_map/ppermute | solution.py:26
  43.5 5.7 %shard_map.119 = (f32[384,1024]{1,0:T(8,128)}, f32[384,1024]{1,0:T(8,128)}) custom-call(s32[1]{0:T(128)} %bitcast.refs_0_, bf16[1792,8192]{1,0:T(8,128)(2,1)} %refs_1_.11, bf16[384,1792]{1,0:T(8,128)(2,1)S(1)} %get-tuple-element.48.refs_2_, bf16[384,1792]{1,0:T(8,128)(2,1)S(1)} %get-tuple-element.97.refs_2_.refs_3_), custom_call_target="tpu_custom_call" | custom-call | tf_op jit(solution)/shard_map/pallas_call | solution.py:60
  49.2 4.1 %shard_map.120 = bf16[384,1024]{1,0:T(8,128)(2,1)} custom-call(s32[1]{0:T(128)} %bitcast.refs_0_, bf16[1792,8192]{1,0:T(8,128)(2,1)} %refs_1_.11, bf16[384,1792]{1,0:T(8,128)(2,1)S(1)} %get-tuple-element.97.refs_2_.refs_3_), custom_call_target="tpu_custom_call" | custom-call | tf_op jit(solution)/shard_map/pallas_call | solution.py:60
  53.5 1.8 %copy-done.3 = f32[384,1024]{1,0:T(8,128)S(1)} copy-done((f32[384,1024]{1,0:T(8,128)S(1)}, f32[384,1024]{1,0:T(8,128)}, u32[]{:S(2)}) %copy-start.3) | copy-done | bytes 1572888
  55.7 3.0 %collective-permute-start.6 = (bf16[432,1024]{1,0:T(8,128)(2,1)S(1)}, bf16[432,1024]{1,0:T(8,128)(2,1)S(1)}, u32[]{:S(2)}, u32[]{:S(2)}) collective-permute-start(bf16[432,1024]{1,0:T(8,128)(2,1)S(1)} %pad_maximum_fusion.2), channel_id=1, source_target_pairs={{0,2},{1,3},{6,4},{7,5},{8,10},{9,11},{14,12},{15,13},{16,18},{17,... | collective-permute-start | bytes 2654216 | tf_op jit(solution)/shard_map/ppermute | solution.py:26
  58.7 1.6 collective-permute-start.5
  60.3 4.0 %shard_map.121 = bf16[384,1024]{1,0:T(8,128)(2,1)} custom-call(s32[1]{0:T(128)} %bitcast.refs_0_, bf16[1792,8192]{1,0:T(8,128)(2,1)} %refs_1_.11, bf16[384,1792]{1,0:T(8,128)(2,1)S(1)} %get-tuple-element.48.refs_2_), custom_call_target="tpu_custom_call" | custom-call | tf_op jit(solution)/shard_map/pallas_call | solution.py:60
  64.3 5.7 %shard_map.122 = (f32[384,1024]{1,0:T(8,128)}, f32[384,1024]{1,0:T(8,128)}) custom-call(s32[1]{0:T(128)} %bitcast.refs_0_, bf16[1792,8192]{1,0:T(8,128)(2,1)} %refs_1_.11, bf16[384,1792]{1,0:T(8,128)(2,1)S(1)} %get-tuple-element.48.refs_2_, bf16[384,1792]{1,0:T(8,128)(2,1)S(1)} %get-tuple-element.97.refs_2_.refs_3_), custom_call_target="tpu_custom_call" | custom-call | tf_op jit(solution)/shard_map/pallas_call | solution.py:60
  70.3 1.3 add_convert_fusion.5
  71.6 4.8 %collective-permute-start.7 = (bf16[384,1024]{1,0:T(8,128)(2,1)}, bf16[384,1024]{1,0:T(8,128)(2,1)}, u32[]{:S(2)}, u32[]{:S(2)}) collective-permute-start(bf16[384,1024]{1,0:T(8,128)(2,1)} %add_convert_fusion.5), channel_id=1, source_target_pairs={{0,2},{1,3},{2,4},{3,5},{8,10},{9,11},{10,12},{11,13},{16,18},{17,... | collective-permute-start | bytes 2359304 | tf_op jit(solution)/shard_map/ppermute | solution.py:26
  76.4 1.6 collective-permute-start.8
  78.0 1.5 collective-permute-start.9
  79.5 4.1 %shard_map.123 = bf16[384,1024]{1,0:T(8,128)(2,1)} custom-call(s32[1]{0:T(128)} %bitcast.refs_0_, bf16[1792,8192]{1,0:T(8,128)(2,1)} %refs_1_.11, bf16[384,1792]{1,0:T(8,128)(2,1)S(1)} %get-tuple-element.97.refs_2_.refs_3_), custom_call_target="tpu_custom_call" | custom-call | tf_op jit(solution)/shard_map/pallas_call | solution.py:60
  83.7 3.5 %collective-permute-done.5 = bf16[384,1024]{1,0:T(8,128)(2,1)S(1)} collective-permute-done((bf16[384,1024]{1,0:T(8,128)(2,1)S(1)}, bf16[384,1024]{1,0:T(8,128)(2,1)S(1)}, u32[]{:S(2)}, u32[]{:S(2)}) %collective-permute-start.5) | collective-permute-done | bytes 786464 | tf_op jit(solution)/shard_map/ppermute | solution.py:31
  87.2 0.4 add_convert_fusion.4
  87.6 1.0 pad_maximum_fusion.3
  88.6 4.9 %collective-permute-start.10 = (bf16[432,1024]{1,0:T(8,128)(2,1)}, bf16[432,1024]{1,0:T(8,128)(2,1)}, u32[]{:S(2)}, u32[]{:S(2)}) collective-permute-start(bf16[432,1024]{1,0:T(8,128)(2,1)} %pad_maximum_fusion.3), channel_id=1, source_target_pairs={{0,2},{1,3},{2,4},{3,5},{8,10},{9,11},{10,12},{11,13},{16,18},{17,... | collective-permute-start | bytes 2654216 | tf_op jit(solution)/shard_map/ppermute | solution.py:26
  93.5 1.6 collective-permute-start.11
  95.1 2.2 %collective-permute-done.7 = bf16[384,1024]{1,0:T(8,128)(2,1)} collective-permute-done((bf16[384,1024]{1,0:T(8,128)(2,1)}, bf16[384,1024]{1,0:T(8,128)(2,1)}, u32[]{:S(2)}, u32[]{:S(2)}) %collective-permute-start.7) | collective-permute-done | bytes 786464 | tf_op jit(solution)/shard_map/ppermute | solution.py:26
  97.4 0.4 collective-permute-start.12
  97.8 5.6 %shard_map.124 = bf16[768,1024]{1,0:T(8,128)(2,1)} custom-call(s32[1]{0:T(128)} %bitcast.refs_0_, bf16[1792,8192]{1,0:T(8,128)(2,1)} %refs_1_.11, bf16[384,1792]{1,0:T(8,128)(2,1)S(1)} %get-tuple-element.48.refs_2_, bf16[384,1792]{1,0:T(8,128)(2,1)S(1)} %get-tuple-element.97.refs_2_.refs_3_), custom_call_target="tpu_custom_call" | custom-call | tf_op jit(solution)/shard_map/pallas_call | solution.py:60
  103.4 6.0 %shard_map.125 = f32[768,1024]{1,0:T(8,128)} custom-call(s32[1]{0:T(128)} %bitcast.refs_0_, bf16[1792,8192]{1,0:T(8,128)(2,1)} %refs_1_.11, bf16[384,1792]{1,0:T(8,128)(2,1)S(1)} %get-tuple-element.48.refs_2_, bf16[384,1792]{1,0:T(8,128)(2,1)S(1)} %get-tuple-element.97.refs_2_.refs_3_), custom_call_target="tpu_custom_call" | custom-call | tf_op jit(solution)/shard_map/pallas_call | solution.py:60
  109.4 1.6 collective-permute-start.15
  111.0 3.7 %add_convert_fusion.1 = (bf16[384,1024]{1,0:T(8,128)(2,1)S(1)}, bf16[384,1024]{1,0:T(8,128)(2,1)}) fusion(bf16[384,1024]{1,0:T(8,128)(2,1)} %collective-permute-done.8, f32[384,1024]{1,0:T(8,128)S(1)} %copy-done.6, bf16[384,1024]{1,0:T(8,128)(2,1)} %collective-permute-done.1, f32[384,1024]{1,0:T(8,128)S(1)} %copy-done.13, ...), kind=kLoop, calls=%fused_computation.24 | loop fusion | flops 4325376 | bytes 7864321 | tf_op jit(solution)/shard_map/convert_element_type | solution.py:137
  114.8 4.4 %collective-permute-start.13 = (bf16[384,1024]{1,0:T(8,128)(2,1)}, bf16[384,1024]{1,0:T(8,128)(2,1)S(1)}, u32[]{:S(2)}, u32[]{:S(2)}) collective-permute-start(bf16[384,1024]{1,0:T(8,128)(2,1)} %get-tuple-element.102), channel_id=1, source_target_pairs={{0,2},{1,3},{2,4},{3,5},{4,6},{5,7},{8,10},{9,11},{10,12},{11,13},... | collective-permute-start | bytes 2359304 | tf_op jit(solution)/shard_map/ppermute | solution.py:26
  119.2 1.3 collective-permute-start.14
  120.5 1.1 add_convert_fusion.8
  121.7 2.5 %add_convert_fusion = (bf16[384,1024]{1,0:T(8,128)(2,1)S(1)}, bf16[384,1024]{1,0:T(8,128)(2,1)S(1)}) fusion(f32[384,1024]{1,0:T(8,128)S(1)} %copy-done.4, bf16[384,1024]{1,0:T(8,128)(2,1)S(1)} %copy-done.2, f32[384,1024]{1,0:T(8,128)S(1)} %copy-done.12, bf16[384,1024]{1,0:T(8,128)(2,1)} %collective-permute-done.12, ...), kind=kLoop, calls=%fused_computation.22 | loop fusion | flops 4325376 | bytes 7864321 | tf_op jit(solution)/shard_map/convert_element_type | solution.py:137
  124.1 1.4 pad_maximum_fusion
  125.6 5.5 %collective-permute-start.16 = (bf16[432,1024]{1,0:T(8,128)(2,1)}, bf16[432,1024]{1,0:T(8,128)(2,1)}, u32[]{:S(2)}, u32[]{:S(2)}) collective-permute-start(bf16[432,1024]{1,0:T(8,128)(2,1)} %get-tuple-element.104), channel_id=1, source_target_pairs={{0,2},{1,3},{2,4},{3,5},{4,6},{5,7},{8,10},{9,11},{10,12},{11,13},... | collective-permute-start | bytes 2654216 | tf_op jit(solution)/shard_map/ppermute | solution.py:26
  131.1 1.3 collective-permute-start.17
  132.3 2.8 %shard_map.126 = bf16[6,64,1024]{2,1,0:T(8,128)(2,1)} custom-call(s32[6]{0:T(128)} %get-tuple-element.108.ids_ref, bf16[32,64,1024]{2,1,0:T(8,128)(2,1)} %factors_ref.3), custom_call_target="tpu_custom_call" | custom-call | tf_op jit(solution)/shard_map/pallas_call | solution.py:93
  135.1 2.8 %shard_map.127 = bf16[6,64,1024]{2,1,0:T(8,128)(2,1)} custom-call(s32[6]{0:T(128)} %get-tuple-element.107.ids_ref, bf16[32,64,1024]{2,1,0:T(8,128)(2,1)} %factors_ref.3), custom_call_target="tpu_custom_call" | custom-call | tf_op jit(solution)/shard_map/pallas_call | solution.py:93
  138.1 3.3 %collective-permute-done.14 = bf16[384,1024]{1,0:T(8,128)(2,1)S(1)} collective-permute-done((bf16[384,1024]{1,0:T(8,128)(2,1)S(1)}, bf16[384,1024]{1,0:T(8,128)(2,1)S(1)}, u32[]{:S(2)}, u32[]{:S(2)}) %collective-permute-start.14) | collective-permute-done | bytes 786464 | tf_op jit(solution)/shard_map/ppermute | solution.py:26
  141.3 1.4 convert_add_fusion.3
  142.7 11.7 %collective-permute-done.15 = bf16[768,1024]{1,0:T(8,128)(2,1)} collective-permute-done((bf16[768,1024]{1,0:T(8,128)(2,1)}, bf16[768,1024]{1,0:T(8,128)(2,1)}, u32[]{:S(2)}, u32[]{:S(2)}) %collective-permute-start.15) | collective-permute-done | bytes 1572896 | tf_op jit(solution)/shard_map/ppermute | solution.py:31
  154.5 1.9 %convert_add_fusion.1 = f32[768,1024]{1,0:T(8,128)S(1)} fusion(f32[768,1024]{1,0:T(8,128)S(1)} %copy-done, bf16[768,1024]{1,0:T(8,128)(2,1)} %collective-permute-done.15), kind=kLoop, calls=%fused_computation.9 | loop fusion | flops 1572864 | bytes 7864320 | tf_op jit(solution)/shard_map/add | solution.py:136
  156.5 1.0 select_select_fusion
  157.6 1.7 convert_add_fusion.2
  159.4 1.9 %convolution_convert_fusion = bf16[6,128,1024]{2,1,0:T(8,128)(2,1)S(1)} fusion(bf16[6,128,64]{2,1,0:T(8,128)(2,1)S(1)} %reshape_reshape.3, bf16[6,64,1024]{2,1,0:T(8,128)(2,1)} %collective-permute-done.18, bf16[6,64,1024]{2,1,0:T(8,128)(2,1)S(1)} %copy-done.8, pred[6]{0:T(512)(128)(4,1)S(1)} %fusion.27), kind=kOutput, calls=%fused_computation.20 | convolution fusion | flops 101842944 | bytes 3244038 | tf_op jit(solution)/shard_map/bcn,bnt->bct/dot_general | solution.py:276
  161.5 2.1 %multiply_reduce_fusion.1 = (f32[768]{0:T(1024)S(1)}, f32[768]{0:T(1024)S(1)}, bf16[768,1024]{1,0:T(8,128)(2,1)}) fusion(f32[1024]{0:T(1024)S(1)} %dynamic-slice-done, f32[768,1024]{1,0:T(8,128)S(1)} %convert_add_fusion.1, f32[384,1024]{1,0:T(8,128)S(1)} %convert_add_fusion.2, f32[384,1024]{1,0:T(8,128)S(1)} %copy-done.7, ...), kind=kLoop, calls=%fused_computation.8 | loop fusion | flops 8649216 | bytes 11020288 | tf_op jit(solution)/shard_map/reduce_sum | solution.py:311
  163.6 1.8 %collective-permute-start.19 = (f32[12,128]{1,0:T(8,128)S(1)}, f32[12,128]{1,0:T(8,128)S(1)}, u32[]{:S(2)}, u32[]{:S(2)}) collective-permute-start(f32[12,128]{1,0:T(8,128)S(1)} %reshape.81), channel_id=1, source_target_pairs={{0,1},{1,0},{2,3},{3,2},{4,5},{5,4},{6,7},{7,6},{8,9},{9,8},{10,11... | collective-permute-start | bytes 18440 | tf_op jit(solution)/shard_map/ppermute | solution.py:31
  165.4 1.9 %collective-permute-done.19 = f32[12,128]{1,0:T(8,128)S(1)} collective-permute-done((f32[12,128]{1,0:T(8,128)S(1)}, f32[12,128]{1,0:T(8,128)S(1)}, u32[]{:S(2)}, u32[]{:S(2)}) %collective-permute-start.19) | collective-permute-done | bytes 6176 | tf_op jit(solution)/shard_map/ppermute | solution.py:31
  167.4 1.8 %collective-permute-start.20 = (f32[12,128]{1,0:T(8,128)S(1)}, f32[12,128]{1,0:T(8,128)S(1)}, u32[]{:S(2)}, u32[]{:S(2)}) collective-permute-start(f32[12,128]{1,0:T(8,128)S(1)} %add.156), channel_id=1, source_target_pairs={{0,2},{1,3},{2,0},{3,1},{4,6},{5,7},{6,4},{7,5},{8,10},{9,11},{10,... | collective-permute-start | bytes 18440 | tf_op jit(solution)/shard_map/ppermute | solution.py:31
  169.1 1.9 %collective-permute-done.20 = f32[12,128]{1,0:T(8,128)S(1)} collective-permute-done((f32[12,128]{1,0:T(8,128)S(1)}, f32[12,128]{1,0:T(8,128)S(1)}, u32[]{:S(2)}, u32[]{:S(2)}) %collective-permute-start.20) | collective-permute-done | bytes 6176 | tf_op jit(solution)/shard_map/ppermute | solution.py:31
  171.0 2.8 %collective-permute-start.21 = (f32[12,128]{1,0:T(8,128)S(1)}, f32[12,128]{1,0:T(8,128)S(1)}, u32[]{:S(2)}, u32[]{:S(2)}) collective-permute-start(f32[12,128]{1,0:T(8,128)S(1)} %add.157), channel_id=1, source_target_pairs={{0,4},{1,5},{2,6},{3,7},{4,0},{5,1},{6,2},{7,3},{8,12},{9,13},{10,... | collective-permute-start | bytes 18440 | tf_op jit(solution)/shard_map/ppermute | solution.py:31
  173.9 1.7 collective-permute-done.21
  175.6 0.7 fusion.21
  (77 shorter events, 2.0 us)
Async XLA Ops:
  5.3 13.8 %collective-permute-start = (bf16[6,64,1792]{2,1,0:T(8,128)(2,1)}, bf16[6,64,1792]{2,1,0:T(8,128)(2,1)}, u32[]{:S(2)}, u32[]{:S(2)}) collective-permute-start(bf16[6,64,1792]{2,1,0:T(8,128)(2,1)} %shard_map.113), channel_id=1, source_target_pairs={{0,8},{8,0},{1,9},{9,1},{2,10},{10,2},{3,11},{11,3},{4,12},{12,4},... | collective-permute-start | bytes 4128776 | tf_op jit(solution)/shard_map/ppermute | solution.py:256
  13.4 25.3 %collective-permute-start.1 = (bf16[384,1024]{1,0:T(8,128)(2,1)}, bf16[384,1024]{1,0:T(8,128)(2,1)}, u32[]{:S(2)}, u32[]{:S(2)}) collective-permute-start(bf16[384,1024]{1,0:T(8,128)(2,1)} %shard_map.114), channel_id=1, source_target_pairs={{0,1},{1,0},{2,3},{3,2},{4,5},{5,4},{6,7},{7,6},{8,9},{9,8},{10,11... | collective-permute-start | bytes 2359304 | tf_op jit(solution)/shard_map/ppermute | solution.py:31
  26.8 26.7 %collective-permute-start.2 = (bf16[432,1024]{1,0:T(8,128)(2,1)}, bf16[432,1024]{1,0:T(8,128)(2,1)S(1)}, u32[]{:S(2)}, u32[]{:S(2)}) collective-permute-start(bf16[432,1024]{1,0:T(8,128)(2,1)} %shard_map.116), channel_id=1, source_target_pairs={{0,1},{1,0},{2,3},{3,2},{4,5},{5,4},{6,7},{7,6},{8,9},{9,8},{10,11... | collective-permute-start | bytes 2654216 | tf_op jit(solution)/shard_map/ppermute | solution.py:31
  32.4 6.2 %copy-start.5 = (f32[384,1024]{1,0:T(8,128)S(1)}, f32[384,1024]{1,0:T(8,128)}, u32[]{:S(2)}) copy-start(f32[384,1024]{1,0:T(8,128)} %get-tuple-element.82) | copy-start | bytes 4718596
  36.6 33.7 %collective-permute-start.3 = (bf16[384,1024]{1,0:T(8,128)(2,1)}, bf16[384,1024]{1,0:T(8,128)(2,1)S(1)}, u32[]{:S(2)}, u32[]{:S(2)}) collective-permute-start(bf16[384,1024]{1,0:T(8,128)(2,1)} %shard_map.118), channel_id=1, source_target_pairs={{0,1},{1,0},{2,3},{3,2},{4,5},{5,4},{6,7},{7,6},{8,9},{9,8},{10,11... | collective-permute-start | bytes 2359304 | tf_op jit(solution)/shard_map/ppermute | solution.py:31
  40.0 30.3 %collective-permute-start.4 = (bf16[384,1024]{1,0:T(8,128)(2,1)S(1)}, bf16[384,1024]{1,0:T(8,128)(2,1)S(1)}, u32[]{:S(2)}, u32[]{:S(2)}) collective-permute-start(bf16[384,1024]{1,0:T(8,128)(2,1)S(1)} %add_convert_fusion.7), channel_id=1, source_target_pairs={{0,2},{1,3},{6,4},{7,5},{8,10},{9,11},{14,12},{15,13},{16,18},{17,... | collective-permute-start | bytes 2359304 | tf_op jit(solution)/shard_map/ppermute | solution.py:26
  53.3 2.0 %copy-start.3 = (f32[384,1024]{1,0:T(8,128)S(1)}, f32[384,1024]{1,0:T(8,128)}, u32[]{:S(2)}) copy-start(f32[384,1024]{1,0:T(8,128)} %get-tuple-element.89) | copy-start | bytes 4718596
  53.5 34.1 %copy-start.14 = (bf16[432,1024]{1,0:T(8,128)(2,1)}, bf16[432,1024]{1,0:T(8,128)(2,1)S(1)}, u32[]{:S(2)}) copy-start(bf16[432,1024]{1,0:T(8,128)(2,1)S(1)} %collective-permute-done.2) | copy-start | bytes 2654212
  53.5 2.0 %copy-start.1 = (bf16[384,1024]{1,0:T(8,128)(2,1)}, bf16[384,1024]{1,0:T(8,128)(2,1)S(1)}, u32[]{:S(2)}) copy-start(bf16[384,1024]{1,0:T(8,128)(2,1)S(1)} %slice.93) | copy-start | bytes 2359300
  55.6 3.1 %copy-start.16 = (bf16[384,1024]{1,0:T(8,128)(2,1)S(1)}, bf16[384,1024]{1,0:T(8,128)(2,1)}, u32[]{:S(2)}) copy-start(bf16[384,1024]{1,0:T(8,128)(2,1)} %shard_map.120) | copy-start | bytes 2359300
  55.7 27.9 %collective-permute-start.6 = (bf16[432,1024]{1,0:T(8,128)(2,1)S(1)}, bf16[432,1024]{1,0:T(8,128)(2,1)S(1)}, u32[]{:S(2)}, u32[]{:S(2)}) collective-permute-start(bf16[432,1024]{1,0:T(8,128)(2,1)S(1)} %pad_maximum_fusion.2), channel_id=1, source_target_pairs={{0,2},{1,3},{6,4},{7,5},{8,10},{9,11},{14,12},{15,13},{16,18},{17,... | collective-permute-start | bytes 2654216 | tf_op jit(solution)/shard_map/ppermute | solution.py:26
  58.7 28.5 %collective-permute-start.5 = (bf16[384,1024]{1,0:T(8,128)(2,1)S(1)}, bf16[384,1024]{1,0:T(8,128)(2,1)S(1)}, u32[]{:S(2)}, u32[]{:S(2)}) collective-permute-start(bf16[384,1024]{1,0:T(8,128)(2,1)S(1)} %copy-done.16), channel_id=1, source_target_pairs={{0,1},{1,0},{2,3},{3,2},{4,5},{5,4},{6,7},{7,6},{8,9},{9,8},{10,11... | collective-permute-start | bytes 2359304 | tf_op jit(solution)/shard_map/ppermute | solution.py:31
  64.3 6.0 %copy-start.10 = (f32[384,1024]{1,0:T(8,128)S(1)}, f32[384,1024]{1,0:T(8,128)}, u32[]{:S(2)}) copy-start(f32[384,1024]{1,0:T(8,128)} %get-tuple-element.65) | copy-start | bytes 4718596
  71.6 25.7 %collective-permute-start.7 = (bf16[384,1024]{1,0:T(8,128)(2,1)}, bf16[384,1024]{1,0:T(8,128)(2,1)}, u32[]{:S(2)}, u32[]{:S(2)}) collective-permute-start(bf16[384,1024]{1,0:T(8,128)(2,1)} %add_convert_fusion.5), channel_id=1, source_target_pairs={{0,2},{1,3},{2,4},{3,5},{8,10},{9,11},{10,12},{11,13},{16,18},{17,... | collective-permute-start | bytes 2359304 | tf_op jit(solution)/shard_map/ppermute | solution.py:26
  76.4 33.0 %collective-permute-start.8 = (bf16[384,1024]{1,0:T(8,128)(2,1)}, bf16[384,1024]{1,0:T(8,128)(2,1)}, u32[]{:S(2)}, u32[]{:S(2)}) collective-permute-start(bf16[384,1024]{1,0:T(8,128)(2,1)} %add_convert_fusion.5), channel_id=1, source_target_pairs={{6,4},{7,5},{4,2},{5,3},{14,12},{15,13},{12,10},{13,11},{22,20},{2... | collective-permute-start | bytes 2359304 | tf_op jit(solution)/shard_map/ppermute | solution.py:26
  78.0 33.0 %collective-permute-start.9 = (bf16[384,1024]{1,0:T(8,128)(2,1)}, bf16[384,1024]{1,0:T(8,128)(2,1)}, u32[]{:S(2)}, u32[]{:S(2)}) collective-permute-start(bf16[384,1024]{1,0:T(8,128)(2,1)} %shard_map.121), channel_id=1, source_target_pairs={{0,1},{1,0},{2,3},{3,2},{4,5},{5,4},{6,7},{7,6},{8,9},{9,8},{10,11... | collective-permute-start | bytes 2359304 | tf_op jit(solution)/shard_map/ppermute | solution.py:31
  83.6 3.6 %copy-start.9 = (f32[384,1024]{1,0:T(8,128)S(1)}, f32[384,1024]{1,0:T(8,128)}, u32[]{:S(2)}) copy-start(f32[384,1024]{1,0:T(8,128)} %get-tuple-element.70) | copy-start | bytes 4718596
  83.6 4.0 %copy-start.15 = (bf16[432,1024]{1,0:T(8,128)(2,1)}, bf16[432,1024]{1,0:T(8,128)(2,1)S(1)}, u32[]{:S(2)}) copy-start(bf16[432,1024]{1,0:T(8,128)(2,1)S(1)} %collective-permute-done.6) | copy-start | bytes 2654212
  88.6 30.6 %collective-permute-start.10 = (bf16[432,1024]{1,0:T(8,128)(2,1)}, bf16[432,1024]{1,0:T(8,128)(2,1)}, u32[]{:S(2)}, u32[]{:S(2)}) collective-permute-start(bf16[432,1024]{1,0:T(8,128)(2,1)} %pad_maximum_fusion.3), channel_id=1, source_target_pairs={{0,2},{1,3},{2,4},{3,5},{8,10},{9,11},{10,12},{11,13},{16,18},{17,... | collective-permute-start | bytes 2654216 | tf_op jit(solution)/shard_map/ppermute | solution.py:26
  93.5 27.0 %collective-permute-start.11 = (bf16[432,1024]{1,0:T(8,128)(2,1)}, bf16[432,1024]{1,0:T(8,128)(2,1)}, u32[]{:S(2)}, u32[]{:S(2)}) collective-permute-start(bf16[432,1024]{1,0:T(8,128)(2,1)} %pad_maximum_fusion.3), channel_id=1, source_target_pairs={{6,4},{7,5},{4,2},{5,3},{14,12},{15,13},{12,10},{13,11},{22,20},{2... | collective-permute-start | bytes 2654216 | tf_op jit(solution)/shard_map/ppermute | solution.py:26
  97.4 24.3 %collective-permute-start.12 = (bf16[384,1024]{1,0:T(8,128)(2,1)}, bf16[384,1024]{1,0:T(8,128)(2,1)}, u32[]{:S(2)}, u32[]{:S(2)}) collective-permute-start(bf16[384,1024]{1,0:T(8,128)(2,1)} %shard_map.123), channel_id=1, source_target_pairs={{0,1},{1,0},{2,3},{3,2},{4,5},{5,4},{6,7},{7,6},{8,9},{9,8},{10,11... | collective-permute-start | bytes 2359304 | tf_op jit(solution)/shard_map/ppermute | solution.py:31
  103.3 7.7 %copy-start.6 = (f32[384,1024]{1,0:T(8,128)S(1)}, f32[384,1024]{1,0:T(8,128)}, u32[]{:S(2)}) copy-start(f32[384,1024]{1,0:T(8,128)} %get-tuple-element.82) | copy-start | bytes 4718596
  103.3 7.7 %copy-start.13 = (f32[384,1024]{1,0:T(8,128)S(1)}, f32[384,1024]{1,0:T(8,128)}, u32[]{:S(2)}) copy-start(f32[384,1024]{1,0:T(8,128)} %get-tuple-element.75) | copy-start | bytes 4718596
  109.4 12.3 %copy-start.2 = (bf16[384,1024]{1,0:T(8,128)(2,1)S(1)}, bf16[384,1024]{1,0:T(8,128)(2,1)}, u32[]{:S(2)}) copy-start(bf16[384,1024]{1,0:T(8,128)(2,1)} %copy-done.1) | copy-start | bytes 2359300
  109.4 45.1 %collective-permute-start.15 = (bf16[768,1024]{1,0:T(8,128)(2,1)}, bf16[768,1024]{1,0:T(8,128)(2,1)}, u32[]{:S(2)}, u32[]{:S(2)}) collective-permute-start(bf16[768,1024]{1,0:T(8,128)(2,1)} %shard_map.124), channel_id=1, source_target_pairs={{0,1},{1,0},{2,3},{3,2},{4,5},{5,4},{6,7},{7,6},{8,9},{9,8},{10,11... | collective-permute-start | bytes 4718600 | tf_op jit(solution)/shard_map/ppermute | solution.py:31
  111.0 10.6 %copy-start.4 = (f32[384,1024]{1,0:T(8,128)S(1)}, f32[384,1024]{1,0:T(8,128)}, u32[]{:S(2)}) copy-start(f32[384,1024]{1,0:T(8,128)} %get-tuple-element.89) | copy-start | bytes 4718596
  111.0 10.6 %copy-start.12 = (f32[384,1024]{1,0:T(8,128)S(1)}, f32[384,1024]{1,0:T(8,128)}, u32[]{:S(2)}) copy-start(f32[384,1024]{1,0:T(8,128)} %get-tuple-element.79) | copy-start | bytes 4718596
  114.8 23.2 %collective-permute-start.13 = (bf16[384,1024]{1,0:T(8,128)(2,1)}, bf16[384,1024]{1,0:T(8,128)(2,1)S(1)}, u32[]{:S(2)}, u32[]{:S(2)}) collective-permute-start(bf16[384,1024]{1,0:T(8,128)(2,1)} %get-tuple-element.102), channel_id=1, source_target_pairs={{0,2},{1,3},{2,4},{3,5},{4,6},{5,7},{8,10},{9,11},{10,12},{11,13},... | collective-permute-start | bytes 2359304 | tf_op jit(solution)/shard_map/ppermute | solution.py:26
  119.2 22.1 %collective-permute-start.14 = (bf16[384,1024]{1,0:T(8,128)(2,1)S(1)}, bf16[384,1024]{1,0:T(8,128)(2,1)S(1)}, u32[]{:S(2)}, u32[]{:S(2)}) collective-permute-start(bf16[384,1024]{1,0:T(8,128)(2,1)S(1)} %get-tuple-element.101), channel_id=1, source_target_pairs={{6,4},{7,5},{4,2},{5,3},{2,0},{3,1},{14,12},{15,13},{12,10},{13,11... | collective-permute-start | bytes 2359304 | tf_op jit(solution)/shard_map/ppermute | solution.py:26
  125.6 30.8 %collective-permute-start.16 = (bf16[432,1024]{1,0:T(8,128)(2,1)}, bf16[432,1024]{1,0:T(8,128)(2,1)}, u32[]{:S(2)}, u32[]{:S(2)}) collective-permute-start(bf16[432,1024]{1,0:T(8,128)(2,1)} %get-tuple-element.104), channel_id=1, source_target_pairs={{0,2},{1,3},{2,4},{3,5},{4,6},{5,7},{8,10},{9,11},{10,12},{11,13},... | collective-permute-start | bytes 2654216 | tf_op jit(solution)/shard_map/ppermute | solution.py:26
  131.1 25.4 %collective-permute-start.17 = (bf16[432,1024]{1,0:T(8,128)(2,1)}, bf16[432,1024]{1,0:T(8,128)(2,1)}, u32[]{:S(2)}, u32[]{:S(2)}) collective-permute-start(bf16[432,1024]{1,0:T(8,128)(2,1)} %get-tuple-element.103), channel_id=1, source_target_pairs={{6,4},{7,5},{4,2},{5,3},{2,0},{3,1},{14,12},{15,13},{12,10},{13,11... | collective-permute-start | bytes 2654216 | tf_op jit(solution)/shard_map/ppermute | solution.py:26
  138.0 16.5 %copy-start = (f32[768,1024]{1,0:T(8,128)S(1)}, f32[768,1024]{1,0:T(8,128)}, u32[]{:S(2)}) copy-start(f32[768,1024]{1,0:T(8,128)} %shard_map.125) | copy-start | bytes 9437188
  138.0 21.4 %collective-permute-start.18 = (bf16[6,64,1024]{2,1,0:T(8,128)(2,1)}, bf16[6,64,1024]{2,1,0:T(8,128)(2,1)}, u32[]{:S(2)}, u32[]{:S(2)}) collective-permute-start(bf16[6,64,1024]{2,1,0:T(8,128)(2,1)} %shard_map.126), channel_id=1, source_target_pairs={{0,8},{8,0},{1,9},{9,1},{2,10},{10,2},{3,11},{11,3},{4,12},{12,4},... | collective-permute-start | bytes 2359304 | tf_op jit(solution)/shard_map/ppermute | solution.py:256
  157.6 1.8 %copy-start.8 = (bf16[6,64,1024]{2,1,0:T(8,128)(2,1)S(1)}, bf16[6,64,1024]{2,1,0:T(8,128)(2,1)}, u32[]{:S(2)}) copy-start(bf16[6,64,1024]{2,1,0:T(8,128)(2,1)} %shard_map.127) | copy-start | bytes 2359300
  159.3 2.0 %copy-start.7 = (f32[384,1024]{1,0:T(8,128)S(1)}, f32[384,1024]{1,0:T(8,128)}, u32[]{:S(2)}) copy-start(f32[384,1024]{1,0:T(8,128)} %convert_add_fusion.3) | copy-start | bytes 4718596
  159.4 2.1 %copy-start.11 = (bf16[768,1024]{1,0:T(8,128)(2,1)S(1)}, bf16[768,1024]{1,0:T(8,128)(2,1)}, u32[]{:S(2)}) copy-start(bf16[768,1024]{1,0:T(8,128)(2,1)} %param.15) | copy-start | bytes 4718596
  159.4 2.1 %dynamic-slice-start = ((f32[8192]{0:T(1024)}, s32[]{:T(128)}), f32[1024]{0:T(1024)S(1)}, s32[]{:S(2)}) async-start(f32[8192]{0:T(1024)} %param.16, s32[]{:T(128)} %select_n.99), calls=%async_computation | async-start | bytes 8704 | tf_op jit(solution)/shard_map/dynamic_slice | solution.py:308
  161.5 14.1 %copy-start.17 = (s32[6]{0:T(128)S(1)}, s32[6]{0:T(128)}, u32[]{:S(2)}) copy-start(s32[6]{0:T(128)} %param.19) | copy-start | bytes 76
  161.5 14.1 %copy-start.18 = (s32[6]{0:T(128)S(1)}, s32[6]{0:T(128)}, u32[]{:S(2)}) copy-start(s32[6]{0:T(128)} %param.18) | copy-start | bytes 76
  163.6 3.7 %collective-permute-start.19 = (f32[12,128]{1,0:T(8,128)S(1)}, f32[12,128]{1,0:T(8,128)S(1)}, u32[]{:S(2)}, u32[]{:S(2)}) collective-permute-start(f32[12,128]{1,0:T(8,128)S(1)} %reshape.81), channel_id=1, source_target_pairs={{0,1},{1,0},{2,3},{3,2},{4,5},{5,4},{6,7},{7,6},{8,9},{9,8},{10,11... | collective-permute-start | bytes 18440 | tf_op jit(solution)/shard_map/ppermute | solution.py:31
  167.4 3.7 %collective-permute-start.20 = (f32[12,128]{1,0:T(8,128)S(1)}, f32[12,128]{1,0:T(8,128)S(1)}, u32[]{:S(2)}, u32[]{:S(2)}) collective-permute-start(f32[12,128]{1,0:T(8,128)S(1)} %add.156), channel_id=1, source_target_pairs={{0,2},{1,3},{2,0},{3,1},{4,6},{5,7},{6,4},{7,5},{8,10},{9,11},{10,... | collective-permute-start | bytes 18440 | tf_op jit(solution)/shard_map/ppermute | solution.py:31
  171.0 4.5 %collective-permute-start.21 = (f32[12,128]{1,0:T(8,128)S(1)}, f32[12,128]{1,0:T(8,128)S(1)}, u32[]{:S(2)}, u32[]{:S(2)}) collective-permute-start(f32[12,128]{1,0:T(8,128)S(1)} %add.157), channel_id=1, source_target_pairs={{0,4},{1,5},{2,6},{3,7},{4,0},{5,1},{6,2},{7,3},{8,12},{9,13},{10,... | collective-permute-start | bytes 18440 | tf_op jit(solution)/shard_map/ppermute | solution.py:31

commit v6 on v5

--- a/solution.py
+++ b/solution.py
@@ -77,15 +77,17 @@
 
 
 def pick_kernel(ids_ref, factors_ref, *refs):
-    out_ref, semaphores = refs[-2:]
-    copies = [
-        pltpu.make_async_copy(factors_ref.at[ids_ref[n]], out_ref.at[n], semaphores.at[n])
-        for n in range(out_ref.shape[0])
-    ]
-    for copy in copies:
-        copy.start()
-    for copy in copies:
-        copy.wait()
+    out_ref, held_ref, came, left = refs[-4:]
+    places = range(out_ref.shape[0])
+    into = [pltpu.make_async_copy(factors_ref.at[ids_ref[n]], held_ref.at[n], came.at[n]) for n in places]
+    out = [pltpu.make_async_copy(held_ref.at[n], out_ref.at[n], left.at[n]) for n in places]
+    for n in places:
+        into[n].start()
+    for n in places:
+        into[n].wait()
+        out[n].start()
+    for n in places:
+        out[n].wait()
 
 
 def pick(ids, factors, earlier=()):
@@ -96,8 +98,8 @@
             num_scalar_prefetch=1,
             grid=(1,),
             in_specs=[pl.BlockSpec(memory_space=pltpu.HBM)] + [ANYWHERE] * len(earlier),
-            out_specs=pl.BlockSpec(shape, lambda i, ids: (0, 0, 0)),
-            scratch_shapes=[pltpu.SemaphoreType.DMA(ids.shape)],
+            out_specs=pl.BlockSpec(memory_space=pltpu.HBM),
+            scratch_shapes=[pltpu.VMEM(shape, factors.dtype)] + [pltpu.SemaphoreType.DMA(ids.shape)] * 2,
         ),
         out_shape=pltpu.HBM(shape, factors.dtype),
         compiler_params=pltpu.CompilerParams(vmem_limit_bytes=60 * 1024 * 1024),
@@ -106,7 +108,7 @@
 
 
 def exchange_sum(value, wire):
-    for bit in (1, 2, 4):
+    for bit in (4, 2, 1):
         value = value + across(value.astype(wire), bit).astype(f32)
     return value
 

time: 177 us -> 177 us (level)
  waiting for transfers between devices: 26.8 us -> 28.6 us
  transfers between devices with their start and end apart: 22 -> 22, of which waited for: 9 -> 10; matrix products, arithmetic and copies ran while one was open for 15% -> 15% of each run, Pallas kernels for 35% -> 35%
where the time goes in v6:
time: 177 us; the launch traced here: 176 us
  Pallas kernels  64.2 us (36%)
  starting transfers between devices  48.5 us (27%)
  waiting for transfers between devices  28.6 us (16%)
  other arithmetic  27.6 us (16%)
  local copies, waits for them, and re-layouts  3.12 us (2%)
  matrix products  3.07 us (2%)
    pallas_call x11, Pallas kernels, product(): pl.pallas_call(lambda *refs: product_kernel(len(inputs), count, more, *re...  53.1 us
    ppermute x10, starting transfers between devices, along_line(): return lax.ppermute(value, 'tensor', pairs)  32.7 us
    ppermute x10, waiting for transfers between devices, across(): return lax.ppermute(value, 'tensor', [(t, t ^ bit) for t in range(size)])  22.5 us
    ppermute x10, starting transfers between devices, across(): return lax.ppermute(value, 'tensor', [(t, t ^ bit) for t in range(size)])  15.2 us
    pallas_call x4, Pallas kernels, pick(): pl.pallas_call(pick_kernel, grid_spec=pltpu.PrefetchScalarGridSpec(num_sc...  11.1 us
    convert_element_type x7, other arithmetic, grid_sums(): narrow = lambda *terms: add(*terms).astype(bf16)  10.6 us
    ppermute x10, waiting for transfers between devices, along_line(): return lax.ppermute(value, 'tensor', pairs)  6.1 us
    add x3, other arithmetic, grid_sums(): add = lambda *terms: sum((t.astype(f32) for t in terms))  5.09 us
  transfers between devices with their start and end apart: 22, of which 10 were waited for; matrix products, arithmetic and copies ran while one was open for 15% of the time, Pallas kernels for 35%

profile of v6, /device:TPU:0, one launch (start us, length us, event | category | flops | bytes accessed | tf_op | source)
XLA Modules:
  0.0 176.2 jit_solution(4140891329226189785)
XLA Ops:
  0.7 0.7 reshape.75
  1.5 0.6 fusion.29
  2.1 2.9 %shard_map.113 = bf16[6,64,1792]{2,1,0:T(8,128)(2,1)} custom-call(s32[6]{0:T(128)} %get-tuple-element.108.ids_ref, bf16[32,64,1792]{2,1,0:T(8,128)(2,1)} %bitcast.31), custom_call_target="tpu_custom_call" | custom-call | tf_op jit(solution)/shard_map/pallas_call | solution.py:95
  5.0 0.5 collective-permute-start
  5.5 3.4 %fusion.9 = (bf16[384,1792]{1,0:T(8,128)(2,1)S(1)}, bf16[384,1792]{1,0:T(8,128)(2,1)S(1)}) fusion(bf16[768,1792]{1,0:T(8,128)(2,1)} %param.11, bf16[768,1792]{1,0:T(8,128)(2,1)} %param.10), kind=kLoop, calls=%fused_computation.18 | loop fusion | flops 11010048 | bytes 8257536 | tf_op jit(solution)/shard_map/convert_element_type | solution.py:286
  9.0 4.1 %shard_map.114 = bf16[384,1024]{1,0:T(8,128)(2,1)} custom-call(s32[1]{0:T(128)} %bitcast.refs_0_, bf16[1792,8192]{1,0:T(8,128)(2,1)} %refs_1_.11, bf16[384,1792]{1,0:T(8,128)(2,1)S(1)} %get-tuple-element.48.refs_2_), custom_call_target="tpu_custom_call" | custom-call | tf_op jit(solution)/shard_map/pallas_call | solution.py:60
  13.0 2.5 %collective-permute-start.1 = (bf16[384,1024]{1,0:T(8,128)(2,1)}, bf16[384,1024]{1,0:T(8,128)(2,1)}, u32[]{:S(2)}, u32[]{:S(2)}) collective-permute-start(bf16[384,1024]{1,0:T(8,128)(2,1)} %shard_map.114), channel_id=1, source_target_pairs={{0,1},{1,0},{2,3},{3,2},{4,5},{5,4},{6,7},{7,6},{8,9},{9,8},{10,11... | collective-permute-start | bytes 2359304 | tf_op jit(solution)/shard_map/ppermute | solution.py:31
  15.6 2.9 %shard_map.115 = bf16[6,64,1792]{2,1,0:T(8,128)(2,1)} custom-call(s32[6]{0:T(128)} %get-tuple-element.107.ids_ref, bf16[32,64,1792]{2,1,0:T(8,128)(2,1)} %bitcast.32), custom_call_target="tpu_custom_call" | custom-call | tf_op jit(solution)/shard_map/pallas_call | solution.py:95
  18.5 2.0 %broadcast_select_fusion = bf16[6,64,1792]{2,1,0:T(8,128)(2,1)S(1)} fusion(bf16[6,64,1792]{2,1,0:T(8,128)(2,1)} %collective-permute-done, bf16[6,64,1792]{2,1,0:T(8,128)(2,1)} %shard_map.115, pred[6]{0:T(512)(128)(4,1)S(1)} %fusion.27), kind=kLoop, calls=%fused_computation.33 | loop fusion | flops 688128 | bytes 4128774 | tf_op jit(solution)/shard_map/jit(_where)/select_n | solution.py:259
  20.5 0.6 convolution_bitcast_fusion
  21.1 0.6 convolution_bitcast_fusion.1
  22.1 4.1 %shard_map.116 = bf16[432,1024]{1,0:T(8,128)(2,1)} custom-call(s32[1]{0:T(128)} %bitcast.refs_0_, bf16[1792,8192]{1,0:T(8,128)(2,1)} %refs_1_.11, bf16[384,1792]{1,0:T(8,128)(2,1)S(1)} %get-tuple-element.97.refs_2_.refs_3_, f32[48,1024]{1,0:T(8,128)S(1)} %reshape.80.refs_3_), custom_call_target="tpu_custom_call" | custom-call | tf_op jit(solution)/shard_map/pallas_call | solution.py:60
  26.1 5.6 %shard_map.117 = (f32[384,1024]{1,0:T(8,128)}, f32[384,1024]{1,0:T(8,128)}) custom-call(s32[1]{0:T(128)} %bitcast.refs_0_, bf16[1792,8192]{1,0:T(8,128)(2,1)} %refs_1_.11, bf16[384,1792]{1,0:T(8,128)(2,1)S(1)} %get-tuple-element.48.refs_2_, bf16[384,1792]{1,0:T(8,128)(2,1)S(1)} %get-tuple-element.97.refs_2_.refs_3_), custom_call_target="tpu_custom_call" | custom-call | tf_op jit(solution)/shard_map/pallas_call | solution.py:60
  31.8 4.2 %shard_map.118 = bf16[384,1024]{1,0:T(8,128)(2,1)} custom-call(s32[1]{0:T(128)} %bitcast.refs_0_, bf16[1792,8192]{1,0:T(8,128)(2,1)} %refs_1_.11, bf16[384,1792]{1,0:T(8,128)(2,1)S(1)} %get-tuple-element.48.refs_2_), custom_call_target="tpu_custom_call" | custom-call | tf_op jit(solution)/shard_map/pallas_call | solution.py:60
  36.0 2.0 %collective-permute-start.3 = (bf16[384,1024]{1,0:T(8,128)(2,1)}, bf16[384,1024]{1,0:T(8,128)(2,1)S(1)}, u32[]{:S(2)}, u32[]{:S(2)}) collective-permute-start(bf16[384,1024]{1,0:T(8,128)(2,1)} %shard_map.118), channel_id=1, source_target_pairs={{0,1},{1,0},{2,3},{3,2},{4,5},{5,4},{6,7},{7,6},{8,9},{9,8},{10,11... | collective-permute-start | bytes 2359304 | tf_op jit(solution)/shard_map/ppermute | solution.py:31
  38.0 1.4 add_convert_fusion.7
  39.4 3.5 %collective-permute-start.4 = (bf16[384,1024]{1,0:T(8,128)(2,1)S(1)}, bf16[384,1024]{1,0:T(8,128)(2,1)S(1)}, u32[]{:S(2)}, u32[]{:S(2)}) collective-permute-start(bf16[384,1024]{1,0:T(8,128)(2,1)S(1)} %add_convert_fusion.7), channel_id=1, source_target_pairs={{0,2},{1,3},{6,4},{7,5},{8,10},{9,11},{14,12},{15,13},{16,18},{17,... | collective-permute-start | bytes 2359304 | tf_op jit(solution)/shard_map/ppermute | solution.py:26
  42.9 5.7 %shard_map.119 = (f32[384,1024]{1,0:T(8,128)}, f32[384,1024]{1,0:T(8,128)}) custom-call(s32[1]{0:T(128)} %bitcast.refs_0_, bf16[1792,8192]{1,0:T(8,128)(2,1)} %refs_1_.11, bf16[384,1792]{1,0:T(8,128)(2,1)S(1)} %get-tuple-element.48.refs_2_, bf16[384,1792]{1,0:T(8,128)(2,1)S(1)} %get-tuple-element.97.refs_2_.refs_3_), custom_call_target="tpu_custom_call" | custom-call | tf_op jit(solution)/shard_map/pallas_call | solution.py:60
  48.6 4.1 %shard_map.120 = bf16[384,1024]{1,0:T(8,128)(2,1)} custom-call(s32[1]{0:T(128)} %bitcast.refs_0_, bf16[1792,8192]{1,0:T(8,128)(2,1)} %refs_1_.11, bf16[384,1792]{1,0:T(8,128)(2,1)S(1)} %get-tuple-element.97.refs_2_.refs_3_), custom_call_target="tpu_custom_call" | custom-call | tf_op jit(solution)/shard_map/pallas_call | solution.py:60
  52.6 0.5 collective-permute-done.2
  53.2 0.9 copy-done.3
  54.4 3.9 %collective-permute-start.6 = (bf16[432,1024]{1,0:T(8,128)(2,1)S(1)}, bf16[432,1024]{1,0:T(8,128)(2,1)S(1)}, u32[]{:S(2)}, u32[]{:S(2)}) collective-permute-start(bf16[432,1024]{1,0:T(8,128)(2,1)S(1)} %pad_maximum_fusion.2), channel_id=1, source_target_pairs={{0,2},{1,3},{6,4},{7,5},{8,10},{9,11},{14,12},{15,13},{16,18},{17,... | collective-permute-start | bytes 2654216 | tf_op jit(solution)/shard_map/ppermute | solution.py:26
  58.4 1.6 collective-permute-start.5
  60.0 4.0 %shard_map.121 = bf16[384,1024]{1,0:T(8,128)(2,1)} custom-call(s32[1]{0:T(128)} %bitcast.refs_0_, bf16[1792,8192]{1,0:T(8,128)(2,1)} %refs_1_.11, bf16[384,1792]{1,0:T(8,128)(2,1)S(1)} %get-tuple-element.48.refs_2_), custom_call_target="tpu_custom_call" | custom-call | tf_op jit(solution)/shard_map/pallas_call | solution.py:60
  64.0 5.7 %shard_map.122 = (f32[384,1024]{1,0:T(8,128)}, f32[384,1024]{1,0:T(8,128)}) custom-call(s32[1]{0:T(128)} %bitcast.refs_0_, bf16[1792,8192]{1,0:T(8,128)(2,1)} %refs_1_.11, bf16[384,1792]{1,0:T(8,128)(2,1)S(1)} %get-tuple-element.48.refs_2_, bf16[384,1792]{1,0:T(8,128)(2,1)S(1)} %get-tuple-element.97.refs_2_.refs_3_), custom_call_target="tpu_custom_call" | custom-call | tf_op jit(solution)/shard_map/pallas_call | solution.py:60
  70.0 1.3 add_convert_fusion.5
  71.3 4.8 %collective-permute-start.7 = (bf16[384,1024]{1,0:T(8,128)(2,1)}, bf16[384,1024]{1,0:T(8,128)(2,1)}, u32[]{:S(2)}, u32[]{:S(2)}) collective-permute-start(bf16[384,1024]{1,0:T(8,128)(2,1)} %add_convert_fusion.5), channel_id=1, source_target_pairs={{0,2},{1,3},{2,4},{3,5},{8,10},{9,11},{10,12},{11,13},{16,18},{17,... | collective-permute-start | bytes 2359304 | tf_op jit(solution)/shard_map/ppermute | solution.py:26
  76.1 1.6 collective-permute-start.8
  77.7 1.5 collective-permute-start.9
  79.2 4.1 %shard_map.123 = bf16[384,1024]{1,0:T(8,128)(2,1)} custom-call(s32[1]{0:T(128)} %bitcast.refs_0_, bf16[1792,8192]{1,0:T(8,128)(2,1)} %refs_1_.11, bf16[384,1792]{1,0:T(8,128)(2,1)S(1)} %get-tuple-element.97.refs_2_.refs_3_), custom_call_target="tpu_custom_call" | custom-call | tf_op jit(solution)/shard_map/pallas_call | solution.py:60
  83.3 3.5 %collective-permute-done.5 = bf16[384,1024]{1,0:T(8,128)(2,1)S(1)} collective-permute-done((bf16[384,1024]{1,0:T(8,128)(2,1)S(1)}, bf16[384,1024]{1,0:T(8,128)(2,1)S(1)}, u32[]{:S(2)}, u32[]{:S(2)}) %collective-permute-start.5) | collective-permute-done | bytes 786464 | tf_op jit(solution)/shard_map/ppermute | solution.py:31
  87.3 1.0 pad_maximum_fusion.3
  88.3 4.9 %collective-permute-start.10 = (bf16[432,1024]{1,0:T(8,128)(2,1)}, bf16[432,1024]{1,0:T(8,128)(2,1)}, u32[]{:S(2)}, u32[]{:S(2)}) collective-permute-start(bf16[432,1024]{1,0:T(8,128)(2,1)} %pad_maximum_fusion.3), channel_id=1, source_target_pairs={{0,2},{1,3},{2,4},{3,5},{8,10},{9,11},{10,12},{11,13},{16,18},{17,... | collective-permute-start | bytes 2654216 | tf_op jit(solution)/shard_map/ppermute | solution.py:26
  93.2 1.6 collective-permute-start.11
  94.8 1.9 %collective-permute-done.7 = bf16[384,1024]{1,0:T(8,128)(2,1)} collective-permute-done((bf16[384,1024]{1,0:T(8,128)(2,1)}, bf16[384,1024]{1,0:T(8,128)(2,1)}, u32[]{:S(2)}, u32[]{:S(2)}) %collective-permute-start.7) | collective-permute-done | bytes 786464 | tf_op jit(solution)/shard_map/ppermute | solution.py:26
  96.7 0.5 collective-permute-start.12
  97.2 5.6 %shard_map.124 = bf16[768,1024]{1,0:T(8,128)(2,1)} custom-call(s32[1]{0:T(128)} %bitcast.refs_0_, bf16[1792,8192]{1,0:T(8,128)(2,1)} %refs_1_.11, bf16[384,1792]{1,0:T(8,128)(2,1)S(1)} %get-tuple-element.48.refs_2_, bf16[384,1792]{1,0:T(8,128)(2,1)S(1)} %get-tuple-element.97.refs_2_.refs_3_), custom_call_target="tpu_custom_call" | custom-call | tf_op jit(solution)/shard_map/pallas_call | solution.py:60
  102.8 6.0 %shard_map.125 = f32[768,1024]{1,0:T(8,128)} custom-call(s32[1]{0:T(128)} %bitcast.refs_0_, bf16[1792,8192]{1,0:T(8,128)(2,1)} %refs_1_.11, bf16[384,1792]{1,0:T(8,128)(2,1)S(1)} %get-tuple-element.48.refs_2_, bf16[384,1792]{1,0:T(8,128)(2,1)S(1)} %get-tuple-element.97.refs_2_.refs_3_), custom_call_target="tpu_custom_call" | custom-call | tf_op jit(solution)/shard_map/pallas_call | solution.py:60
  108.8 1.5 collective-permute-start.15
  110.4 3.7 %add_convert_fusion.1 = (bf16[384,1024]{1,0:T(8,128)(2,1)S(1)}, bf16[384,1024]{1,0:T(8,128)(2,1)}) fusion(bf16[384,1024]{1,0:T(8,128)(2,1)} %collective-permute-done.8, f32[384,1024]{1,0:T(8,128)S(1)} %copy-done.6, bf16[384,1024]{1,0:T(8,128)(2,1)} %collective-permute-done.1, f32[384,1024]{1,0:T(8,128)S(1)} %copy-done.13, ...), kind=kLoop, calls=%fused_computation.24 | loop fusion | flops 4325376 | bytes 7864321 | tf_op jit(solution)/shard_map/convert_element_type | solution.py:139
  114.1 4.4 %collective-permute-start.13 = (bf16[384,1024]{1,0:T(8,128)(2,1)}, bf16[384,1024]{1,0:T(8,128)(2,1)S(1)}, u32[]{:S(2)}, u32[]{:S(2)}) collective-permute-start(bf16[384,1024]{1,0:T(8,128)(2,1)} %get-tuple-element.102), channel_id=1, source_target_pairs={{0,2},{1,3},{2,4},{3,5},{4,6},{5,7},{8,10},{9,11},{10,12},{11,13},... | collective-permute-start | bytes 2359304 | tf_op jit(solution)/shard_map/ppermute | solution.py:26
  118.5 1.3 collective-permute-start.14
  119.9 1.1 add_convert_fusion.8
  121.0 2.5 %add_convert_fusion = (bf16[384,1024]{1,0:T(8,128)(2,1)S(1)}, bf16[384,1024]{1,0:T(8,128)(2,1)S(1)}) fusion(f32[384,1024]{1,0:T(8,128)S(1)} %copy-done.4, bf16[384,1024]{1,0:T(8,128)(2,1)S(1)} %copy-done.2, f32[384,1024]{1,0:T(8,128)S(1)} %copy-done.12, bf16[384,1024]{1,0:T(8,128)(2,1)} %collective-permute-done.12, ...), kind=kLoop, calls=%fused_computation.22 | loop fusion | flops 4325376 | bytes 7864321 | tf_op jit(solution)/shard_map/convert_element_type | solution.py:139
  123.5 1.4 pad_maximum_fusion
  124.9 5.5 %collective-permute-start.16 = (bf16[432,1024]{1,0:T(8,128)(2,1)}, bf16[432,1024]{1,0:T(8,128)(2,1)}, u32[]{:S(2)}, u32[]{:S(2)}) collective-permute-start(bf16[432,1024]{1,0:T(8,128)(2,1)} %get-tuple-element.104), channel_id=1, source_target_pairs={{0,2},{1,3},{2,4},{3,5},{4,6},{5,7},{8,10},{9,11},{10,12},{11,13},... | collective-permute-start | bytes 2654216 | tf_op jit(solution)/shard_map/ppermute | solution.py:26
  130.4 1.3 collective-permute-start.17
  131.7 2.6 %shard_map.126 = bf16[6,64,1024]{2,1,0:T(8,128)(2,1)} custom-call(s32[6]{0:T(128)} %get-tuple-element.108.ids_ref, bf16[32,64,1024]{2,1,0:T(8,128)(2,1)} %factors_ref.3), custom_call_target="tpu_custom_call" | custom-call | tf_op jit(solution)/shard_map/pallas_call | solution.py:95
  134.3 2.6 %shard_map.127 = bf16[6,64,1024]{2,1,0:T(8,128)(2,1)} custom-call(s32[6]{0:T(128)} %get-tuple-element.107.ids_ref, bf16[32,64,1024]{2,1,0:T(8,128)(2,1)} %factors_ref.3), custom_call_target="tpu_custom_call" | custom-call | tf_op jit(solution)/shard_map/pallas_call | solution.py:95
  137.1 3.8 %collective-permute-done.14 = bf16[384,1024]{1,0:T(8,128)(2,1)S(1)} collective-permute-done((bf16[384,1024]{1,0:T(8,128)(2,1)S(1)}, bf16[384,1024]{1,0:T(8,128)(2,1)S(1)}, u32[]{:S(2)}, u32[]{:S(2)}) %collective-permute-start.14) | collective-permute-done | bytes 786464 | tf_op jit(solution)/shard_map/ppermute | solution.py:26
  140.9 1.4 convert_add_fusion.3
  142.4 11.8 %collective-permute-done.15 = bf16[768,1024]{1,0:T(8,128)(2,1)} collective-permute-done((bf16[768,1024]{1,0:T(8,128)(2,1)}, bf16[768,1024]{1,0:T(8,128)(2,1)}, u32[]{:S(2)}, u32[]{:S(2)}) %collective-permute-start.15) | collective-permute-done | bytes 1572896 | tf_op jit(solution)/shard_map/ppermute | solution.py:31
  154.2 1.9 %convert_add_fusion.1 = f32[768,1024]{1,0:T(8,128)S(1)} fusion(f32[768,1024]{1,0:T(8,128)S(1)} %copy-done, bf16[768,1024]{1,0:T(8,128)(2,1)} %collective-permute-done.15), kind=kLoop, calls=%fused_computation.9 | loop fusion | flops 1572864 | bytes 7864320 | tf_op jit(solution)/shard_map/add | solution.py:138
  156.4 1.0 select_select_fusion
  157.6 1.7 convert_add_fusion.2
  159.4 1.9 %convolution_convert_fusion = bf16[6,128,1024]{2,1,0:T(8,128)(2,1)S(1)} fusion(bf16[6,128,64]{2,1,0:T(8,128)(2,1)S(1)} %reshape_reshape.3, bf16[6,64,1024]{2,1,0:T(8,128)(2,1)} %collective-permute-done.18, bf16[6,64,1024]{2,1,0:T(8,128)(2,1)S(1)} %copy-done.8, pred[6]{0:T(512)(128)(4,1)S(1)} %fusion.27), kind=kOutput, calls=%fused_computation.20 | convolution fusion | flops 101842944 | bytes 3244038 | tf_op jit(solution)/shard_map/bcn,bnt->bct/dot_general | solution.py:278
  161.4 2.1 %multiply_reduce_fusion.1 = (f32[768]{0:T(1024)S(1)}, f32[768]{0:T(1024)S(1)}, bf16[768,1024]{1,0:T(8,128)(2,1)}) fusion(f32[1024]{0:T(1024)S(1)} %dynamic-slice-done, f32[768,1024]{1,0:T(8,128)S(1)} %convert_add_fusion.1, f32[384,1024]{1,0:T(8,128)S(1)} %convert_add_fusion.2, f32[384,1024]{1,0:T(8,128)S(1)} %copy-done.7, ...), kind=kLoop, calls=%fused_computation.8 | loop fusion | flops 8649216 | bytes 11020288 | tf_op jit(solution)/shard_map/reduce_sum | solution.py:313
  163.6 2.6 %collective-permute-start.19 = (f32[12,128]{1,0:T(8,128)S(1)}, f32[12,128]{1,0:T(8,128)S(1)}, u32[]{:S(2)}, u32[]{:S(2)}) collective-permute-start(f32[12,128]{1,0:T(8,128)S(1)} %reshape.81), channel_id=1, source_target_pairs={{0,4},{1,5},{2,6},{3,7},{4,0},{5,1},{6,2},{7,3},{8,12},{9,13},{10,... | collective-permute-start | bytes 18440 | tf_op jit(solution)/shard_map/ppermute | solution.py:31
  166.2 2.0 %collective-permute-done.19 = f32[12,128]{1,0:T(8,128)S(1)} collective-permute-done((f32[12,128]{1,0:T(8,128)S(1)}, f32[12,128]{1,0:T(8,128)S(1)}, u32[]{:S(2)}, u32[]{:S(2)}) %collective-permute-start.19) | collective-permute-done | bytes 6176 | tf_op jit(solution)/shard_map/ppermute | solution.py:31
  168.2 1.5 collective-permute-start.20
  169.7 2.2 %collective-permute-done.20 = f32[12,128]{1,0:T(8,128)S(1)} collective-permute-done((f32[12,128]{1,0:T(8,128)S(1)}, f32[12,128]{1,0:T(8,128)S(1)}, u32[]{:S(2)}, u32[]{:S(2)}) %collective-permute-start.20) | collective-permute-done | bytes 6176 | tf_op jit(solution)/shard_map/ppermute | solution.py:31
  171.9 1.4 collective-permute-start.21
  173.3 2.2 %collective-permute-done.21 = f32[12,128]{1,0:T(8,128)S(1)} collective-permute-done((f32[12,128]{1,0:T(8,128)S(1)}, f32[12,128]{1,0:T(8,128)S(1)}, u32[]{:S(2)}, u32[]{:S(2)}) %collective-permute-start.21) | collective-permute-done | bytes 6176 | tf_op jit(solution)/shard_map/ppermute | solution.py:31
  175.5 0.7 fusion.21
  (77 shorter events, 2.5 us)
Async XLA Ops:
  5.0 13.5 %collective-permute-start = (bf16[6,64,1792]{2,1,0:T(8,128)(2,1)}, bf16[6,64,1792]{2,1,0:T(8,128)(2,1)}, u32[]{:S(2)}, u32[]{:S(2)}) collective-permute-start(bf16[6,64,1792]{2,1,0:T(8,128)(2,1)} %shard_map.113), channel_id=1, source_target_pairs={{0,8},{8,0},{1,9},{9,1},{2,10},{10,2},{3,11},{11,3},{4,12},{12,4},... | collective-permute-start | bytes 4128776 | tf_op jit(solution)/shard_map/ppermute | solution.py:258
  13.0 25.0 %collective-permute-start.1 = (bf16[384,1024]{1,0:T(8,128)(2,1)}, bf16[384,1024]{1,0:T(8,128)(2,1)}, u32[]{:S(2)}, u32[]{:S(2)}) collective-permute-start(bf16[384,1024]{1,0:T(8,128)(2,1)} %shard_map.114), channel_id=1, source_target_pairs={{0,1},{1,0},{2,3},{3,2},{4,5},{5,4},{6,7},{7,6},{8,9},{9,8},{10,11... | collective-permute-start | bytes 2359304 | tf_op jit(solution)/shard_map/ppermute | solution.py:31
  26.1 27.0 %collective-permute-start.2 = (bf16[432,1024]{1,0:T(8,128)(2,1)}, bf16[432,1024]{1,0:T(8,128)(2,1)S(1)}, u32[]{:S(2)}, u32[]{:S(2)}) collective-permute-start(bf16[432,1024]{1,0:T(8,128)(2,1)} %shard_map.116), channel_id=1, source_target_pairs={{0,1},{1,0},{2,3},{3,2},{4,5},{5,4},{6,7},{7,6},{8,9},{9,8},{10,11... | collective-permute-start | bytes 2654216 | tf_op jit(solution)/shard_map/ppermute | solution.py:31
  31.8 6.2 %copy-start.5 = (f32[384,1024]{1,0:T(8,128)S(1)}, f32[384,1024]{1,0:T(8,128)}, u32[]{:S(2)}) copy-start(f32[384,1024]{1,0:T(8,128)} %get-tuple-element.82) | copy-start | bytes 4718596
  36.0 34.0 %collective-permute-start.3 = (bf16[384,1024]{1,0:T(8,128)(2,1)}, bf16[384,1024]{1,0:T(8,128)(2,1)S(1)}, u32[]{:S(2)}, u32[]{:S(2)}) collective-permute-start(bf16[384,1024]{1,0:T(8,128)(2,1)} %shard_map.118), channel_id=1, source_target_pairs={{0,1},{1,0},{2,3},{3,2},{4,5},{5,4},{6,7},{7,6},{8,9},{9,8},{10,11... | collective-permute-start | bytes 2359304 | tf_op jit(solution)/shard_map/ppermute | solution.py:31
  39.4 30.6 %collective-permute-start.4 = (bf16[384,1024]{1,0:T(8,128)(2,1)S(1)}, bf16[384,1024]{1,0:T(8,128)(2,1)S(1)}, u32[]{:S(2)}, u32[]{:S(2)}) collective-permute-start(bf16[384,1024]{1,0:T(8,128)(2,1)S(1)} %add_convert_fusion.7), channel_id=1, source_target_pairs={{0,2},{1,3},{6,4},{7,5},{8,10},{9,11},{14,12},{15,13},{16,18},{17,... | collective-permute-start | bytes 2359304 | tf_op jit(solution)/shard_map/ppermute | solution.py:26
  52.6 1.4 copy-start.3
  53.1 34.1 %copy-start.14 = (bf16[432,1024]{1,0:T(8,128)(2,1)}, bf16[432,1024]{1,0:T(8,128)(2,1)S(1)}, u32[]{:S(2)}) copy-start(bf16[432,1024]{1,0:T(8,128)(2,1)S(1)} %collective-permute-done.2) | copy-start | bytes 2654212
  53.2 1.1 copy-start.1
  54.3 4.0 %copy-start.16 = (bf16[384,1024]{1,0:T(8,128)(2,1)S(1)}, bf16[384,1024]{1,0:T(8,128)(2,1)}, u32[]{:S(2)}) copy-start(bf16[384,1024]{1,0:T(8,128)(2,1)} %shard_map.120) | copy-start | bytes 2359300
  54.4 28.8 %collective-permute-start.6 = (bf16[432,1024]{1,0:T(8,128)(2,1)S(1)}, bf16[432,1024]{1,0:T(8,128)(2,1)S(1)}, u32[]{:S(2)}, u32[]{:S(2)}) collective-permute-start(bf16[432,1024]{1,0:T(8,128)(2,1)S(1)} %pad_maximum_fusion.2), channel_id=1, source_target_pairs={{0,2},{1,3},{6,4},{7,5},{8,10},{9,11},{14,12},{15,13},{16,18},{17,... | collective-permute-start | bytes 2654216 | tf_op jit(solution)/shard_map/ppermute | solution.py:26
  58.4 28.5 %collective-permute-start.5 = (bf16[384,1024]{1,0:T(8,128)(2,1)S(1)}, bf16[384,1024]{1,0:T(8,128)(2,1)S(1)}, u32[]{:S(2)}, u32[]{:S(2)}) collective-permute-start(bf16[384,1024]{1,0:T(8,128)(2,1)S(1)} %copy-done.16), channel_id=1, source_target_pairs={{0,1},{1,0},{2,3},{3,2},{4,5},{5,4},{6,7},{7,6},{8,9},{9,8},{10,11... | collective-permute-start | bytes 2359304 | tf_op jit(solution)/shard_map/ppermute | solution.py:31
  64.0 6.0 %copy-start.10 = (f32[384,1024]{1,0:T(8,128)S(1)}, f32[384,1024]{1,0:T(8,128)}, u32[]{:S(2)}) copy-start(f32[384,1024]{1,0:T(8,128)} %get-tuple-element.65) | copy-start | bytes 4718596
  71.3 25.4 %collective-permute-start.7 = (bf16[384,1024]{1,0:T(8,128)(2,1)}, bf16[384,1024]{1,0:T(8,128)(2,1)}, u32[]{:S(2)}, u32[]{:S(2)}) collective-permute-start(bf16[384,1024]{1,0:T(8,128)(2,1)} %add_convert_fusion.5), channel_id=1, source_target_pairs={{0,2},{1,3},{2,4},{3,5},{8,10},{9,11},{10,12},{11,13},{16,18},{17,... | collective-permute-start | bytes 2359304 | tf_op jit(solution)/shard_map/ppermute | solution.py:26
  76.1 32.7 %collective-permute-start.8 = (bf16[384,1024]{1,0:T(8,128)(2,1)}, bf16[384,1024]{1,0:T(8,128)(2,1)}, u32[]{:S(2)}, u32[]{:S(2)}) collective-permute-start(bf16[384,1024]{1,0:T(8,128)(2,1)} %add_convert_fusion.5), channel_id=1, source_target_pairs={{6,4},{7,5},{4,2},{5,3},{14,12},{15,13},{12,10},{13,11},{22,20},{2... | collective-permute-start | bytes 2359304 | tf_op jit(solution)/shard_map/ppermute | solution.py:26
  77.7 32.7 %collective-permute-start.9 = (bf16[384,1024]{1,0:T(8,128)(2,1)}, bf16[384,1024]{1,0:T(8,128)(2,1)}, u32[]{:S(2)}, u32[]{:S(2)}) collective-permute-start(bf16[384,1024]{1,0:T(8,128)(2,1)} %shard_map.121), channel_id=1, source_target_pairs={{0,1},{1,0},{2,3},{3,2},{4,5},{5,4},{6,7},{7,6},{8,9},{9,8},{10,11... | collective-permute-start | bytes 2359304 | tf_op jit(solution)/shard_map/ppermute | solution.py:31
  83.3 3.6 %copy-start.9 = (f32[384,1024]{1,0:T(8,128)S(1)}, f32[384,1024]{1,0:T(8,128)}, u32[]{:S(2)}) copy-start(f32[384,1024]{1,0:T(8,128)} %get-tuple-element.70) | copy-start | bytes 4718596
  83.3 4.0 %copy-start.15 = (bf16[432,1024]{1,0:T(8,128)(2,1)}, bf16[432,1024]{1,0:T(8,128)(2,1)S(1)}, u32[]{:S(2)}) copy-start(bf16[432,1024]{1,0:T(8,128)(2,1)S(1)} %collective-permute-done.6) | copy-start | bytes 2654212
  88.3 30.2 %collective-permute-start.10 = (bf16[432,1024]{1,0:T(8,128)(2,1)}, bf16[432,1024]{1,0:T(8,128)(2,1)}, u32[]{:S(2)}, u32[]{:S(2)}) collective-permute-start(bf16[432,1024]{1,0:T(8,128)(2,1)} %pad_maximum_fusion.3), channel_id=1, source_target_pairs={{0,2},{1,3},{2,4},{3,5},{8,10},{9,11},{10,12},{11,13},{16,18},{17,... | collective-permute-start | bytes 2654216 | tf_op jit(solution)/shard_map/ppermute | solution.py:26
  93.2 26.6 %collective-permute-start.11 = (bf16[432,1024]{1,0:T(8,128)(2,1)}, bf16[432,1024]{1,0:T(8,128)(2,1)}, u32[]{:S(2)}, u32[]{:S(2)}) collective-permute-start(bf16[432,1024]{1,0:T(8,128)(2,1)} %pad_maximum_fusion.3), channel_id=1, source_target_pairs={{6,4},{7,5},{4,2},{5,3},{14,12},{15,13},{12,10},{13,11},{22,20},{2... | collective-permute-start | bytes 2654216 | tf_op jit(solution)/shard_map/ppermute | solution.py:26
  96.7 24.3 %collective-permute-start.12 = (bf16[384,1024]{1,0:T(8,128)(2,1)}, bf16[384,1024]{1,0:T(8,128)(2,1)}, u32[]{:S(2)}, u32[]{:S(2)}) collective-permute-start(bf16[384,1024]{1,0:T(8,128)(2,1)} %shard_map.123), channel_id=1, source_target_pairs={{0,1},{1,0},{2,3},{3,2},{4,5},{5,4},{6,7},{7,6},{8,9},{9,8},{10,11... | collective-permute-start | bytes 2359304 | tf_op jit(solution)/shard_map/ppermute | solution.py:31
  102.8 7.6 %copy-start.6 = (f32[384,1024]{1,0:T(8,128)S(1)}, f32[384,1024]{1,0:T(8,128)}, u32[]{:S(2)}) copy-start(f32[384,1024]{1,0:T(8,128)} %get-tuple-element.82) | copy-start | bytes 4718596
  102.8 7.6 %copy-start.13 = (f32[384,1024]{1,0:T(8,128)S(1)}, f32[384,1024]{1,0:T(8,128)}, u32[]{:S(2)}) copy-start(f32[384,1024]{1,0:T(8,128)} %get-tuple-element.75) | copy-start | bytes 4718596
  108.8 12.2 %copy-start.2 = (bf16[384,1024]{1,0:T(8,128)(2,1)S(1)}, bf16[384,1024]{1,0:T(8,128)(2,1)}, u32[]{:S(2)}) copy-start(bf16[384,1024]{1,0:T(8,128)(2,1)} %copy-done.1) | copy-start | bytes 2359300
  108.8 45.3 %collective-permute-start.15 = (bf16[768,1024]{1,0:T(8,128)(2,1)}, bf16[768,1024]{1,0:T(8,128)(2,1)}, u32[]{:S(2)}, u32[]{:S(2)}) collective-permute-start(bf16[768,1024]{1,0:T(8,128)(2,1)} %shard_map.124), channel_id=1, source_target_pairs={{0,1},{1,0},{2,3},{3,2},{4,5},{5,4},{6,7},{7,6},{8,9},{9,8},{10,11... | collective-permute-start | bytes 4718600 | tf_op jit(solution)/shard_map/ppermute | solution.py:31
  110.3 10.6 %copy-start.4 = (f32[384,1024]{1,0:T(8,128)S(1)}, f32[384,1024]{1,0:T(8,128)}, u32[]{:S(2)}) copy-start(f32[384,1024]{1,0:T(8,128)} %get-tuple-element.89) | copy-start | bytes 4718596
  110.4 10.6 %copy-start.12 = (f32[384,1024]{1,0:T(8,128)S(1)}, f32[384,1024]{1,0:T(8,128)}, u32[]{:S(2)}) copy-start(f32[384,1024]{1,0:T(8,128)} %get-tuple-element.79) | copy-start | bytes 4718596
  114.1 22.9 %collective-permute-start.13 = (bf16[384,1024]{1,0:T(8,128)(2,1)}, bf16[384,1024]{1,0:T(8,128)(2,1)S(1)}, u32[]{:S(2)}, u32[]{:S(2)}) collective-permute-start(bf16[384,1024]{1,0:T(8,128)(2,1)} %get-tuple-element.102), channel_id=1, source_target_pairs={{0,2},{1,3},{2,4},{3,5},{4,6},{5,7},{8,10},{9,11},{10,12},{11,13},... | collective-permute-start | bytes 2359304 | tf_op jit(solution)/shard_map/ppermute | solution.py:26
  118.5 22.4 %collective-permute-start.14 = (bf16[384,1024]{1,0:T(8,128)(2,1)S(1)}, bf16[384,1024]{1,0:T(8,128)(2,1)S(1)}, u32[]{:S(2)}, u32[]{:S(2)}) collective-permute-start(bf16[384,1024]{1,0:T(8,128)(2,1)S(1)} %get-tuple-element.101), channel_id=1, source_target_pairs={{6,4},{7,5},{4,2},{5,3},{2,0},{3,1},{14,12},{15,13},{12,10},{13,11... | collective-permute-start | bytes 2359304 | tf_op jit(solution)/shard_map/ppermute | solution.py:26
  124.9 31.2 %collective-permute-start.16 = (bf16[432,1024]{1,0:T(8,128)(2,1)}, bf16[432,1024]{1,0:T(8,128)(2,1)}, u32[]{:S(2)}, u32[]{:S(2)}) collective-permute-start(bf16[432,1024]{1,0:T(8,128)(2,1)} %get-tuple-element.104), channel_id=1, source_target_pairs={{0,2},{1,3},{2,4},{3,5},{4,6},{5,7},{8,10},{9,11},{10,12},{11,13},... | collective-permute-start | bytes 2654216 | tf_op jit(solution)/shard_map/ppermute | solution.py:26
  130.4 26.0 %collective-permute-start.17 = (bf16[432,1024]{1,0:T(8,128)(2,1)}, bf16[432,1024]{1,0:T(8,128)(2,1)}, u32[]{:S(2)}, u32[]{:S(2)}) collective-permute-start(bf16[432,1024]{1,0:T(8,128)(2,1)} %get-tuple-element.103), channel_id=1, source_target_pairs={{6,4},{7,5},{4,2},{5,3},{2,0},{3,1},{14,12},{15,13},{12,10},{13,11... | collective-permute-start | bytes 2654216 | tf_op jit(solution)/shard_map/ppermute | solution.py:26
  137.0 17.2 %copy-start = (f32[768,1024]{1,0:T(8,128)S(1)}, f32[768,1024]{1,0:T(8,128)}, u32[]{:S(2)}) copy-start(f32[768,1024]{1,0:T(8,128)} %shard_map.125) | copy-start | bytes 9437188
  137.0 22.4 %collective-permute-start.18 = (bf16[6,64,1024]{2,1,0:T(8,128)(2,1)}, bf16[6,64,1024]{2,1,0:T(8,128)(2,1)}, u32[]{:S(2)}, u32[]{:S(2)}) collective-permute-start(bf16[6,64,1024]{2,1,0:T(8,128)(2,1)} %shard_map.126), channel_id=1, source_target_pairs={{0,8},{8,0},{1,9},{9,1},{2,10},{10,2},{3,11},{11,3},{4,12},{12,4},... | collective-permute-start | bytes 2359304 | tf_op jit(solution)/shard_map/ppermute | solution.py:258
  157.6 1.8 %copy-start.8 = (bf16[6,64,1024]{2,1,0:T(8,128)(2,1)S(1)}, bf16[6,64,1024]{2,1,0:T(8,128)(2,1)}, u32[]{:S(2)}) copy-start(bf16[6,64,1024]{2,1,0:T(8,128)(2,1)} %shard_map.127) | copy-start | bytes 2359300
  159.3 2.0 %copy-start.7 = (f32[384,1024]{1,0:T(8,128)S(1)}, f32[384,1024]{1,0:T(8,128)}, u32[]{:S(2)}) copy-start(f32[384,1024]{1,0:T(8,128)} %convert_add_fusion.3) | copy-start | bytes 4718596
  159.3 2.1 %copy-start.11 = (bf16[768,1024]{1,0:T(8,128)(2,1)S(1)}, bf16[768,1024]{1,0:T(8,128)(2,1)}, u32[]{:S(2)}) copy-start(bf16[768,1024]{1,0:T(8,128)(2,1)} %param.15) | copy-start | bytes 4718596
  159.3 2.1 %dynamic-slice-start = ((f32[8192]{0:T(1024)}, s32[]{:T(128)}), f32[1024]{0:T(1024)S(1)}, s32[]{:S(2)}) async-start(f32[8192]{0:T(1024)} %param.16, s32[]{:T(128)} %select_n.99), calls=%async_computation | async-start | bytes 8704 | tf_op jit(solution)/shard_map/dynamic_slice | solution.py:310
  161.4 14.1 %copy-start.17 = (s32[6]{0:T(128)S(1)}, s32[6]{0:T(128)}, u32[]{:S(2)}) copy-start(s32[6]{0:T(128)} %param.19) | copy-start | bytes 76
  161.4 14.1 %copy-start.18 = (s32[6]{0:T(128)S(1)}, s32[6]{0:T(128)}, u32[]{:S(2)}) copy-start(s32[6]{0:T(128)} %param.18) | copy-start | bytes 76
  163.6 4.6 %collective-permute-start.19 = (f32[12,128]{1,0:T(8,128)S(1)}, f32[12,128]{1,0:T(8,128)S(1)}, u32[]{:S(2)}, u32[]{:S(2)}) collective-permute-start(f32[12,128]{1,0:T(8,128)S(1)} %reshape.81), channel_id=1, source_target_pairs={{0,4},{1,5},{2,6},{3,7},{4,0},{5,1},{6,2},{7,3},{8,12},{9,13},{10,... | collective-permute-start | bytes 18440 | tf_op jit(solution)/shard_map/ppermute | solution.py:31
  168.2 3.7 %collective-permute-start.20 = (f32[12,128]{1,0:T(8,128)S(1)}, f32[12,128]{1,0:T(8,128)S(1)}, u32[]{:S(2)}, u32[]{:S(2)}) collective-permute-start(f32[12,128]{1,0:T(8,128)S(1)} %add.156), channel_id=1, source_target_pairs={{0,2},{1,3},{2,0},{3,1},{4,6},{5,7},{6,4},{7,5},{8,10},{9,11},{10,... | collective-permute-start | bytes 18440 | tf_op jit(solution)/shard_map/ppermute | solution.py:31
  171.9 3.7 %collective-permute-start.21 = (f32[12,128]{1,0:T(8,128)S(1)}, f32[12,128]{1,0:T(8,128)S(1)}, u32[]{:S(2)}, u32[]{:S(2)}) collective-permute-start(f32[12,128]{1,0:T(8,128)S(1)} %add.157), channel_id=1, source_target_pairs={{0,1},{1,0},{2,3},{3,2},{4,5},{5,4},{6,7},{7,6},{8,9},{9,8},{10,11... | collective-permute-start | bytes 18440 | tf_op jit(solution)/shard_map/ppermute | solution.py:31

commit v7 on v5

--- a/solution.py
+++ b/solution.py
@@ -15,7 +15,7 @@
 PAIR = 2
 ORDER = ((3, 2, 1, 0), (0, 3, 2, 1), (1, 0, 3, 2), (0, 1, 2, 3))
 PIECES = 2
-TILE = 512
+TILE = 1024
 
 ANYWHERE = pl.BlockSpec(memory_space=pl.ANY)
 NO_COST = pl.CostEstimate(flops=0, bytes_accessed=0, transcendentals=0)

time: 177 us -> 181 us (1.023)
  starting transfers between devices: 48.5 us -> 38.9 us
  Pallas kernels: 65.1 us -> 72 us
  waiting for transfers between devices: 26.8 us -> 32.8 us
    pallas_call x11, Pallas kernels: 53.1 us -> 60 us  [product(): pl.pallas_call(lambda *refs: product_kernel(len(inputs), count, more, *re...]
    ppermute x10, starting transfers between devices: 16.1 us -> 9.41 us  [across(): return lax.ppermute(value, 'tensor', [(t, t ^ bit) for t in range(size)])]
    ppermute x10, waiting for transfers between devices: 5.56 us -> 10.4 us  [along_line(): return lax.ppermute(value, 'tensor', pairs)]
    ppermute x10, starting transfers between devices: 31.8 us -> 28.8 us  [along_line(): return lax.ppermute(value, 'tensor', pairs)]
  transfers between devices with their start and end apart: 22 -> 22, of which waited for: 9 -> 8; matrix products, arithmetic and copies ran while one was open for 15% -> 15% of each run, Pallas kernels for 35% -> 38%
where the time goes in v7:
time: 181 us; the launch traced here: 180 us
  Pallas kernels  72 us (40%)
  starting transfers between devices  38.9 us (21%)
  waiting for transfers between devices  32.8 us (18%)
  other arithmetic  27.6 us (15%)
  local copies, waits for them, and re-layouts  4.2 us (2%)
  matrix products  3.07 us (2%)
    pallas_call x11, Pallas kernels, product(): pl.pallas_call(lambda *refs: product_kernel(len(inputs), count, more, *re...  60 us
    ppermute x10, starting transfers between devices, along_line(): return lax.ppermute(value, 'tensor', pairs)  28.8 us
    ppermute x10, waiting for transfers between devices, across(): return lax.ppermute(value, 'tensor', [(t, t ^ bit) for t in range(size)])  22.4 us
    pallas_call x4, Pallas kernels, pick(): pl.pallas_call(pick_kernel, grid_spec=pltpu.PrefetchScalarGridSpec(num_sc...  12 us
    convert_element_type x7, other arithmetic, grid_sums(): narrow = lambda *terms: add(*terms).astype(bf16)  10.6 us
    ppermute x10, waiting for transfers between devices, along_line(): return lax.ppermute(value, 'tensor', pairs)  10.4 us
    ppermute x10, starting transfers between devices, across(): return lax.ppermute(value, 'tensor', [(t, t ^ bit) for t in range(size)])  9.41 us
    add x3, other arithmetic, grid_sums(): add = lambda *terms: sum((t.astype(f32) for t in terms))  5.09 us
  transfers between devices with their start and end apart: 22, of which 8 were waited for; matrix products, arithmetic and copies ran while one was open for 15% of the time, Pallas kernels for 38%

profile of v7, /device:TPU:0, one launch (start us, length us, event | category | flops | bytes accessed | tf_op | source)
XLA Modules:
  0.0 179.7 jit_solution(7527172172782743546)
XLA Ops:
  0.7 0.7 reshape.75
  1.5 0.6 fusion.29
  2.1 3.2 %shard_map.113 = bf16[6,64,1792]{2,1,0:T(8,128)(2,1)} custom-call(s32[6]{0:T(128)} %get-tuple-element.108.ids_ref, bf16[32,64,1792]{2,1,0:T(8,128)(2,1)} %bitcast.31), custom_call_target="tpu_custom_call" | custom-call | tf_op jit(solution)/shard_map/pallas_call | solution.py:93
  5.3 0.6 collective-permute-start
  6.0 3.4 %fusion.9 = (bf16[384,1792]{1,0:T(8,128)(2,1)S(1)}, bf16[384,1792]{1,0:T(8,128)(2,1)S(1)}) fusion(bf16[768,1792]{1,0:T(8,128)(2,1)} %param.11, bf16[768,1792]{1,0:T(8,128)(2,1)} %param.10), kind=kLoop, calls=%fused_computation.18 | loop fusion | flops 11010048 | bytes 8257536 | tf_op jit(solution)/shard_map/convert_element_type | solution.py:284
  9.4 4.5 %shard_map.114 = bf16[384,1024]{1,0:T(8,128)(2,1)} custom-call(s32[1]{0:T(128)} %bitcast.refs_0_, bf16[1792,8192]{1,0:T(8,128)(2,1)} %refs_1_.11, bf16[384,1792]{1,0:T(8,128)(2,1)S(1)} %get-tuple-element.48.refs_2_), custom_call_target="tpu_custom_call" | custom-call | tf_op jit(solution)/shard_map/pallas_call | solution.py:60
  13.9 2.4 %collective-permute-start.1 = (bf16[384,1024]{1,0:T(8,128)(2,1)}, bf16[384,1024]{1,0:T(8,128)(2,1)}, u32[]{:S(2)}, u32[]{:S(2)}) collective-permute-start(bf16[384,1024]{1,0:T(8,128)(2,1)} %shard_map.114), channel_id=1, source_target_pairs={{0,1},{1,0},{2,3},{3,2},{4,5},{5,4},{6,7},{7,6},{8,9},{9,8},{10,11... | collective-permute-start | bytes 2359304 | tf_op jit(solution)/shard_map/ppermute | solution.py:31
  16.4 3.2 %shard_map.115 = bf16[6,64,1792]{2,1,0:T(8,128)(2,1)} custom-call(s32[6]{0:T(128)} %get-tuple-element.107.ids_ref, bf16[32,64,1792]{2,1,0:T(8,128)(2,1)} %bitcast.32), custom_call_target="tpu_custom_call" | custom-call | tf_op jit(solution)/shard_map/pallas_call | solution.py:93
  19.6 2.0 %broadcast_select_fusion = bf16[6,64,1792]{2,1,0:T(8,128)(2,1)S(1)} fusion(bf16[6,64,1792]{2,1,0:T(8,128)(2,1)} %collective-permute-done, bf16[6,64,1792]{2,1,0:T(8,128)(2,1)} %shard_map.115, pred[6]{0:T(512)(128)(4,1)S(1)} %fusion.27), kind=kLoop, calls=%fused_computation.33 | loop fusion | flops 688128 | bytes 4128774 | tf_op jit(solution)/shard_map/jit(_where)/select_n | solution.py:257
  21.6 0.6 convolution_bitcast_fusion
  22.1 0.6 convolution_bitcast_fusion.1
  23.1 4.5 %shard_map.116 = bf16[432,1024]{1,0:T(8,128)(2,1)} custom-call(s32[1]{0:T(128)} %bitcast.refs_0_, bf16[1792,8192]{1,0:T(8,128)(2,1)} %refs_1_.11, bf16[384,1792]{1,0:T(8,128)(2,1)S(1)} %get-tuple-element.97.refs_2_.refs_3_, f32[48,1024]{1,0:T(8,128)S(1)} %reshape.80.refs_3_), custom_call_target="tpu_custom_call" | custom-call | tf_op jit(solution)/shard_map/pallas_call | solution.py:60
  27.7 6.5 %shard_map.117 = (f32[384,1024]{1,0:T(8,128)}, f32[384,1024]{1,0:T(8,128)}) custom-call(s32[1]{0:T(128)} %bitcast.refs_0_, bf16[1792,8192]{1,0:T(8,128)(2,1)} %refs_1_.11, bf16[384,1792]{1,0:T(8,128)(2,1)S(1)} %get-tuple-element.48.refs_2_, bf16[384,1792]{1,0:T(8,128)(2,1)S(1)} %get-tuple-element.97.refs_2_.refs_3_), custom_call_target="tpu_custom_call" | custom-call | tf_op jit(solution)/shard_map/pallas_call | solution.py:60
  34.2 4.7 %shard_map.118 = bf16[384,1024]{1,0:T(8,128)(2,1)} custom-call(s32[1]{0:T(128)} %bitcast.refs_0_, bf16[1792,8192]{1,0:T(8,128)(2,1)} %refs_1_.11, bf16[384,1792]{1,0:T(8,128)(2,1)S(1)} %get-tuple-element.48.refs_2_), custom_call_target="tpu_custom_call" | custom-call | tf_op jit(solution)/shard_map/pallas_call | solution.py:60
  38.9 2.0 %collective-permute-start.3 = (bf16[384,1024]{1,0:T(8,128)(2,1)}, bf16[384,1024]{1,0:T(8,128)(2,1)S(1)}, u32[]{:S(2)}, u32[]{:S(2)}) collective-permute-start(bf16[384,1024]{1,0:T(8,128)(2,1)} %shard_map.118), channel_id=1, source_target_pairs={{0,1},{1,0},{2,3},{3,2},{4,5},{5,4},{6,7},{7,6},{8,9},{9,8},{10,11... | collective-permute-start | bytes 2359304 | tf_op jit(solution)/shard_map/ppermute | solution.py:31
  40.9 1.4 add_convert_fusion.7
  42.3 3.5 %collective-permute-start.4 = (bf16[384,1024]{1,0:T(8,128)(2,1)S(1)}, bf16[384,1024]{1,0:T(8,128)(2,1)S(1)}, u32[]{:S(2)}, u32[]{:S(2)}) collective-permute-start(bf16[384,1024]{1,0:T(8,128)(2,1)S(1)} %add_convert_fusion.7), channel_id=1, source_target_pairs={{0,2},{1,3},{6,4},{7,5},{8,10},{9,11},{14,12},{15,13},{16,18},{17,... | collective-permute-start | bytes 2359304 | tf_op jit(solution)/shard_map/ppermute | solution.py:26
  45.8 6.5 %shard_map.119 = (f32[384,1024]{1,0:T(8,128)}, f32[384,1024]{1,0:T(8,128)}) custom-call(s32[1]{0:T(128)} %bitcast.refs_0_, bf16[1792,8192]{1,0:T(8,128)(2,1)} %refs_1_.11, bf16[384,1792]{1,0:T(8,128)(2,1)S(1)} %get-tuple-element.48.refs_2_, bf16[384,1792]{1,0:T(8,128)(2,1)S(1)} %get-tuple-element.97.refs_2_.refs_3_), custom_call_target="tpu_custom_call" | custom-call | tf_op jit(solution)/shard_map/pallas_call | solution.py:60
  52.4 4.5 %shard_map.120 = bf16[384,1024]{1,0:T(8,128)(2,1)} custom-call(s32[1]{0:T(128)} %bitcast.refs_0_, bf16[1792,8192]{1,0:T(8,128)(2,1)} %refs_1_.11, bf16[384,1792]{1,0:T(8,128)(2,1)S(1)} %get-tuple-element.97.refs_2_.refs_3_), custom_call_target="tpu_custom_call" | custom-call | tf_op jit(solution)/shard_map/pallas_call | solution.py:60
  57.0 1.9 %copy-done.3 = f32[384,1024]{1,0:T(8,128)S(1)} copy-done((f32[384,1024]{1,0:T(8,128)S(1)}, f32[384,1024]{1,0:T(8,128)}, u32[]{:S(2)}) %copy-start.3) | copy-done | bytes 1572888
  58.9 0.3 add_convert_fusion.6
  59.3 1.7 collective-permute-start.6
  61.0 0.6 collective-permute-start.5
  61.5 4.5 %shard_map.121 = bf16[384,1024]{1,0:T(8,128)(2,1)} custom-call(s32[1]{0:T(128)} %bitcast.refs_0_, bf16[1792,8192]{1,0:T(8,128)(2,1)} %refs_1_.11, bf16[384,1792]{1,0:T(8,128)(2,1)S(1)} %get-tuple-element.48.refs_2_), custom_call_target="tpu_custom_call" | custom-call | tf_op jit(solution)/shard_map/pallas_call | solution.py:60
  66.1 6.6 %shard_map.122 = (f32[384,1024]{1,0:T(8,128)}, f32[384,1024]{1,0:T(8,128)}) custom-call(s32[1]{0:T(128)} %bitcast.refs_0_, bf16[1792,8192]{1,0:T(8,128)(2,1)} %refs_1_.11, bf16[384,1792]{1,0:T(8,128)(2,1)S(1)} %get-tuple-element.48.refs_2_, bf16[384,1792]{1,0:T(8,128)(2,1)S(1)} %get-tuple-element.97.refs_2_.refs_3_), custom_call_target="tpu_custom_call" | custom-call | tf_op jit(solution)/shard_map/pallas_call | solution.py:60
  72.7 1.3 add_convert_fusion.5
  74.0 2.9 %collective-permute-start.7 = (bf16[384,1024]{1,0:T(8,128)(2,1)}, bf16[384,1024]{1,0:T(8,128)(2,1)}, u32[]{:S(2)}, u32[]{:S(2)}) collective-permute-start(bf16[384,1024]{1,0:T(8,128)(2,1)} %add_convert_fusion.5), channel_id=1, source_target_pairs={{0,2},{1,3},{2,4},{3,5},{8,10},{9,11},{10,12},{11,13},{16,18},{17,... | collective-permute-start | bytes 2359304 | tf_op jit(solution)/shard_map/ppermute | solution.py:26
  76.9 1.6 collective-permute-start.8
  78.4 1.5 collective-permute-start.9
  80.0 4.5 %shard_map.123 = bf16[384,1024]{1,0:T(8,128)(2,1)} custom-call(s32[1]{0:T(128)} %bitcast.refs_0_, bf16[1792,8192]{1,0:T(8,128)(2,1)} %refs_1_.11, bf16[384,1792]{1,0:T(8,128)(2,1)S(1)} %get-tuple-element.97.refs_2_.refs_3_), custom_call_target="tpu_custom_call" | custom-call | tf_op jit(solution)/shard_map/pallas_call | solution.py:60
  84.5 3.1 %collective-permute-done.5 = bf16[384,1024]{1,0:T(8,128)(2,1)S(1)} collective-permute-done((bf16[384,1024]{1,0:T(8,128)(2,1)S(1)}, bf16[384,1024]{1,0:T(8,128)(2,1)S(1)}, u32[]{:S(2)}, u32[]{:S(2)}) %collective-permute-start.5) | collective-permute-done | bytes 786464 | tf_op jit(solution)/shard_map/ppermute | solution.py:31
  87.6 0.4 add_convert_fusion.4
  88.1 1.0 pad_maximum_fusion.3
  89.1 4.9 %collective-permute-start.10 = (bf16[432,1024]{1,0:T(8,128)(2,1)}, bf16[432,1024]{1,0:T(8,128)(2,1)}, u32[]{:S(2)}, u32[]{:S(2)}) collective-permute-start(bf16[432,1024]{1,0:T(8,128)(2,1)} %pad_maximum_fusion.3), channel_id=1, source_target_pairs={{0,2},{1,3},{2,4},{3,5},{8,10},{9,11},{10,12},{11,13},{16,18},{17,... | collective-permute-start | bytes 2654216 | tf_op jit(solution)/shard_map/ppermute | solution.py:26
  94.0 1.6 collective-permute-start.11
  95.6 4.1 %collective-permute-done.7 = bf16[384,1024]{1,0:T(8,128)(2,1)} collective-permute-done((bf16[384,1024]{1,0:T(8,128)(2,1)}, bf16[384,1024]{1,0:T(8,128)(2,1)}, u32[]{:S(2)}, u32[]{:S(2)}) %collective-permute-start.7) | collective-permute-done | bytes 786464 | tf_op jit(solution)/shard_map/ppermute | solution.py:26
  99.7 0.5 collective-permute-start.12
  100.2 6.2 %shard_map.124 = bf16[768,1024]{1,0:T(8,128)(2,1)} custom-call(s32[1]{0:T(128)} %bitcast.refs_0_, bf16[1792,8192]{1,0:T(8,128)(2,1)} %refs_1_.11, bf16[384,1792]{1,0:T(8,128)(2,1)S(1)} %get-tuple-element.48.refs_2_, bf16[384,1792]{1,0:T(8,128)(2,1)S(1)} %get-tuple-element.97.refs_2_.refs_3_), custom_call_target="tpu_custom_call" | custom-call | tf_op jit(solution)/shard_map/pallas_call | solution.py:60
  106.4 6.8 %shard_map.125 = f32[768,1024]{1,0:T(8,128)} custom-call(s32[1]{0:T(128)} %bitcast.refs_0_, bf16[1792,8192]{1,0:T(8,128)(2,1)} %refs_1_.11, bf16[384,1792]{1,0:T(8,128)(2,1)S(1)} %get-tuple-element.48.refs_2_, bf16[384,1792]{1,0:T(8,128)(2,1)S(1)} %get-tuple-element.97.refs_2_.refs_3_), custom_call_target="tpu_custom_call" | custom-call | tf_op jit(solution)/shard_map/pallas_call | solution.py:60
  113.2 1.5 collective-permute-start.15
  114.8 3.7 %add_convert_fusion.1 = (bf16[384,1024]{1,0:T(8,128)(2,1)S(1)}, bf16[384,1024]{1,0:T(8,128)(2,1)}) fusion(bf16[384,1024]{1,0:T(8,128)(2,1)} %collective-permute-done.8, f32[384,1024]{1,0:T(8,128)S(1)} %copy-done.6, bf16[384,1024]{1,0:T(8,128)(2,1)} %collective-permute-done.1, f32[384,1024]{1,0:T(8,128)S(1)} %copy-done.13, ...), kind=kLoop, calls=%fused_computation.24 | loop fusion | flops 4325376 | bytes 7864321 | tf_op jit(solution)/shard_map/convert_element_type | solution.py:137
  118.5 4.4 %collective-permute-start.13 = (bf16[384,1024]{1,0:T(8,128)(2,1)}, bf16[384,1024]{1,0:T(8,128)(2,1)S(1)}, u32[]{:S(2)}, u32[]{:S(2)}) collective-permute-start(bf16[384,1024]{1,0:T(8,128)(2,1)} %get-tuple-element.102), channel_id=1, source_target_pairs={{0,2},{1,3},{2,4},{3,5},{4,6},{5,7},{8,10},{9,11},{10,12},{11,13},... | collective-permute-start | bytes 2359304 | tf_op jit(solution)/shard_map/ppermute | solution.py:26
  122.9 1.3 collective-permute-start.14
  124.3 1.1 add_convert_fusion.8
  125.4 2.5 %add_convert_fusion = (bf16[384,1024]{1,0:T(8,128)(2,1)S(1)}, bf16[384,1024]{1,0:T(8,128)(2,1)S(1)}) fusion(f32[384,1024]{1,0:T(8,128)S(1)} %copy-done.4, bf16[384,1024]{1,0:T(8,128)(2,1)S(1)} %copy-done.2, f32[384,1024]{1,0:T(8,128)S(1)} %copy-done.12, bf16[384,1024]{1,0:T(8,128)(2,1)} %collective-permute-done.12, ...), kind=kLoop, calls=%fused_computation.22 | loop fusion | flops 4325376 | bytes 7864321 | tf_op jit(solution)/shard_map/convert_element_type | solution.py:137
  127.9 1.4 pad_maximum_fusion
  129.3 5.5 %collective-permute-start.16 = (bf16[432,1024]{1,0:T(8,128)(2,1)}, bf16[432,1024]{1,0:T(8,128)(2,1)}, u32[]{:S(2)}, u32[]{:S(2)}) collective-permute-start(bf16[432,1024]{1,0:T(8,128)(2,1)} %get-tuple-element.104), channel_id=1, source_target_pairs={{0,2},{1,3},{2,4},{3,5},{4,6},{5,7},{8,10},{9,11},{10,12},{11,13},... | collective-permute-start | bytes 2654216 | tf_op jit(solution)/shard_map/ppermute | solution.py:26
  134.8 1.5 collective-permute-start.17
  136.3 2.8 %shard_map.126 = bf16[6,64,1024]{2,1,0:T(8,128)(2,1)} custom-call(s32[6]{0:T(128)} %get-tuple-element.108.ids_ref, bf16[32,64,1024]{2,1,0:T(8,128)(2,1)} %factors_ref.3), custom_call_target="tpu_custom_call" | custom-call | tf_op jit(solution)/shard_map/pallas_call | solution.py:93
  139.1 2.8 %shard_map.127 = bf16[6,64,1024]{2,1,0:T(8,128)(2,1)} custom-call(s32[6]{0:T(128)} %get-tuple-element.107.ids_ref, bf16[32,64,1024]{2,1,0:T(8,128)(2,1)} %factors_ref.3), custom_call_target="tpu_custom_call" | custom-call | tf_op jit(solution)/shard_map/pallas_call | solution.py:93
  142.0 3.3 %collective-permute-done.14 = bf16[384,1024]{1,0:T(8,128)(2,1)S(1)} collective-permute-done((bf16[384,1024]{1,0:T(8,128)(2,1)S(1)}, bf16[384,1024]{1,0:T(8,128)(2,1)S(1)}, u32[]{:S(2)}, u32[]{:S(2)}) %collective-permute-start.14) | collective-permute-done | bytes 786464 | tf_op jit(solution)/shard_map/ppermute | solution.py:26
  145.3 1.4 convert_add_fusion.3
  146.8 8.2 %collective-permute-done.15 = bf16[768,1024]{1,0:T(8,128)(2,1)} collective-permute-done((bf16[768,1024]{1,0:T(8,128)(2,1)}, bf16[768,1024]{1,0:T(8,128)(2,1)}, u32[]{:S(2)}, u32[]{:S(2)}) %collective-permute-start.15) | collective-permute-done | bytes 1572896 | tf_op jit(solution)/shard_map/ppermute | solution.py:31
  154.9 1.9 %convert_add_fusion.1 = f32[768,1024]{1,0:T(8,128)S(1)} fusion(f32[768,1024]{1,0:T(8,128)S(1)} %copy-done, bf16[768,1024]{1,0:T(8,128)(2,1)} %collective-permute-done.15), kind=kLoop, calls=%fused_computation.9 | loop fusion | flops 1572864 | bytes 7864320 | tf_op jit(solution)/shard_map/add | solution.py:136
  156.9 3.0 %collective-permute-done.17 = bf16[432,1024]{1,0:T(8,128)(2,1)} collective-permute-done((bf16[432,1024]{1,0:T(8,128)(2,1)}, bf16[432,1024]{1,0:T(8,128)(2,1)}, u32[]{:S(2)}, u32[]{:S(2)}) %collective-permute-start.17) | collective-permute-done | bytes 884768 | tf_op jit(solution)/shard_map/ppermute | solution.py:26
  159.9 1.0 select_select_fusion
  161.0 1.7 convert_add_fusion.2
  162.8 1.9 %convolution_convert_fusion = bf16[6,128,1024]{2,1,0:T(8,128)(2,1)S(1)} fusion(bf16[6,128,64]{2,1,0:T(8,128)(2,1)S(1)} %reshape_reshape.3, bf16[6,64,1024]{2,1,0:T(8,128)(2,1)} %collective-permute-done.18, bf16[6,64,1024]{2,1,0:T(8,128)(2,1)S(1)} %copy-done.8, pred[6]{0:T(512)(128)(4,1)S(1)} %fusion.27), kind=kOutput, calls=%fused_computation.20 | convolution fusion | flops 101842944 | bytes 3244038 | tf_op jit(solution)/shard_map/bcn,bnt->bct/dot_general | solution.py:276
  164.9 2.1 %multiply_reduce_fusion.1 = (f32[768]{0:T(1024)S(1)}, f32[768]{0:T(1024)S(1)}, bf16[768,1024]{1,0:T(8,128)(2,1)}) fusion(f32[1024]{0:T(1024)S(1)} %dynamic-slice-done, f32[768,1024]{1,0:T(8,128)S(1)} %convert_add_fusion.1, f32[384,1024]{1,0:T(8,128)S(1)} %convert_add_fusion.2, f32[384,1024]{1,0:T(8,128)S(1)} %copy-done.7, ...), kind=kLoop, calls=%fused_computation.8 | loop fusion | flops 8649216 | bytes 11020288 | tf_op jit(solution)/shard_map/reduce_sum | solution.py:311
  167.1 0.6 collective-permute-start.19
  167.6 3.2 %collective-permute-done.19 = f32[12,128]{1,0:T(8,128)S(1)} collective-permute-done((f32[12,128]{1,0:T(8,128)S(1)}, f32[12,128]{1,0:T(8,128)S(1)}, u32[]{:S(2)}, u32[]{:S(2)}) %collective-permute-start.19) | collective-permute-done | bytes 6176 | tf_op jit(solution)/shard_map/ppermute | solution.py:31
  171.0 3.4 %collective-permute-done.20 = f32[12,128]{1,0:T(8,128)S(1)} collective-permute-done((f32[12,128]{1,0:T(8,128)S(1)}, f32[12,128]{1,0:T(8,128)S(1)}, u32[]{:S(2)}, u32[]{:S(2)}) %collective-permute-start.20) | collective-permute-done | bytes 6176 | tf_op jit(solution)/shard_map/ppermute | solution.py:31
  174.4 4.5 %collective-permute-done.21 = f32[12,128]{1,0:T(8,128)S(1)} collective-permute-done((f32[12,128]{1,0:T(8,128)S(1)}, f32[12,128]{1,0:T(8,128)S(1)}, u32[]{:S(2)}, u32[]{:S(2)}) %collective-permute-start.21) | collective-permute-done | bytes 6176 | tf_op jit(solution)/shard_map/ppermute | solution.py:31
  179.0 0.7 fusion.21
  (77 shorter events, 1.5 us)
Async XLA Ops:
  5.3 14.3 %collective-permute-start = (bf16[6,64,1792]{2,1,0:T(8,128)(2,1)}, bf16[6,64,1792]{2,1,0:T(8,128)(2,1)}, u32[]{:S(2)}, u32[]{:S(2)}) collective-permute-start(bf16[6,64,1792]{2,1,0:T(8,128)(2,1)} %shard_map.113), channel_id=1, source_target_pairs={{0,8},{8,0},{1,9},{9,1},{2,10},{10,2},{3,11},{11,3},{4,12},{12,4},... | collective-permute-start | bytes 4128776 | tf_op jit(solution)/shard_map/ppermute | solution.py:256
  13.9 27.0 %collective-permute-start.1 = (bf16[384,1024]{1,0:T(8,128)(2,1)}, bf16[384,1024]{1,0:T(8,128)(2,1)}, u32[]{:S(2)}, u32[]{:S(2)}) collective-permute-start(bf16[384,1024]{1,0:T(8,128)(2,1)} %shard_map.114), channel_id=1, source_target_pairs={{0,1},{1,0},{2,3},{3,2},{4,5},{5,4},{6,7},{7,6},{8,9},{9,8},{10,11... | collective-permute-start | bytes 2359304 | tf_op jit(solution)/shard_map/ppermute | solution.py:31
  27.7 29.2 %collective-permute-start.2 = (bf16[432,1024]{1,0:T(8,128)(2,1)}, bf16[432,1024]{1,0:T(8,128)(2,1)S(1)}, u32[]{:S(2)}, u32[]{:S(2)}) collective-permute-start(bf16[432,1024]{1,0:T(8,128)(2,1)} %shard_map.116), channel_id=1, source_target_pairs={{0,1},{1,0},{2,3},{3,2},{4,5},{5,4},{6,7},{7,6},{8,9},{9,8},{10,11... | collective-permute-start | bytes 2654216 | tf_op jit(solution)/shard_map/ppermute | solution.py:31
  34.2 6.7 %copy-start.5 = (f32[384,1024]{1,0:T(8,128)S(1)}, f32[384,1024]{1,0:T(8,128)}, u32[]{:S(2)}) copy-start(f32[384,1024]{1,0:T(8,128)} %get-tuple-element.82) | copy-start | bytes 4718596
  38.9 33.8 %collective-permute-start.3 = (bf16[384,1024]{1,0:T(8,128)(2,1)}, bf16[384,1024]{1,0:T(8,128)(2,1)S(1)}, u32[]{:S(2)}, u32[]{:S(2)}) collective-permute-start(bf16[384,1024]{1,0:T(8,128)(2,1)} %shard_map.118), channel_id=1, source_target_pairs={{0,1},{1,0},{2,3},{3,2},{4,5},{5,4},{6,7},{7,6},{8,9},{9,8},{10,11... | collective-permute-start | bytes 2359304 | tf_op jit(solution)/shard_map/ppermute | solution.py:31
  42.3 30.4 %collective-permute-start.4 = (bf16[384,1024]{1,0:T(8,128)(2,1)S(1)}, bf16[384,1024]{1,0:T(8,128)(2,1)S(1)}, u32[]{:S(2)}, u32[]{:S(2)}) collective-permute-start(bf16[384,1024]{1,0:T(8,128)(2,1)S(1)} %add_convert_fusion.7), channel_id=1, source_target_pairs={{0,2},{1,3},{6,4},{7,5},{8,10},{9,11},{14,12},{15,13},{16,18},{17,... | collective-permute-start | bytes 2359304 | tf_op jit(solution)/shard_map/ppermute | solution.py:26
  56.9 2.0 %copy-start.3 = (f32[384,1024]{1,0:T(8,128)S(1)}, f32[384,1024]{1,0:T(8,128)}, u32[]{:S(2)}) copy-start(f32[384,1024]{1,0:T(8,128)} %get-tuple-element.89) | copy-start | bytes 4718596
  56.9 31.1 %copy-start.14 = (bf16[432,1024]{1,0:T(8,128)(2,1)}, bf16[432,1024]{1,0:T(8,128)(2,1)S(1)}, u32[]{:S(2)}) copy-start(bf16[432,1024]{1,0:T(8,128)(2,1)S(1)} %collective-permute-done.2) | copy-start | bytes 2654212
  57.0 2.2 %copy-start.1 = (bf16[384,1024]{1,0:T(8,128)(2,1)}, bf16[384,1024]{1,0:T(8,128)(2,1)S(1)}, u32[]{:S(2)}) copy-start(bf16[384,1024]{1,0:T(8,128)(2,1)S(1)} %slice.93) | copy-start | bytes 2359300
  59.2 1.8 copy-start.16
  59.3 25.2 %collective-permute-start.6 = (bf16[432,1024]{1,0:T(8,128)(2,1)S(1)}, bf16[432,1024]{1,0:T(8,128)(2,1)S(1)}, u32[]{:S(2)}, u32[]{:S(2)}) collective-permute-start(bf16[432,1024]{1,0:T(8,128)(2,1)S(1)} %pad_maximum_fusion.2), channel_id=1, source_target_pairs={{0,2},{1,3},{6,4},{7,5},{8,10},{9,11},{14,12},{15,13},{16,18},{17,... | collective-permute-start | bytes 2654216 | tf_op jit(solution)/shard_map/ppermute | solution.py:26
  61.0 26.6 %collective-permute-start.5 = (bf16[384,1024]{1,0:T(8,128)(2,1)S(1)}, bf16[384,1024]{1,0:T(8,128)(2,1)S(1)}, u32[]{:S(2)}, u32[]{:S(2)}) collective-permute-start(bf16[384,1024]{1,0:T(8,128)(2,1)S(1)} %copy-done.16), channel_id=1, source_target_pairs={{0,1},{1,0},{2,3},{3,2},{4,5},{5,4},{6,7},{7,6},{8,9},{9,8},{10,11... | collective-permute-start | bytes 2359304 | tf_op jit(solution)/shard_map/ppermute | solution.py:31
  66.1 6.6 %copy-start.10 = (f32[384,1024]{1,0:T(8,128)S(1)}, f32[384,1024]{1,0:T(8,128)}, u32[]{:S(2)}) copy-start(f32[384,1024]{1,0:T(8,128)} %get-tuple-element.65) | copy-start | bytes 4718596
  74.0 25.7 %collective-permute-start.7 = (bf16[384,1024]{1,0:T(8,128)(2,1)}, bf16[384,1024]{1,0:T(8,128)(2,1)}, u32[]{:S(2)}, u32[]{:S(2)}) collective-permute-start(bf16[384,1024]{1,0:T(8,128)(2,1)} %add_convert_fusion.5), channel_id=1, source_target_pairs={{0,2},{1,3},{2,4},{3,5},{8,10},{9,11},{10,12},{11,13},{16,18},{17,... | collective-permute-start | bytes 2359304 | tf_op jit(solution)/shard_map/ppermute | solution.py:26
  76.9 36.3 %collective-permute-start.8 = (bf16[384,1024]{1,0:T(8,128)(2,1)}, bf16[384,1024]{1,0:T(8,128)(2,1)}, u32[]{:S(2)}, u32[]{:S(2)}) collective-permute-start(bf16[384,1024]{1,0:T(8,128)(2,1)} %add_convert_fusion.5), channel_id=1, source_target_pairs={{6,4},{7,5},{4,2},{5,3},{14,12},{15,13},{12,10},{13,11},{22,20},{2... | collective-permute-start | bytes 2359304 | tf_op jit(solution)/shard_map/ppermute | solution.py:26
  78.4 36.3 %collective-permute-start.9 = (bf16[384,1024]{1,0:T(8,128)(2,1)}, bf16[384,1024]{1,0:T(8,128)(2,1)}, u32[]{:S(2)}, u32[]{:S(2)}) collective-permute-start(bf16[384,1024]{1,0:T(8,128)(2,1)} %shard_map.121), channel_id=1, source_target_pairs={{0,1},{1,0},{2,3},{3,2},{4,5},{5,4},{6,7},{7,6},{8,9},{9,8},{10,11... | collective-permute-start | bytes 2359304 | tf_op jit(solution)/shard_map/ppermute | solution.py:31
  84.5 3.1 %copy-start.9 = (f32[384,1024]{1,0:T(8,128)S(1)}, f32[384,1024]{1,0:T(8,128)}, u32[]{:S(2)}) copy-start(f32[384,1024]{1,0:T(8,128)} %get-tuple-element.70) | copy-start | bytes 4718596
  84.5 3.5 %copy-start.15 = (bf16[432,1024]{1,0:T(8,128)(2,1)}, bf16[432,1024]{1,0:T(8,128)(2,1)S(1)}, u32[]{:S(2)}) copy-start(bf16[432,1024]{1,0:T(8,128)(2,1)S(1)} %collective-permute-done.6) | copy-start | bytes 2654212
  89.1 33.8 %collective-permute-start.10 = (bf16[432,1024]{1,0:T(8,128)(2,1)}, bf16[432,1024]{1,0:T(8,128)(2,1)}, u32[]{:S(2)}, u32[]{:S(2)}) collective-permute-start(bf16[432,1024]{1,0:T(8,128)(2,1)} %pad_maximum_fusion.3), channel_id=1, source_target_pairs={{0,2},{1,3},{2,4},{3,5},{8,10},{9,11},{10,12},{11,13},{16,18},{17,... | collective-permute-start | bytes 2654216 | tf_op jit(solution)/shard_map/ppermute | solution.py:26
  94.0 30.3 %collective-permute-start.11 = (bf16[432,1024]{1,0:T(8,128)(2,1)}, bf16[432,1024]{1,0:T(8,128)(2,1)}, u32[]{:S(2)}, u32[]{:S(2)}) collective-permute-start(bf16[432,1024]{1,0:T(8,128)(2,1)} %pad_maximum_fusion.3), channel_id=1, source_target_pairs={{6,4},{7,5},{4,2},{5,3},{14,12},{15,13},{12,10},{13,11},{22,20},{2... | collective-permute-start | bytes 2654216 | tf_op jit(solution)/shard_map/ppermute | solution.py:26
  99.7 25.7 %collective-permute-start.12 = (bf16[384,1024]{1,0:T(8,128)(2,1)}, bf16[384,1024]{1,0:T(8,128)(2,1)}, u32[]{:S(2)}, u32[]{:S(2)}) collective-permute-start(bf16[384,1024]{1,0:T(8,128)(2,1)} %shard_map.123), channel_id=1, source_target_pairs={{0,1},{1,0},{2,3},{3,2},{4,5},{5,4},{6,7},{7,6},{8,9},{9,8},{10,11... | collective-permute-start | bytes 2359304 | tf_op jit(solution)/shard_map/ppermute | solution.py:31
  106.4 8.4 %copy-start.6 = (f32[384,1024]{1,0:T(8,128)S(1)}, f32[384,1024]{1,0:T(8,128)}, u32[]{:S(2)}) copy-start(f32[384,1024]{1,0:T(8,128)} %get-tuple-element.82) | copy-start | bytes 4718596
  106.4 8.4 %copy-start.13 = (f32[384,1024]{1,0:T(8,128)S(1)}, f32[384,1024]{1,0:T(8,128)}, u32[]{:S(2)}) copy-start(f32[384,1024]{1,0:T(8,128)} %get-tuple-element.75) | copy-start | bytes 4718596
  113.2 12.2 %copy-start.2 = (bf16[384,1024]{1,0:T(8,128)(2,1)S(1)}, bf16[384,1024]{1,0:T(8,128)(2,1)}, u32[]{:S(2)}) copy-start(bf16[384,1024]{1,0:T(8,128)(2,1)} %copy-done.1) | copy-start | bytes 2359300
  113.2 41.7 %collective-permute-start.15 = (bf16[768,1024]{1,0:T(8,128)(2,1)}, bf16[768,1024]{1,0:T(8,128)(2,1)}, u32[]{:S(2)}, u32[]{:S(2)}) collective-permute-start(bf16[768,1024]{1,0:T(8,128)(2,1)} %shard_map.124), channel_id=1, source_target_pairs={{0,1},{1,0},{2,3},{3,2},{4,5},{5,4},{6,7},{7,6},{8,9},{9,8},{10,11... | collective-permute-start | bytes 4718600 | tf_op jit(solution)/shard_map/ppermute | solution.py:31
  114.7 10.6 %copy-start.4 = (f32[384,1024]{1,0:T(8,128)S(1)}, f32[384,1024]{1,0:T(8,128)}, u32[]{:S(2)}) copy-start(f32[384,1024]{1,0:T(8,128)} %get-tuple-element.89) | copy-start | bytes 4718596
  114.8 10.6 %copy-start.12 = (f32[384,1024]{1,0:T(8,128)S(1)}, f32[384,1024]{1,0:T(8,128)}, u32[]{:S(2)}) copy-start(f32[384,1024]{1,0:T(8,128)} %get-tuple-element.79) | copy-start | bytes 4718596
  118.5 23.4 %collective-permute-start.13 = (bf16[384,1024]{1,0:T(8,128)(2,1)}, bf16[384,1024]{1,0:T(8,128)(2,1)S(1)}, u32[]{:S(2)}, u32[]{:S(2)}) collective-permute-start(bf16[384,1024]{1,0:T(8,128)(2,1)} %get-tuple-element.102), channel_id=1, source_target_pairs={{0,2},{1,3},{2,4},{3,5},{4,6},{5,7},{8,10},{9,11},{10,12},{11,13},... | collective-permute-start | bytes 2359304 | tf_op jit(solution)/shard_map/ppermute | solution.py:26
  122.9 22.4 %collective-permute-start.14 = (bf16[384,1024]{1,0:T(8,128)(2,1)S(1)}, bf16[384,1024]{1,0:T(8,128)(2,1)S(1)}, u32[]{:S(2)}, u32[]{:S(2)}) collective-permute-start(bf16[384,1024]{1,0:T(8,128)(2,1)S(1)} %get-tuple-element.101), channel_id=1, source_target_pairs={{6,4},{7,5},{4,2},{5,3},{2,0},{3,1},{14,12},{15,13},{12,10},{13,11... | collective-permute-start | bytes 2359304 | tf_op jit(solution)/shard_map/ppermute | solution.py:26
  129.3 27.6 %collective-permute-start.16 = (bf16[432,1024]{1,0:T(8,128)(2,1)}, bf16[432,1024]{1,0:T(8,128)(2,1)}, u32[]{:S(2)}, u32[]{:S(2)}) collective-permute-start(bf16[432,1024]{1,0:T(8,128)(2,1)} %get-tuple-element.104), channel_id=1, source_target_pairs={{0,2},{1,3},{2,4},{3,5},{4,6},{5,7},{8,10},{9,11},{10,12},{11,13},... | collective-permute-start | bytes 2654216 | tf_op jit(solution)/shard_map/ppermute | solution.py:26
  134.8 25.1 %collective-permute-start.17 = (bf16[432,1024]{1,0:T(8,128)(2,1)}, bf16[432,1024]{1,0:T(8,128)(2,1)}, u32[]{:S(2)}, u32[]{:S(2)}) collective-permute-start(bf16[432,1024]{1,0:T(8,128)(2,1)} %get-tuple-element.103), channel_id=1, source_target_pairs={{6,4},{7,5},{4,2},{5,3},{2,0},{3,1},{14,12},{15,13},{12,10},{13,11... | collective-permute-start | bytes 2654216 | tf_op jit(solution)/shard_map/ppermute | solution.py:26
  141.9 13.0 %copy-start = (f32[768,1024]{1,0:T(8,128)S(1)}, f32[768,1024]{1,0:T(8,128)}, u32[]{:S(2)}) copy-start(f32[768,1024]{1,0:T(8,128)} %shard_map.125) | copy-start | bytes 9437188
  141.9 20.9 %collective-permute-start.18 = (bf16[6,64,1024]{2,1,0:T(8,128)(2,1)}, bf16[6,64,1024]{2,1,0:T(8,128)(2,1)}, u32[]{:S(2)}, u32[]{:S(2)}) collective-permute-start(bf16[6,64,1024]{2,1,0:T(8,128)(2,1)} %shard_map.126), channel_id=1, source_target_pairs={{0,8},{8,0},{1,9},{9,1},{2,10},{10,2},{3,11},{11,3},{4,12},{12,4},... | collective-permute-start | bytes 2359304 | tf_op jit(solution)/shard_map/ppermute | solution.py:256
  161.0 1.8 copy-start.8
  162.8 2.0 %copy-start.7 = (f32[384,1024]{1,0:T(8,128)S(1)}, f32[384,1024]{1,0:T(8,128)}, u32[]{:S(2)}) copy-start(f32[384,1024]{1,0:T(8,128)} %convert_add_fusion.3) | copy-start | bytes 4718596
  162.8 2.1 %copy-start.11 = (bf16[768,1024]{1,0:T(8,128)(2,1)S(1)}, bf16[768,1024]{1,0:T(8,128)(2,1)}, u32[]{:S(2)}) copy-start(bf16[768,1024]{1,0:T(8,128)(2,1)} %param.15) | copy-start | bytes 4718596
  162.8 2.1 %dynamic-slice-start = ((f32[8192]{0:T(1024)}, s32[]{:T(128)}), f32[1024]{0:T(1024)S(1)}, s32[]{:S(2)}) async-start(f32[8192]{0:T(1024)} %param.16, s32[]{:T(128)} %select_n.99), calls=%async_computation | async-start | bytes 8704 | tf_op jit(solution)/shard_map/dynamic_slice | solution.py:308
  164.9 14.1 %copy-start.17 = (s32[6]{0:T(128)S(1)}, s32[6]{0:T(128)}, u32[]{:S(2)}) copy-start(s32[6]{0:T(128)} %param.19) | copy-start | bytes 76
  164.9 14.1 %copy-start.18 = (s32[6]{0:T(128)S(1)}, s32[6]{0:T(128)}, u32[]{:S(2)}) copy-start(s32[6]{0:T(128)} %param.18) | copy-start | bytes 76
  167.1 3.7 %collective-permute-start.19 = (f32[12,128]{1,0:T(8,128)S(1)}, f32[12,128]{1,0:T(8,128)S(1)}, u32[]{:S(2)}, u32[]{:S(2)}) collective-permute-start(f32[12,128]{1,0:T(8,128)S(1)} %reshape.81), channel_id=1, source_target_pairs={{0,1},{1,0},{2,3},{3,2},{4,5},{5,4},{6,7},{7,6},{8,9},{9,8},{10,11... | collective-permute-start | bytes 18440 | tf_op jit(solution)/shard_map/ppermute | solution.py:31
  170.8 3.7 %collective-permute-start.20 = (f32[12,128]{1,0:T(8,128)S(1)}, f32[12,128]{1,0:T(8,128)S(1)}, u32[]{:S(2)}, u32[]{:S(2)}) collective-permute-start(f32[12,128]{1,0:T(8,128)S(1)} %add.156), channel_id=1, source_target_pairs={{0,2},{1,3},{2,0},{3,1},{4,6},{5,7},{6,4},{7,5},{8,10},{9,11},{10,... | collective-permute-start | bytes 18440 | tf_op jit(solution)/shard_map/ppermute | solution.py:31
  174.4 4.5 %collective-permute-start.21 = (f32[12,128]{1,0:T(8,128)S(1)}, f32[12,128]{1,0:T(8,128)S(1)}, u32[]{:S(2)}, u32[]{:S(2)}) collective-permute-start(f32[12,128]{1,0:T(8,128)S(1)} %add.157), channel_id=1, source_target_pairs={{0,4},{1,5},{2,6},{3,7},{4,0},{5,1},{6,2},{7,3},{8,12},{9,13},{10,... | collective-permute-start | bytes 18440 | tf_op jit(solution)/shard_map/ppermute | solution.py:31
